TPU v7x, 32 devices: a whole 2x2x4 slice. The times are simulated.
32 devices in a mesh: occ: 4 (over z), virt: 8 (over y, x, core).
Axes of the slice: x: 2, y: 2, z: 4, core: 2. Of those that a mesh axis runs over, the one named last changes fastest.
Arguments:
- basis_integrals: bfloat16 [16, 1280, 2048], P(None, 'virt', 'occ'), may hold values from -2 to 2
- group_sizes: int32 [4], replicated, may hold values from 1 to 6, 16 in all
- orbital_order: int32 [16], replicated, may hold values from 0 to 15, each once
- eps_occ: float32 [16], replicated, may hold values from -1.5 to -0.3
- eps_vir: float32 [1280], replicated, may hold values from 0.2 to 2.5
Outputs:
- density: bfloat16 [4, 6, 1280, 2048], P('occ', None, 'virt')
Inputs may be any that keep to these rules, and one draw needn't show every extreme that they name: `group_sizes`: each group holds 1 to 6 orbitals, 16 together, and some group holds exactly 6. `orbital_order`: each window orbital appears once.
All inputs are finite; a program needn't handle non-finite values.
Results may differ from a plain program's by a relative error of at most 0.0034.
Values may be sent and summed in bfloat16 or wider, within the bound.
No kernel may reach another device: no remote copies, remote signals or barrier semaphores. Data moves between devices by JAX's collectives and lax.ppermute only.
A program may use at most 128 MiB of HBM per device.

v0:
```python
import functools

import jax
import jax.numpy as jnp
from jax import lax
from jax.experimental import pallas as pl
from jax.experimental.pallas import tpu as pltpu
from jax.sharding import PartitionSpec as P

CAP = 6
LANES = 256
VMEM_LIMIT = (64 << 20) - (512 << 10)
SMALL = pl.CostEstimate(flops=1 << 10, bytes_accessed=1 << 10, transcendentals=0)
ANY = pl.BlockSpec(memory_space=pl.ANY)
VMEM = pl.BlockSpec(memory_space=pltpu.VMEM)
SMEM = pl.BlockSpec(memory_space=pltpu.SMEM)


def group_slots(sizes, order, group, n_groups):
    offset = jnp.int32(0)
    count = jnp.int32(0)
    for other in range(n_groups):
        offset = offset + jnp.where(other < group, sizes[other], 0)
        count = count + jnp.where(other == group, sizes[other], 0)
    last = order.shape[0] - 1
    return [
        (order[jnp.minimum(offset + slot, last)], slot < count) for slot in range(CAP)
    ]


def stage_kernel(n_occ, low, high, with_own, split, me, sizes, order, basis, token_in, *refs):
    outs, own, (held, read, sent) = refs[1:-3], refs[-4], refs[-3:]
    reads = []
    copies = []
    rows = pl.ds(low, high - low)
    for mask in range(n_occ):
        whole = with_own and mask == 0
        for slot, (orbital, live) in enumerate(
            group_slots(sizes, order, me[0] ^ mask, n_occ)
        ):
            index = mask * CAP + slot
            if whole:
                copy = pltpu.make_async_copy(basis.at[orbital], held.at[0, slot], read.at[index])
            else:
                copy = pltpu.make_async_copy(
                    basis.at[orbital, rows], held.at[mask, slot, pl.ds(0, high - low)], read.at[index]
                )
            copy.start()
            reads.append((copy, live))
    for mask in range(n_occ):
        for slot in range(CAP):
            copy, live = reads[mask * CAP + slot]
            copy.wait()

            @pl.when(jnp.logical_not(live))
            def _():
                held[mask, slot] = jnp.zeros(held.shape[2:], held.dtype)

        if mask or not split:
            target = outs[mask - 1] if split else outs[0].at[me[0] ^ mask]
            copies.append(
                pltpu.make_async_copy(held.at[mask, :, pl.ds(0, high - low)], target, sent.at[mask])
            )
            copies[-1].start()
        if with_own and mask == 0:
            copies.append(pltpu.make_async_copy(held.at[0], own, sent.at[n_occ]))
            copies[-1].start()
    for copy in copies:
        copy.wait()


def stage(token, basis, me, sizes, order, n_occ, low, high, with_own=False, split=False):
    width, aux = basis.shape[1:]
    piece = (CAP, high - low, aux)
    shapes = [piece] * (n_occ - 1) if split else [(n_occ, *piece)]
    shapes += [(CAP, width, aux)] * with_own
    return pl.pallas_call(
        functools.partial(stage_kernel, n_occ, low, high, with_own, split),
        out_shape=[
            jax.ShapeDtypeStruct(token.shape, token.dtype),
            *[jax.ShapeDtypeStruct(shape, basis.dtype) for shape in shapes],
        ],
        in_specs=[SMEM, SMEM, SMEM, ANY, ANY],
        out_specs=[ANY] * (1 + len(shapes)),
        scratch_shapes=[
            pltpu.VMEM((n_occ, CAP, width if with_own else high - low, aux), basis.dtype),
            pltpu.SemaphoreType.DMA((n_occ * CAP,)),
            pltpu.SemaphoreType.DMA((1 + n_occ,)),
        ],
        input_output_aliases={4: 0},
        compiler_params=pltpu.CompilerParams(vmem_limit_bytes=VMEM_LIMIT),
        cost_estimate=SMALL,
    )(me, sizes, order, basis, token)


def gate(token, needs=(), gives=()):
    operands = [token, *gives, *needs]
    kept = 1 + len(gives)
    done = pl.pallas_call(
        lambda *refs: None,
        out_shape=[jax.ShapeDtypeStruct(x.shape, x.dtype) for x in operands[:kept]],
        in_specs=[ANY] * len(operands),
        out_specs=[ANY] * kept,
        input_output_aliases={i: i for i in range(kept)},
        compiler_params=pltpu.CompilerParams(vmem_limit_bytes=VMEM_LIMIT),
        cost_estimate=SMALL,
    )(*operands)
    return done[0], done[1:]


def join_kernel(n_occ, n_got, parts, me, token_in, *refs):
    got, outs, (held, read, sent) = refs[:n_got], refs[n_got + 1 : -3], refs[-3:]
    sources = got if n_got > 1 else [got[0].at[me[0] ^ mask] for mask in range(1, n_occ)]
    reads = [
        pltpu.make_async_copy(source, held.at[i], read.at[i]) for i, source in enumerate(sources)
    ]
    width = held.shape[2] // parts
    sends = [
        pltpu.make_async_copy(held.at[:, :, pl.ds(i * width, width)], outs[i], sent.at[i])
        for i in range(parts)
    ]
    for copy in reads:
        copy.start()
    for copy in reads:
        copy.wait()
    for copy in sends:
        copy.start()
    for copy in sends:
        copy.wait()


def join(token, me, got, parts):
    cap, rows, aux = got[0].shape[-3:]
    n_occ = got[0].shape[0] if len(got) == 1 else len(got) + 1
    shape = jax.ShapeDtypeStruct((n_occ - 1, cap, rows // parts, aux), got[0].dtype)
    done = pl.pallas_call(
        functools.partial(join_kernel, n_occ, len(got), parts),
        out_shape=[jax.ShapeDtypeStruct(token.shape, token.dtype)] + [shape] * parts,
        in_specs=[SMEM] + [ANY] * (1 + len(got)),
        out_specs=[ANY] * (1 + parts),
        scratch_shapes=[
            pltpu.VMEM((n_occ - 1, cap, rows, aux), got[0].dtype),
            pltpu.SemaphoreType.DMA((n_occ,)),
            pltpu.SemaphoreType.DMA((parts,)),
        ],
        input_output_aliases={1: 0},
        compiler_params=pltpu.CompilerParams(vmem_limit_bytes=VMEM_LIMIT),
        cost_estimate=SMALL,
    )(me, token, *got)
    return done[0], done[1:]


def runs(flags, low, high):
    out = []
    for p in range(low, high):
        if out and flags[p] == out[-1][2]:
            out[-1] = (out[-1][0], p + 1, flags[p])
        else:
            out.append((p, p + 1, flags[p]))
    return out


def density_kernel(
    n_occ, n_blocks, cuts, jobs, held, last, me, sizes, order, eps_occ, va, vb, *refs
):
    refs = list(refs)
    refs.pop(0)
    n_parts = sum(cuts)
    first_blocks = [refs.pop(0) for _ in range(n_blocks)]
    units, chunks, row_chunks = plan(cuts, jobs)
    col_blocks = {c: [refs.pop(0) for _ in range(n_blocks)] for c in chunks}
    own = {c: col_blocks[c][0] if c in chunks else refs.pop(0) for c in row_chunks}
    before = refs.pop(0) if any(held) else None
    refs.pop(0)
    out, rows, cols, kbuf, abuf, total, result, sems = refs
    width, aux = rows.shape[2], rows.shape[3]
    part = width // n_parts
    n_copies = 0

    def copy(source, target):
        nonlocal n_copies
        made = pltpu.make_async_copy(source, target, sems.at[n_copies])
        made.start()
        n_copies += 1
        return made

    def load_rows(c):
        place = pl.ds(sum(cuts[:c]) * part, cuts[c] * part)
        return [
            copy(first_blocks[0].at[:, place], rows.at[0, :, place]),
            copy(own[c], rows.at[pl.ds(1, n_occ - 1), :, place]),
        ]

    def load_cols(unit, first, count):
        index, slots = units.index(unit), pl.ds(first, count)
        c = chunk_of(cuts, unit)
        inside = pl.ds((unit - sum(cuts[:c])) * part, part)
        copies = []
        for b in range(n_blocks):
            place = pl.ds(b * part, part)
            copies.append(
                copy(
                    first_blocks[b].at[slots, pl.ds(unit * part, part)],
                    cols.at[index, 0, slots, place],
                )
            )
            copies.append(
                copy(
                    col_blocks[c][b].at[:, slots, inside],
                    cols.at[index, pl.ds(1, n_occ - 1), slots, place],
                )
            )
        return copies

    def needed_rows(job):
        return [c for c in row_chunks if job[0] < sum(cuts[: c + 1]) and sum(cuts[:c]) < job[1]]

    row_copies = {c: load_rows(c) for c in needed_rows(jobs[0])}
    col_copies = {
        (units[0], first): load_cols(units[0], first, count)
        for first, count in ((0, 2), (2, 2), (4, 2))
    }
    for c in row_chunks:
        if c not in row_copies:
            row_copies[c] = load_rows(c)
    for unit in units[1:]:
        col_copies[unit, 0] = load_cols(unit, 0, CAP)
    total_copies = []
    energy = []
    for orbital, live in group_slots(sizes, order, me[0], n_occ):
        energy.append(jnp.where(live, eps_occ[orbital], jnp.float32(0.0)))

    def combine(low, n_rows, unit, at, i, j):
        step = 32 if n_rows % 32 == 0 else 16
        for r in range(0, n_rows, step):
            gap = (energy[i] + energy[j]) - (va[pl.ds(low + r, step), :] + vb[unit])
            inverse = pltpu.reciprocal(gap, approx=True)
            inverse = inverse * (2.0 - gap * inverse)
            upper = kbuf[j, pl.ds(i * n_rows + r, step), :]
            if i == j:
                abuf[pl.ds(i * n_rows + r, step), pl.ds(at + j * LANES, LANES)] = (
                    upper * inverse
                ).astype(abuf.dtype)
            else:
                lower = kbuf[i, pl.ds(j * n_rows + r, step), :]
                abuf[pl.ds(i * n_rows + r, step), pl.ds(at + j * LANES, LANES)] = (
                    (upper + upper - lower) * inverse
                ).astype(abuf.dtype)
                abuf[pl.ds(j * n_rows + r, step), pl.ds(at + i * LANES, LANES)] = (
                    (lower + lower - upper) * inverse
                ).astype(abuf.dtype)

    span = min(n_occ, max(1, 1024 // aux))
    spans = [(s, span) for s in range(0, n_occ - span, span)]
    tail = max(1, span // 2)
    spans += [(s, tail) for s in range(n_occ - span, n_occ, tail)]
    flags = list(held)
    sent = []
    for number, (low, high, chosen) in enumerate(jobs):
        first_row, n_rows = low * part, (high - low) * part
        for c in needed_rows((low, high)):
            for made in row_copies.pop(c, ()):
                made.wait()
        for slot, unit in enumerate(chosen):
            index = units.index(unit)
            for j in range(CAP + 1):
                for made in col_copies.pop((unit, j), ()):
                    made.wait()
                if number == 0 and slot == 0 and j == 2:
                    total_copies = [
                        copy(before.at[:, pl.ds(a * part, (b - a) * part)], total.at[:, pl.ds(a * part, (b - a) * part)])
                        for a, b, flag in runs(held, 0, n_parts)
                        if flag
                    ]
                if j < CAP:
                    left = jnp.concatenate(
                        [
                            rows[s, :, first_row : first_row + n_rows].reshape(CAP * n_rows, aux)
                            for s in range(n_occ)
                        ],
                        axis=1,
                    )
                    right = jnp.concatenate([cols[index, s, j] for s in range(n_occ)], axis=1)
                    kbuf[j, pl.ds(0, CAP * n_rows)] = lax.dot_general(
                        left, right, (((1,), (1,)), ((), ())), preferred_element_type=jnp.float32
                    )
                for i in range(j):
                    combine(first_row, n_rows, unit, slot * CAP * LANES, i, j - 1)
        if number == 0:
            for made in total_copies:
                made.wait()
        depth = len(chosen) * CAP * LANES
        for s, span in spans:
            lanes = pl.ds(s * aux, span * aux)
            right = jnp.concatenate(
                [
                    jnp.concatenate(
                        [cols[units.index(unit), t].reshape(CAP * LANES, aux) for unit in chosen],
                        axis=0,
                    )
                    for t in range(s, s + span)
                ],
                axis=1,
            )
            added = jnp.dot(
                abuf[pl.ds(0, CAP * n_rows), pl.ds(0, depth)], right, preferred_element_type=jnp.float32
            ).reshape(CAP, n_rows, span * aux)
            final = number == len(jobs) - 1
            for a, b, flag in runs(flags, low, high):
                where = pl.ds(a * part, (b - a) * part)
                piece = added[:, (a - low) * part : (b - low) * part]
                if flag:
                    piece = piece + total[:, where, lanes]
                if last and final:
                    result[:, where, lanes] = piece.astype(result.dtype)
                else:
                    total[:, where, lanes] = piece
            if final:
                if last:
                    for t in range(s, s + span):
                        place = pl.multiple_of((me[0] ^ t) * aux, aux)
                        sent.append(
                            copy(result.at[:, :, pl.ds(t * aux, aux)], out.at[:, :, pl.ds(place, aux)])
                        )
                else:
                    for a, b, flag in runs(
                        [f or low <= p < high for p, f in enumerate(flags)], 0, n_parts
                    ):
                        where = pl.ds(a * part, (b - a) * part)
                        if flag:
                            sent.append(
                                copy(total.at[:, where, lanes], out.at[:, where, lanes])
                            )
        flags = [f or low <= p < high for p, f in enumerate(flags)]
    for made in sent:
        made.wait()


def chunk_of(cuts, unit):
    return next(c for c in range(len(cuts)) if unit < sum(cuts[: c + 1]))


def plan(cuts, jobs):
    units = []
    for _, _, chosen in jobs:
        units += [unit for unit in chosen if unit not in units]
    chunks = sorted({chunk_of(cuts, unit) for unit in units})
    rows = sorted({chunk_of(cuts, p) for low, high, _ in jobs for p in range(low, high)})
    return units, chunks, rows


def density(token, scalars, first_blocks, blocks, before, held, jobs, last, cuts):
    n_blocks = len(first_blocks)
    width, aux = first_blocks[0].shape[1:]
    part = width // sum(cuts)
    n_occ = blocks[0][0].shape[0] + 1
    naux = n_occ * aux
    units, chunks, row_chunks = plan(cuts, jobs)
    kept = jnp.bfloat16 if last else jnp.float32
    deepest = max(len(chosen) for _, _, chosen in jobs)
    tallest = max(high - low for low, high, _ in jobs) * part * CAP
    operands = [*scalars, token, *first_blocks]
    for c in chunks:
        operands += blocks[c]
    operands += [blocks[c][0] for c in row_chunks if c not in chunks]
    operands += [before] if any(held) else []
    at = len(scalars)
    done = pl.pallas_call(
        functools.partial(density_kernel, n_occ, n_blocks, cuts, jobs, held, last),
        out_shape=[
            jax.ShapeDtypeStruct(token.shape, token.dtype),
            jax.ShapeDtypeStruct((CAP, width, naux), kept),
        ],
        in_specs=[SMEM] * 4 + [VMEM] * 2 + [ANY] * (len(operands) - at),
        out_specs=[ANY] * 2,
        scratch_shapes=[
            pltpu.VMEM((n_occ, CAP, width, aux), jnp.bfloat16),
            pltpu.VMEM((len(units), n_occ, CAP, LANES, aux), jnp.bfloat16),
            pltpu.VMEM((CAP, tallest, LANES), jnp.float32),
            pltpu.VMEM((tallest, deepest * CAP * LANES), jnp.bfloat16),
            pltpu.VMEM((CAP, width, naux), jnp.float32),
            pltpu.VMEM((CAP, width, naux) if last else (1, 16, 128), jnp.bfloat16),
            pltpu.SemaphoreType.DMA((48 + 2 * n_blocks * (len(units) + 4),)),
        ],
        input_output_aliases={at: 0},
        compiler_params=pltpu.CompilerParams(vmem_limit_bytes=VMEM_LIMIT),
        cost_estimate=SMALL,
    )(*operands)
    held = tuple(
        f or any(low <= p < high for low, high, _ in jobs) for p, f in enumerate(held)
    )
    return done[0], done[1], held


def on_device(basis, group_sizes, orbital_order, eps_occ, eps_vir):
    n_virt, n_occ = lax.axis_size("virt"), lax.axis_size("occ")
    me_occ, me_virt = lax.axis_index("occ"), lax.axis_index("virt")
    width, aux = basis.shape[1:]
    dims = (n_virt // 2).bit_length() - 1
    part = LANES // n_virt
    n_parts = width // part
    me = me_occ.reshape(1).astype(jnp.int32)
    n_own = 1 << dims

    def bit(dim, core):
        return 2 << ((dim + core) % dims)

    def hop(block, dim):
        pairs = [(d, d ^ bit(dim, d & 1)) for d in range(n_virt)]
        return lax.ppermute(block, "virt", pairs)

    def sibling(block):
        return lax.ppermute(block, "virt", [(d, d ^ 1) for d in range(n_virt)])

    def across(block, mask):
        return lax.ppermute(block, "occ", [(d, d ^ mask) for d in range(n_occ)])

    def origin(mask, core):
        return sum(bit(dim, core) for dim in range(dims) if mask >> dim & 1)

    core = me_virt & 1
    origins = [
        me_virt ^ jnp.where(core == 0, origin(m, 0), origin(m, 1)) for m in range(n_own)
    ] + [
        me_virt ^ 1 ^ jnp.where(core == 0, origin(m, 1), origin(m, 0)) for m in range(n_own)
    ]
    by_owner = eps_vir.reshape(n_virt, n_parts, part)
    vb = by_owner[jnp.stack(origins)].transpose(1, 0, 2).reshape(n_parts, 1, LANES)
    va = lax.dynamic_slice_in_dim(eps_vir, me_virt * width, width).reshape(width, 1)
    scalars = (me, group_sizes, orbital_order, eps_occ, va, vb)

    z_parts = (1, 2, 2)
    cuts = z_parts
    starts = [sum(cuts[:c]) * part for c in range(len(cuts) + 1)]
    sends = []
    token = jnp.zeros((8, 128), jnp.float32)
    token, send, first = stage(token, basis, *scalars[:3], n_occ, 0, starts[1], with_own=True)
    sends.append([send])
    blocks = {}

    def spread(name, block):
        held = blocks[name] = [block] + [None] * (2 * n_own - 1)
        held[n_own] = sibling(block)
        for dim in range(dims):
            held[1 << dim] = hop(block, dim)

    def relay(token, name, level):
        held = blocks[name]
        arrived = [m for m in range(1, n_own) if m.bit_count() == level]
        token, gated = gate(token, (), [held[m] for m in arrived])
        for m, block in zip(arrived, gated):
            held[m] = block
        for m in arrived:
            for dim in range(m.bit_length(), dims):
                held[m | 1 << dim] = hop(held[m], dim)
        for m in arrived:
            held[n_own + m] = sibling(held[m])
        return token

    crossing = []
    n_chunks = len(z_parts)

    def cross(token, c):
        token, gated = gate(token, (), sends[c])
        if len(gated) == 1:
            crossing.append([lax.all_to_all(gated[0], "occ", 0, 0, tiled=True)])
        else:
            crossing.append([across(block, mask) for mask, block in enumerate(gated, 1)])
        return token

    total, held = None, (False,) * n_parts

    def add(jobs, last=False):
        nonlocal token, total, held
        token, total, held = density(
            token, scalars, blocks["first"], chunks, total, held, jobs, last, cuts
        )

    def arrive(name):
        nonlocal token
        for level in range(2, dims + 1):
            token = relay(token, name, level)

    chunks = {}

    def collect(c):
        nonlocal token
        token, (block,) = join(token, me, crossing[c], 1)
        spread(c, block)
        chunks[c] = blocks[c]

    token = cross(token, 0)
    spread("first", first)
    for c in range(1, n_chunks):
        token, *send = stage(token, basis, *scalars[:3], n_occ, starts[c], starts[c + 1])
        sends.append(send)
    for c in range(1, n_chunks):
        token = cross(token, c)
    collect(0)
    token = relay(token, "first", 1)
    arrive("first")
    token = relay(token, 0, 1)
    arrive(0)
    collect(1)
    early = cuts[0] + cuts[1]
    add([(0, early, (0,))])
    token = relay(token, 1, 1)
    collect(2)
    arrive(1)
    add([(early, n_parts, (0,)), (0, n_parts, (1,))])
    token = relay(token, 2, 1)
    add([(0, n_parts, (2,))])
    arrive(2)
    add([(0, n_parts, (3, 4))], True)
    return total.reshape(1, CAP, width, n_occ * aux)


def solution(mesh):
    return jax.shard_map(
        on_device,
        mesh=mesh,
        in_specs=(P(None, "virt", "occ"), P(), P(), P(), P()),
        out_specs=P("occ", None, "virt", None),
        check_vma=False,
    )
```

profile of v0, /device:TPU:0, one launch (start us, length us, event | category | flops | bytes accessed | tf_op | source)
XLA Modules:
  0.0 209.6 jit_solution(17360466688108352171)
XLA Ops:
  0.0 0.6 broadcast_in_dim.4.token_in
  0.6 3.5 %shard_map.55 = (f32[8,128]{1,0:T(8,128)}, bf16[4,6,32,512]{3,2,1,0:T(8,128)(2,1)}, bf16[6,160,512]{2,1,0:T(8,128)(2,1)}) custom-call(s32[1]{0:T(128)} %bitcast.me, s32[4]{0:T(128)} %sizes.13, s32[16]{0:T(128)} %order.13, bf16[16,160,512]{2,1,0:T(8,128)(2,1)} %basis.5, f32[8,128]{1,0:T(8,128)} %broadcast_in_dim.4.token_in), custom_call_target="tpu_custom_call", output_to_operand_aliasing={{0}: (4, {})} | custom-call | flops 1024 | bytes 1024 | tf_op jit(solution)/shard_map/pallas_call | solution.py:77
  4.1 6.4 %all-to-all-start = ((bf16[4,6,32,512]{3,2,1,0:T(8,128)(2,1)}), bf16[4,6,32,512]{3,2,1,0:T(8,128)(2,1)}, u32[]{:S(2)}, u32[]{:S(2)}) async-start(bf16[4,6,32,512]{3,2,1,0:T(8,128)(2,1)} %get-tuple-element.60), calls=%async_computation | async-start | bytes 1572864 | tf_op jit(solution)/shard_map/all_to_all | solution.py:466
  10.5 1.5 collective-permute-start
  12.0 1.5 collective-permute-start.1
  13.5 3.1 %shard_map.57 = (f32[8,128]{1,0:T(8,128)}, bf16[4,6,64,512]{3,2,1,0:T(8,128)(2,1)}) custom-call(s32[1]{0:T(128)} %bitcast.me, s32[4]{0:T(128)} %sizes.13, s32[16]{0:T(128)} %order.13, bf16[16,160,512]{2,1,0:T(8,128)(2,1)} %basis.5, f32[8,128]{1,0:T(8,128)} %get-tuple-element.53.token_in), custom_call_target="tpu_custom_call", output_to_operand_aliasing={{0}: (4, {})} | custom-call | flops 1024 | bytes 1024 | tf_op jit(solution)/shard_map/pallas_call | solution.py:77
  16.6 3.6 %shard_map.58 = (f32[8,128]{1,0:T(8,128)}, bf16[4,6,64,512]{3,2,1,0:T(8,128)(2,1)}) custom-call(s32[1]{0:T(128)} %bitcast.me, s32[4]{0:T(128)} %sizes.13, s32[16]{0:T(128)} %order.13, bf16[16,160,512]{2,1,0:T(8,128)(2,1)} %basis.5, f32[8,128]{1,0:T(8,128)} %get-tuple-element.54.token_in), custom_call_target="tpu_custom_call", output_to_operand_aliasing={{0}: (4, {})} | custom-call | flops 1024 | bytes 1024 | tf_op jit(solution)/shard_map/pallas_call | solution.py:77
  20.2 10.5 %all-to-all-done.refs_0_ = bf16[4,6,32,512]{3,2,1,0:T(8,128)(2,1)} async-done(((bf16[4,6,32,512]{3,2,1,0:T(8,128)(2,1)}), bf16[4,6,32,512]{3,2,1,0:T(8,128)(2,1)}, u32[]{:S(2)}, u32[]{:S(2)}) %all-to-all-start) | async-done | bytes 786464 | tf_op jit(solution)/shard_map/all_to_all | solution.py:466
  30.7 4.4 %all-to-all-start.1 = ((bf16[4,6,64,512]{3,2,1,0:T(8,128)(2,1)}), bf16[4,6,64,512]{3,2,1,0:T(8,128)(2,1)}, u32[]{:S(2)}, u32[]{:S(2)}) async-start(bf16[4,6,64,512]{3,2,1,0:T(8,128)(2,1)} %get-tuple-element.70), calls=%async_computation.1 | async-start | bytes 3145728 | tf_op jit(solution)/shard_map/all_to_all | solution.py:466
  35.1 2.0 shard_map.61
  37.1 0.0 collective-permute-done.1.refs_2_
  37.1 1.6 collective-permute-start.2
  38.7 1.5 collective-permute-start.3
  40.2 0.5 collective-permute-start.4
  40.7 0.5 collective-permute-start.7
  41.2 16.0 %collective-permute-done.2.refs_1_ = bf16[6,160,512]{2,1,0:T(8,128)(2,1)} collective-permute-done((bf16[6,160,512]{2,1,0:T(8,128)(2,1)}, bf16[6,160,512]{2,1,0:T(8,128)(2,1)}, u32[]{:S(2)}, u32[]{:S(2)}) %collective-permute-start.2) | collective-permute-done | bytes 983072 | tf_op jit(solution)/shard_map/ppermute | solution.py:410
  57.2 0.0 collective-permute-done.3.refs_1_
  57.2 6.3 %collective-permute-done.4.refs_2_ = bf16[3,6,32,512]{3,2,1,0:T(8,128)(2,1)} collective-permute-done((bf16[3,6,32,512]{3,2,1,0:T(8,128)(2,1)}, bf16[3,6,32,512]{3,2,1,0:T(8,128)(2,1)}, u32[]{:S(2)}, u32[]{:S(2)}) %collective-permute-start.4) | collective-permute-done | bytes 589856 | tf_op jit(solution)/shard_map/ppermute | solution.py:410
  63.5 1.5 collective-permute-start.5
  65.1 0.0 collective-permute-start.10
  65.1 0.5 collective-permute-start.8
  65.6 8.2 %collective-permute-done.5.refs_1_ = bf16[3,6,32,512]{3,2,1,0:T(8,128)(2,1)} collective-permute-done((bf16[3,6,32,512]{3,2,1,0:T(8,128)(2,1)}, bf16[3,6,32,512]{3,2,1,0:T(8,128)(2,1)}, u32[]{:S(2)}, u32[]{:S(2)}) %collective-permute-start.5) | collective-permute-done | bytes 589856 | tf_op jit(solution)/shard_map/ppermute | solution.py:410
  73.7 0.0 all-to-all-done.1.refs_0_
  73.7 2.3 %shard_map.66 = (f32[8,128]{1,0:T(8,128)}, bf16[3,6,64,512]{3,2,1,0:T(8,128)(2,1)}) custom-call(s32[1]{0:T(128)} %bitcast.me, f32[8,128]{1,0:T(8,128)} %get-tuple-element.69.token_in, bf16[4,6,64,512]{3,2,1,0:T(8,128)(2,1)} %all-to-all-done.1.refs_0_), custom_call_target="tpu_custom_call", output_to_operand_aliasing={{0}: (1, {})} | custom-call | flops 1024 | bytes 1024 | tf_op jit(solution)/shard_map/pallas_call | solution.py:136
  76.1 0.6 collective-permute-start.14
  76.7 0.0 collective-permute-done.10.refs_13_
  76.7 1.5 collective-permute-start.15
  78.2 5.0 %all-to-all-start.2 = ((bf16[4,6,64,512]{3,2,1,0:T(8,128)(2,1)}), bf16[4,6,64,512]{3,2,1,0:T(8,128)(2,1)}, u32[]{:S(2)}, u32[]{:S(2)}) async-start(bf16[4,6,64,512]{3,2,1,0:T(8,128)(2,1)} %get-tuple-element.79), calls=%async_computation.2 | async-start | bytes 3145728 | tf_op jit(solution)/shard_map/all_to_all | solution.py:466
  83.2 0.0 collective-permute-done.7.refs_6_
  83.2 0.1 collective-permute-start.9
  83.3 0.5 collective-permute-start.12
  83.8 0.1 collective-permute-start.13
  83.9 0.1 reshape.330
  84.0 0.1 stack.35
  84.1 0.6 gather_fusion
  84.7 0.7 reshape.331.vb
  85.4 0.1 dynamic_slice.3
  85.4 0.8 copy.46.va
  86.2 0.9 collective-permute-done.12.refs_15_
  87.1 0.8 collective-permute-done.13.refs_16_
  87.9 14.0 %shard_map.67 = (f32[8,128]{1,0:T(8,128)}, f32[6,160,2048]{2,1,0:T(8,128)}) custom-call(s32[1]{0:T(128)} %bitcast.me, s32[4]{0:T(128)} %sizes.13, s32[16]{0:T(128)} %order.13, f32[16]{0:T(128)} %eps_occ.7, f32[160,1]{1,0:T(8,128)} %copy.46.va, f32[5,1,256]{2,1,0:T(1,128)} %reshape.331.vb, ...), custom_call_target="tpu_custom_call", output_to_operand_aliasing={{0}: (6, {})} | custom-call | flops 1024 | bytes 1024 | tf_op jit(solution)/shard_map/pallas_call | solution.py:368
  101.9 2.6 %collective-permute-done.14.refs_1_ = bf16[3,6,64,512]{3,2,1,0:T(8,128)(2,1)} collective-permute-done((bf16[3,6,64,512]{3,2,1,0:T(8,128)(2,1)}, bf16[3,6,64,512]{3,2,1,0:T(8,128)(2,1)}, u32[]{:S(2)}, u32[]{:S(2)}) %collective-permute-start.14) | collective-permute-done | bytes 1179680 | tf_op jit(solution)/shard_map/ppermute | solution.py:410
  104.5 0.3 collective-permute-done.15.refs_2_
  104.8 1.8 collective-permute-start.16
  106.6 0.0 collective-permute-start.17
  106.6 0.5 collective-permute-start.18
  107.1 0.0 collective-permute-start.19
  107.1 13.2 %all-to-all-done.2.refs_0_ = bf16[4,6,64,512]{3,2,1,0:T(8,128)(2,1)} async-done(((bf16[4,6,64,512]{3,2,1,0:T(8,128)(2,1)}), bf16[4,6,64,512]{3,2,1,0:T(8,128)(2,1)}, u32[]{:S(2)}, u32[]{:S(2)}) %all-to-all-start.2) | async-done | bytes 1572896 | tf_op jit(solution)/shard_map/all_to_all | solution.py:466
  120.3 2.3 %shard_map.69 = (f32[8,128]{1,0:T(8,128)}, bf16[3,6,64,512]{3,2,1,0:T(8,128)(2,1)}) custom-call(s32[1]{0:T(128)} %bitcast.me, f32[8,128]{1,0:T(8,128)} %get-tuple-element.78.token_in, bf16[4,6,64,512]{3,2,1,0:T(8,128)(2,1)} %all-to-all-done.2.refs_0_), custom_call_target="tpu_custom_call", output_to_operand_aliasing={{0}: (1, {})} | custom-call | flops 1024 | bytes 1024 | tf_op jit(solution)/shard_map/pallas_call | solution.py:136
  122.6 0.0 collective-permute-done.16.refs_1_
  122.6 0.1 collective-permute-start.20
  122.7 1.6 collective-permute-start.21
  124.3 0.0 collective-permute-done.17.refs_21_.refs_13_
  124.3 0.5 collective-permute-start.22
  124.8 1.1 collective-permute-done.20.refs_24_.refs_16_
  125.9 26.5 %shard_map.71 = (f32[8,128]{1,0:T(8,128)}, f32[6,160,2048]{2,1,0:T(8,128)}) custom-call(s32[1]{0:T(128)} %bitcast.me, s32[4]{0:T(128)} %sizes.13, s32[16]{0:T(128)} %order.13, f32[16]{0:T(128)} %eps_occ.7, f32[160,1]{1,0:T(8,128)} %copy.46.va, f32[5,1,256]{2,1,0:T(1,128)} %reshape.331.vb, ...), custom_call_target="tpu_custom_call", output_to_operand_aliasing={{0}: (6, {})} | custom-call | flops 1024 | bytes 1024 | tf_op jit(solution)/shard_map/pallas_call | solution.py:368
  152.4 0.0 collective-permute-done.22.refs_2_
  152.4 0.6 collective-permute-start.23
  153.0 0.8 collective-permute-start.24
  153.8 0.5 collective-permute-start.26
  154.3 19.8 %shard_map.73 = (f32[8,128]{1,0:T(8,128)}, f32[6,160,2048]{2,1,0:T(8,128)}) custom-call(s32[1]{0:T(128)} %bitcast.me, s32[4]{0:T(128)} %sizes.13, s32[16]{0:T(128)} %order.13, f32[16]{0:T(128)} %eps_occ.7, f32[160,1]{1,0:T(8,128)} %copy.46.va, f32[5,1,256]{2,1,0:T(1,128)} %reshape.331.vb, ...), custom_call_target="tpu_custom_call", output_to_operand_aliasing={{0}: (6, {})} | custom-call | flops 1024 | bytes 1024 | tf_op jit(solution)/shard_map/pallas_call | solution.py:368
  174.2 0.1 collective-permute-start.27
  174.3 3.1 %collective-permute-done.27.refs_16_ = bf16[3,6,64,512]{3,2,1,0:T(8,128)(2,1)} collective-permute-done((bf16[3,6,64,512]{3,2,1,0:T(8,128)(2,1)}, bf16[3,6,64,512]{3,2,1,0:T(8,128)(2,1)}, u32[]{:S(2)}, u32[]{:S(2)}) %collective-permute-start.27) | collective-permute-done | bytes 1179680 | tf_op jit(solution)/shard_map/ppermute | solution.py:413
  177.4 32.0 %shard_map.75 = (f32[8,128]{1,0:T(8,128)}, bf16[6,160,2048]{2,1,0:T(8,128)(2,1)}) custom-call(s32[1]{0:T(128)} %bitcast.me, s32[4]{0:T(128)} %sizes.13, s32[16]{0:T(128)} %order.13, f32[16]{0:T(128)} %eps_occ.7, f32[160,1]{1,0:T(8,128)} %copy.46.va, f32[5,1,256]{2,1,0:T(1,128)} %reshape.331.vb, ...), custom_call_target="tpu_custom_call", output_to_operand_aliasing={{0}: (6, {})} | custom-call | flops 1024 | bytes 1024 | tf_op jit(solution)/shard_map/pallas_call | solution.py:368
  (31 shorter events, 0.1 us)
Async XLA Ops:
  4.1 26.6 %all-to-all-start = ((bf16[4,6,32,512]{3,2,1,0:T(8,128)(2,1)}), bf16[4,6,32,512]{3,2,1,0:T(8,128)(2,1)}, u32[]{:S(2)}, u32[]{:S(2)}) async-start(bf16[4,6,32,512]{3,2,1,0:T(8,128)(2,1)} %get-tuple-element.60), calls=%async_computation | async-start | bytes 1572864 | tf_op jit(solution)/shard_map/all_to_all | solution.py:466
  10.5 26.6 %collective-permute-start = (bf16[6,160,512]{2,1,0:T(8,128)(2,1)}, bf16[6,160,512]{2,1,0:T(8,128)(2,1)}, u32[]{:S(2)}, u32[]{:S(2)}) collective-permute-start(bf16[6,160,512]{2,1,0:T(8,128)(2,1)} %get-tuple-element.62.refs_1_), channel_id=1, source_target_pairs={{0,2},{1,5},{2,0},{3,7},{4,6},{5,1},{6,4},{7,3},{8,10},{9,13},{10,... | collective-permute-start | bytes 2949128 | tf_op jit(solution)/shard_map/ppermute | solution.py:410
  12.0 25.1 %collective-permute-start.1 = (bf16[6,160,512]{2,1,0:T(8,128)(2,1)}, bf16[6,160,512]{2,1,0:T(8,128)(2,1)}, u32[]{:S(2)}, u32[]{:S(2)}) collective-permute-start(bf16[6,160,512]{2,1,0:T(8,128)(2,1)} %get-tuple-element.62.refs_1_), channel_id=1, source_target_pairs={{0,4},{1,3},{2,6},{3,1},{4,0},{5,7},{6,2},{7,5},{8,12},{9,11},{10,... | collective-permute-start | bytes 2949128 | tf_op jit(solution)/shard_map/ppermute | solution.py:410
  30.7 43.0 %all-to-all-start.1 = ((bf16[4,6,64,512]{3,2,1,0:T(8,128)(2,1)}), bf16[4,6,64,512]{3,2,1,0:T(8,128)(2,1)}, u32[]{:S(2)}, u32[]{:S(2)}) async-start(bf16[4,6,64,512]{3,2,1,0:T(8,128)(2,1)} %get-tuple-element.70), calls=%async_computation.1 | async-start | bytes 3145728 | tf_op jit(solution)/shard_map/all_to_all | solution.py:466
  37.1 20.1 %collective-permute-start.2 = (bf16[6,160,512]{2,1,0:T(8,128)(2,1)}, bf16[6,160,512]{2,1,0:T(8,128)(2,1)}, u32[]{:S(2)}, u32[]{:S(2)}) collective-permute-start(bf16[6,160,512]{2,1,0:T(8,128)(2,1)} %get-tuple-element.64.refs_2_), channel_id=1, source_target_pairs={{0,4},{1,3},{2,6},{3,1},{4,0},{5,7},{6,2},{7,5},{8,12},{9,11},{10,... | collective-permute-start | bytes 2949128 | tf_op jit(solution)/shard_map/ppermute | solution.py:410
  38.7 18.5 %collective-permute-start.3 = (bf16[3,6,32,512]{3,2,1,0:T(8,128)(2,1)}, bf16[3,6,32,512]{3,2,1,0:T(8,128)(2,1)}, u32[]{:S(2)}, u32[]{:S(2)}) collective-permute-start(bf16[3,6,32,512]{3,2,1,0:T(8,128)(2,1)} %get-tuple-element.66.refs_9_.refs_17_), channel_id=1, source_target_pairs={{0,2},{1,5},{2,0},{3,7},{4,6},{5,1},{6,4},{7,3},{8,10},{9,13},{10,... | collective-permute-start | bytes 1769480 | tf_op jit(solution)/shard_map/ppermute | solution.py:410
  40.2 23.3 %collective-permute-start.4 = (bf16[3,6,32,512]{3,2,1,0:T(8,128)(2,1)}, bf16[3,6,32,512]{3,2,1,0:T(8,128)(2,1)}, u32[]{:S(2)}, u32[]{:S(2)}) collective-permute-start(bf16[3,6,32,512]{3,2,1,0:T(8,128)(2,1)} %get-tuple-element.66.refs_9_.refs_17_), channel_id=1, source_target_pairs={{0,4},{1,3},{2,6},{3,1},{4,0},{5,7},{6,2},{7,5},{8,12},{9,11},{10,... | collective-permute-start | bytes 1769480 | tf_op jit(solution)/shard_map/ppermute | solution.py:410
  40.7 35.4 %collective-permute-start.6 = (bf16[6,160,512]{2,1,0:T(8,128)(2,1)}, bf16[6,160,512]{2,1,0:T(8,128)(2,1)}, u32[]{:S(2)}, u32[]{:S(2)}) collective-permute-start(bf16[6,160,512]{2,1,0:T(8,128)(2,1)} %get-tuple-element.62.refs_1_), channel_id=1, source_target_pairs={{0,1},{1,0},{2,3},{3,2},{4,5},{5,4},{6,7},{7,6},{8,9},{9,8},{10,11... | collective-permute-start | bytes 2949128 | tf_op jit(solution)/shard_map/ppermute | solution.py:413
  40.7 42.5 %collective-permute-start.7 = (bf16[6,160,512]{2,1,0:T(8,128)(2,1)}, bf16[6,160,512]{2,1,0:T(8,128)(2,1)}, u32[]{:S(2)}, u32[]{:S(2)}) collective-permute-start(bf16[6,160,512]{2,1,0:T(8,128)(2,1)} %get-tuple-element.64.refs_2_), channel_id=1, source_target_pairs={{0,1},{1,0},{2,3},{3,2},{4,5},{5,4},{6,7},{7,6},{8,9},{9,8},{10,11... | collective-permute-start | bytes 2949128 | tf_op jit(solution)/shard_map/ppermute | solution.py:413
  63.5 10.2 %collective-permute-start.5 = (bf16[3,6,32,512]{3,2,1,0:T(8,128)(2,1)}, bf16[3,6,32,512]{3,2,1,0:T(8,128)(2,1)}, u32[]{:S(2)}, u32[]{:S(2)}) collective-permute-start(bf16[3,6,32,512]{3,2,1,0:T(8,128)(2,1)} %get-tuple-element.68.refs_10_), channel_id=1, source_target_pairs={{0,4},{1,3},{2,6},{3,1},{4,0},{5,7},{6,2},{7,5},{8,12},{9,11},{10,... | collective-permute-start | bytes 1769480 | tf_op jit(solution)/shard_map/ppermute | solution.py:410
  65.1 11.6 %collective-permute-start.10 = (bf16[3,6,32,512]{3,2,1,0:T(8,128)(2,1)}, bf16[3,6,32,512]{3,2,1,0:T(8,128)(2,1)}, u32[]{:S(2)}, u32[]{:S(2)}) collective-permute-start(bf16[3,6,32,512]{3,2,1,0:T(8,128)(2,1)} %get-tuple-element.66.refs_9_.refs_17_), channel_id=1, source_target_pairs={{0,1},{1,0},{2,3},{3,2},{4,5},{5,4},{6,7},{7,6},{8,9},{9,8},{10,11... | collective-permute-start | bytes 1769480 | tf_op jit(solution)/shard_map/ppermute | solution.py:413
  65.1 18.3 %collective-permute-start.8 = (bf16[6,160,512]{2,1,0:T(8,128)(2,1)}, bf16[6,160,512]{2,1,0:T(8,128)(2,1)}, u32[]{:S(2)}, u32[]{:S(2)}) collective-permute-start(bf16[6,160,512]{2,1,0:T(8,128)(2,1)} %get-tuple-element.72.refs_3_), channel_id=1, source_target_pairs={{0,1},{1,0},{2,3},{3,2},{4,5},{5,4},{6,7},{7,6},{8,9},{9,8},{10,11... | collective-permute-start | bytes 2949128 | tf_op jit(solution)/shard_map/ppermute | solution.py:413
  73.7 10.1 %collective-permute-start.11 = (bf16[3,6,32,512]{3,2,1,0:T(8,128)(2,1)}, bf16[3,6,32,512]{3,2,1,0:T(8,128)(2,1)}, u32[]{:S(2)}, u32[]{:S(2)}) collective-permute-start(bf16[3,6,32,512]{3,2,1,0:T(8,128)(2,1)} %get-tuple-element.68.refs_10_), channel_id=1, source_target_pairs={{0,1},{1,0},{2,3},{3,2},{4,5},{5,4},{6,7},{7,6},{8,9},{9,8},{10,11... | collective-permute-start | bytes 1769480 | tf_op jit(solution)/shard_map/ppermute | solution.py:413
  76.1 28.5 %collective-permute-start.14 = (bf16[3,6,64,512]{3,2,1,0:T(8,128)(2,1)}, bf16[3,6,64,512]{3,2,1,0:T(8,128)(2,1)}, u32[]{:S(2)}, u32[]{:S(2)}) collective-permute-start(bf16[3,6,64,512]{3,2,1,0:T(8,128)(2,1)} %get-tuple-element.76.refs_17_.refs_9_.refs_18_), channel_id=1, source_target_pairs={{0,2},{1,5},{2,0},{3,7},{4,6},{5,1},{6,4},{7,3},{8,10},{9,13},{10,... | collective-permute-start | bytes 3538952 | tf_op jit(solution)/shard_map/ppermute | solution.py:410
  76.7 28.2 %collective-permute-start.15 = (bf16[3,6,64,512]{3,2,1,0:T(8,128)(2,1)}, bf16[3,6,64,512]{3,2,1,0:T(8,128)(2,1)}, u32[]{:S(2)}, u32[]{:S(2)}) collective-permute-start(bf16[3,6,64,512]{3,2,1,0:T(8,128)(2,1)} %get-tuple-element.76.refs_17_.refs_9_.refs_18_), channel_id=1, source_target_pairs={{0,4},{1,3},{2,6},{3,1},{4,0},{5,7},{6,2},{7,5},{8,12},{9,11},{10,... | collective-permute-start | bytes 3538952 | tf_op jit(solution)/shard_map/ppermute | solution.py:410
  78.2 5.7 %copy-start = (f32[1280]{0:T(1024)S(1)}, f32[1280]{0:T(1024)}, u32[]{:S(2)}) copy-start(f32[1280]{0:T(1024)} %param.9) | copy-start | bytes 15364
  78.2 42.1 %all-to-all-start.2 = ((bf16[4,6,64,512]{3,2,1,0:T(8,128)(2,1)}), bf16[4,6,64,512]{3,2,1,0:T(8,128)(2,1)}, u32[]{:S(2)}, u32[]{:S(2)}) async-start(bf16[4,6,64,512]{3,2,1,0:T(8,128)(2,1)} %get-tuple-element.79), calls=%async_computation.2 | async-start | bytes 3145728 | tf_op jit(solution)/shard_map/all_to_all | solution.py:466
  83.2 3.8 %collective-permute-start.9 = (bf16[6,160,512]{2,1,0:T(8,128)(2,1)}, bf16[6,160,512]{2,1,0:T(8,128)(2,1)}, u32[]{:S(2)}, u32[]{:S(2)}) collective-permute-start(bf16[6,160,512]{2,1,0:T(8,128)(2,1)} %get-tuple-element.73.refs_4_), channel_id=1, source_target_pairs={{0,1},{1,0},{2,3},{3,2},{4,5},{5,4},{6,7},{7,6},{8,9},{9,8},{10,11... | collective-permute-start | bytes 2949128 | tf_op jit(solution)/shard_map/ppermute | solution.py:413
  83.3 3.7 %collective-permute-start.12 = (bf16[3,6,32,512]{3,2,1,0:T(8,128)(2,1)}, bf16[3,6,32,512]{3,2,1,0:T(8,128)(2,1)}, u32[]{:S(2)}, u32[]{:S(2)}) collective-permute-start(bf16[3,6,32,512]{3,2,1,0:T(8,128)(2,1)} %get-tuple-element.74.refs_11_), channel_id=1, source_target_pairs={{0,1},{1,0},{2,3},{3,2},{4,5},{5,4},{6,7},{7,6},{8,9},{9,8},{10,11... | collective-permute-start | bytes 1769480 | tf_op jit(solution)/shard_map/ppermute | solution.py:413
  83.8 4.1 %collective-permute-start.13 = (bf16[3,6,32,512]{3,2,1,0:T(8,128)(2,1)}, bf16[3,6,32,512]{3,2,1,0:T(8,128)(2,1)}, u32[]{:S(2)}, u32[]{:S(2)}) collective-permute-start(bf16[3,6,32,512]{3,2,1,0:T(8,128)(2,1)} %get-tuple-element.75.refs_12_), channel_id=1, source_target_pairs={{0,1},{1,0},{2,3},{3,2},{4,5},{5,4},{6,7},{7,6},{8,9},{9,8},{10,11... | collective-permute-start | bytes 1769480 | tf_op jit(solution)/shard_map/ppermute | solution.py:413
  104.8 17.8 %collective-permute-start.16 = (bf16[3,6,64,512]{3,2,1,0:T(8,128)(2,1)}, bf16[3,6,64,512]{3,2,1,0:T(8,128)(2,1)}, u32[]{:S(2)}, u32[]{:S(2)}) collective-permute-start(bf16[3,6,64,512]{3,2,1,0:T(8,128)(2,1)} %get-tuple-element.81.refs_18_.refs_10_), channel_id=1, source_target_pairs={{0,4},{1,3},{2,6},{3,1},{4,0},{5,7},{6,2},{7,5},{8,12},{9,11},{10,... | collective-permute-start | bytes 3538952 | tf_op jit(solution)/shard_map/ppermute | solution.py:410
  106.6 17.7 %collective-permute-start.17 = (bf16[3,6,64,512]{3,2,1,0:T(8,128)(2,1)}, bf16[3,6,64,512]{3,2,1,0:T(8,128)(2,1)}, u32[]{:S(2)}, u32[]{:S(2)}) collective-permute-start(bf16[3,6,64,512]{3,2,1,0:T(8,128)(2,1)} %get-tuple-element.76.refs_17_.refs_9_.refs_18_), channel_id=1, source_target_pairs={{0,1},{1,0},{2,3},{3,2},{4,5},{5,4},{6,7},{7,6},{8,9},{9,8},{10,11... | collective-permute-start | bytes 3538952 | tf_op jit(solution)/shard_map/ppermute | solution.py:413
  106.6 18.2 %collective-permute-start.18 = (bf16[3,6,64,512]{3,2,1,0:T(8,128)(2,1)}, bf16[3,6,64,512]{3,2,1,0:T(8,128)(2,1)}, u32[]{:S(2)}, u32[]{:S(2)}) collective-permute-start(bf16[3,6,64,512]{3,2,1,0:T(8,128)(2,1)} %get-tuple-element.81.refs_18_.refs_10_), channel_id=1, source_target_pairs={{0,1},{1,0},{2,3},{3,2},{4,5},{5,4},{6,7},{7,6},{8,9},{9,8},{10,11... | collective-permute-start | bytes 3538952 | tf_op jit(solution)/shard_map/ppermute | solution.py:413
  107.1 17.7 %collective-permute-start.19 = (bf16[3,6,64,512]{3,2,1,0:T(8,128)(2,1)}, bf16[3,6,64,512]{3,2,1,0:T(8,128)(2,1)}, u32[]{:S(2)}, u32[]{:S(2)}) collective-permute-start(bf16[3,6,64,512]{3,2,1,0:T(8,128)(2,1)} %get-tuple-element.83.refs_19_.refs_11_), channel_id=1, source_target_pairs={{0,1},{1,0},{2,3},{3,2},{4,5},{5,4},{6,7},{7,6},{8,9},{9,8},{10,11... | collective-permute-start | bytes 3538952 | tf_op jit(solution)/shard_map/ppermute | solution.py:413
  122.6 3.3 %collective-permute-start.20 = (bf16[3,6,64,512]{3,2,1,0:T(8,128)(2,1)}, bf16[3,6,64,512]{3,2,1,0:T(8,128)(2,1)}, u32[]{:S(2)}, u32[]{:S(2)}) collective-permute-start(bf16[3,6,64,512]{3,2,1,0:T(8,128)(2,1)} %get-tuple-element.84.refs_20_.refs_12_), channel_id=1, source_target_pairs={{0,1},{1,0},{2,3},{3,2},{4,5},{5,4},{6,7},{7,6},{8,9},{9,8},{10,11... | collective-permute-start | bytes 3538952 | tf_op jit(solution)/shard_map/ppermute | solution.py:413
  122.7 29.7 %collective-permute-start.21 = (bf16[3,6,64,512]{3,2,1,0:T(8,128)(2,1)}, bf16[3,6,64,512]{3,2,1,0:T(8,128)(2,1)}, u32[]{:S(2)}, u32[]{:S(2)}) collective-permute-start(bf16[3,6,64,512]{3,2,1,0:T(8,128)(2,1)} %get-tuple-element.85.refs_25_.refs_18_.refs_9_), channel_id=1, source_target_pairs={{0,2},{1,5},{2,0},{3,7},{4,6},{5,1},{6,4},{7,3},{8,10},{9,13},{10,... | collective-permute-start | bytes 3538952 | tf_op jit(solution)/shard_map/ppermute | solution.py:410
  124.3 28.1 %collective-permute-start.22 = (bf16[3,6,64,512]{3,2,1,0:T(8,128)(2,1)}, bf16[3,6,64,512]{3,2,1,0:T(8,128)(2,1)}, u32[]{:S(2)}, u32[]{:S(2)}) collective-permute-start(bf16[3,6,64,512]{3,2,1,0:T(8,128)(2,1)} %get-tuple-element.85.refs_25_.refs_18_.refs_9_), channel_id=1, source_target_pairs={{0,4},{1,3},{2,6},{3,1},{4,0},{5,7},{6,2},{7,5},{8,12},{9,11},{10,... | collective-permute-start | bytes 3538952 | tf_op jit(solution)/shard_map/ppermute | solution.py:410
  152.4 21.8 %collective-permute-start.23 = (bf16[3,6,64,512]{3,2,1,0:T(8,128)(2,1)}, bf16[3,6,64,512]{3,2,1,0:T(8,128)(2,1)}, u32[]{:S(2)}, u32[]{:S(2)}) collective-permute-start(bf16[3,6,64,512]{3,2,1,0:T(8,128)(2,1)} %get-tuple-element.91.refs_10_), channel_id=1, source_target_pairs={{0,4},{1,3},{2,6},{3,1},{4,0},{5,7},{6,2},{7,5},{8,12},{9,11},{10,... | collective-permute-start | bytes 3538952 | tf_op jit(solution)/shard_map/ppermute | solution.py:410
  153.0 21.3 %collective-permute-start.24 = (bf16[3,6,64,512]{3,2,1,0:T(8,128)(2,1)}, bf16[3,6,64,512]{3,2,1,0:T(8,128)(2,1)}, u32[]{:S(2)}, u32[]{:S(2)}) collective-permute-start(bf16[3,6,64,512]{3,2,1,0:T(8,128)(2,1)} %get-tuple-element.85.refs_25_.refs_18_.refs_9_), channel_id=1, source_target_pairs={{0,1},{1,0},{2,3},{3,2},{4,5},{5,4},{6,7},{7,6},{8,9},{9,8},{10,11... | collective-permute-start | bytes 3538952 | tf_op jit(solution)/shard_map/ppermute | solution.py:413
  153.8 20.5 %collective-permute-start.25 = (bf16[3,6,64,512]{3,2,1,0:T(8,128)(2,1)}, bf16[3,6,64,512]{3,2,1,0:T(8,128)(2,1)}, u32[]{:S(2)}, u32[]{:S(2)}) collective-permute-start(bf16[3,6,64,512]{3,2,1,0:T(8,128)(2,1)} %get-tuple-element.91.refs_10_), channel_id=1, source_target_pairs={{0,1},{1,0},{2,3},{3,2},{4,5},{5,4},{6,7},{7,6},{8,9},{9,8},{10,11... | collective-permute-start | bytes 3538952 | tf_op jit(solution)/shard_map/ppermute | solution.py:413
  153.8 20.5 %collective-permute-start.26 = (bf16[3,6,64,512]{3,2,1,0:T(8,128)(2,1)}, bf16[3,6,64,512]{3,2,1,0:T(8,128)(2,1)}, u32[]{:S(2)}, u32[]{:S(2)}) collective-permute-start(bf16[3,6,64,512]{3,2,1,0:T(8,128)(2,1)} %get-tuple-element.93.refs_11_), channel_id=1, source_target_pairs={{0,1},{1,0},{2,3},{3,2},{4,5},{5,4},{6,7},{7,6},{8,9},{9,8},{10,11... | collective-permute-start | bytes 3538952 | tf_op jit(solution)/shard_map/ppermute | solution.py:413
  174.2 3.3 %collective-permute-start.27 = (bf16[3,6,64,512]{3,2,1,0:T(8,128)(2,1)}, bf16[3,6,64,512]{3,2,1,0:T(8,128)(2,1)}, u32[]{:S(2)}, u32[]{:S(2)}) collective-permute-start(bf16[3,6,64,512]{3,2,1,0:T(8,128)(2,1)} %get-tuple-element.94.refs_12_), channel_id=1, source_target_pairs={{0,1},{1,0},{2,3},{3,2},{4,5},{5,4},{6,7},{7,6},{8,9},{9,8},{10,11... | collective-permute-start | bytes 3538952 | tf_op jit(solution)/shard_map/ppermute | solution.py:413
where the time goes:
time: 213 us; the launch traced here: 210 us
  Pallas kernels  109 us (51%)
  waiting for transfers between devices  63.1 us (30%)
  starting transfers between devices  34.1 us (16%)
  local copies, waits for them, and re-layouts  2.83 us (1%)
    pallas_call x4, Pallas kernels, density(): pl.pallas_call(functools.partial(density_kernel, n_occ, n_blocks, cuts, j...  92.3 us
    ppermute x12, waiting for transfers between devices, hop(): return lax.ppermute(block, 'virt', pairs)  33.4 us
    all_to_all x3, waiting for transfers between devices, cross(): crossing.append([lax.all_to_all(gated[0], 'occ', 0, 0, tiled=True)])  23.7 us
    all_to_all x3, starting transfers between devices, cross(): crossing.append([lax.all_to_all(gated[0], 'occ', 0, 0, tiled=True)])  15.8 us
    ppermute x12, starting transfers between devices, hop(): return lax.ppermute(block, 'virt', pairs)  14.6 us
    pallas_call x3, Pallas kernels, stage(): pl.pallas_call(functools.partial(stage_kernel, n_occ, low, high, with_own...  10.2 us
    pallas_call x3, Pallas kernels, join(): pl.pallas_call(functools.partial(join_kernel, n_occ, len(got), parts), ou...  6.63 us
    ppermute x16, waiting for transfers between devices, sibling(): return lax.ppermute(block, 'virt', [(d, d ^ 1) for d in range(n_virt)])  5.99 us
  transfers between devices with their start and end apart: 31, of which 11 were waited for; matrix products, arithmetic and copies ran while one was open for 1% of the time, Pallas kernels for 35%

commit v1 on v0

--- a/solution.py
+++ b/solution.py
@@ -28,8 +28,11 @@
     ]
 
 
-def stage_kernel(n_occ, low, high, with_own, split, me, sizes, order, basis, token_in, *refs):
+def stage_kernel(n_occ, low, high, with_own, split, me, sizes, order, basis, *refs):
+    refs = refs if with_own else refs[1:]
     outs, own, (held, read, sent) = refs[1:-3], refs[-4], refs[-3:]
+    if with_own:
+        refs[0][...] = jnp.zeros(refs[0].shape, refs[0].dtype)
     reads = []
     copies = []
     rows = pl.ds(low, high - low)
@@ -77,20 +80,20 @@
     return pl.pallas_call(
         functools.partial(stage_kernel, n_occ, low, high, with_own, split),
         out_shape=[
-            jax.ShapeDtypeStruct(token.shape, token.dtype),
+            jax.ShapeDtypeStruct((8, 128), jnp.float32),
             *[jax.ShapeDtypeStruct(shape, basis.dtype) for shape in shapes],
         ],
-        in_specs=[SMEM, SMEM, SMEM, ANY, ANY],
-        out_specs=[ANY] * (1 + len(shapes)),
+        in_specs=[SMEM, SMEM, SMEM, ANY] + [ANY] * (not with_own),
+        out_specs=[VMEM if with_own else ANY] + [ANY] * len(shapes),
         scratch_shapes=[
             pltpu.VMEM((n_occ, CAP, width if with_own else high - low, aux), basis.dtype),
             pltpu.SemaphoreType.DMA((n_occ * CAP,)),
             pltpu.SemaphoreType.DMA((1 + n_occ,)),
         ],
-        input_output_aliases={4: 0},
+        input_output_aliases={} if with_own else {4: 0},
         compiler_params=pltpu.CompilerParams(vmem_limit_bytes=VMEM_LIMIT),
         cost_estimate=SMALL,
-    )(me, sizes, order, basis, token)
+    )(me, sizes, order, basis, *([] if with_own else [token]))
 
 
 def gate(token, needs=(), gives=()):
@@ -433,8 +436,7 @@
     cuts = z_parts
     starts = [sum(cuts[:c]) * part for c in range(len(cuts) + 1)]
     sends = []
-    token = jnp.zeros((8, 128), jnp.float32)
-    token, send, first = stage(token, basis, *scalars[:3], n_occ, 0, starts[1], with_own=True)
+    token, send, first = stage(None, basis, *scalars[:3], n_occ, 0, starts[1], with_own=True)
     sends.append([send])
     blocks = {}
 
@@ -496,12 +498,13 @@
         sends.append(send)
     for c in range(1, n_chunks):
         token = cross(token, c)
+    token, _ = gate(token, (va, vb))
     collect(0)
     token = relay(token, "first", 1)
     arrive("first")
     token = relay(token, 0, 1)
+    collect(1)
     arrive(0)
-    collect(1)
     early = cuts[0] + cuts[1]
     add([(0, early, (0,))])
     token = relay(token, 1, 1)

time: 213 us -> 210 us (0.986)
  waiting for transfers between devices: 63.1 us -> 60.4 us
    ppermute x12, waiting for transfers between devices: 33.4 us -> 24.1 us  [hop(): return lax.ppermute(block, 'virt', pairs)]
    all_to_all x3, waiting for transfers between devices: 23.7 us -> 27.6 us  [cross(): crossing.append([lax.all_to_all(gated[0], 'occ', 0, 0, tiled=True)])]
    ppermute x16, waiting for transfers between devices: 5.99 us -> 8.77 us  [sibling(): return lax.ppermute(block, 'virt', [(d, d ^ 1) for d in range(n_virt)])]
  transfers between devices with their start and end apart: 31 -> 31, of which waited for: 11 -> 10; matrix products, arithmetic and copies ran while one was open for 1% -> 1% of each run, Pallas kernels for 35% -> 36%
where the time goes in v1:
time: 210 us; the launch traced here: 206 us
  Pallas kernels  110 us (52%)
  waiting for transfers between devices  60.4 us (29%)
  starting transfers between devices  32.8 us (16%)
  local copies, waits for them, and re-layouts  2.9 us (1%)
    pallas_call x4, Pallas kernels, density(): pl.pallas_call(functools.partial(density_kernel, n_occ, n_blocks, cuts, j...  92.3 us
    all_to_all x3, waiting for transfers between devices, cross(): crossing.append([lax.all_to_all(gated[0], 'occ', 0, 0, tiled=True)])  27.6 us
    ppermute x12, waiting for transfers between devices, hop(): return lax.ppermute(block, 'virt', pairs)  24.1 us
    all_to_all x3, starting transfers between devices, cross(): crossing.append([lax.all_to_all(gated[0], 'occ', 0, 0, tiled=True)])  15.5 us
    ppermute x12, starting transfers between devices, hop(): return lax.ppermute(block, 'virt', pairs)  13.9 us
    pallas_call x3, Pallas kernels, stage(): pl.pallas_call(functools.partial(stage_kernel, n_occ, low, high, with_own...  10.6 us
    ppermute x16, waiting for transfers between devices, sibling(): return lax.ppermute(block, 'virt', [(d, d ^ 1) for d in range(n_virt)])  8.77 us
    pallas_call x3, Pallas kernels, join(): pl.pallas_call(functools.partial(join_kernel, n_occ, len(got), parts), ou...  6.62 us
  transfers between devices with their start and end apart: 31, of which 10 were waited for; matrix products, arithmetic and copies ran while one was open for 1% of the time, Pallas kernels for 36%

profile of v1, /device:TPU:0, one launch (start us, length us, event | category | flops | bytes accessed | tf_op | source)
XLA Modules:
  0.0 206.3 jit_solution(1537726504221070069)
XLA Ops:
  0.0 4.1 %shard_map.55 = (f32[8,128]{1,0:T(8,128)}, bf16[4,6,32,512]{3,2,1,0:T(8,128)(2,1)}, bf16[6,160,512]{2,1,0:T(8,128)(2,1)}) custom-call(s32[1]{0:T(128)} %bitcast.me, s32[4]{0:T(128)} %sizes.13, s32[16]{0:T(128)} %order.13, bf16[16,160,512]{2,1,0:T(8,128)(2,1)} %basis.5), custom_call_target="tpu_custom_call" | custom-call | flops 1024 | bytes 1024 | tf_op jit(solution)/shard_map/pallas_call | solution.py:80
  4.1 6.6 %all-to-all-start = ((bf16[4,6,32,512]{3,2,1,0:T(8,128)(2,1)}), bf16[4,6,32,512]{3,2,1,0:T(8,128)(2,1)}, u32[]{:S(2)}, u32[]{:S(2)}) async-start(bf16[4,6,32,512]{3,2,1,0:T(8,128)(2,1)} %get-tuple-element.60), calls=%async_computation | async-start | bytes 1572864 | tf_op jit(solution)/shard_map/all_to_all | solution.py:468
  10.7 1.5 collective-permute-start
  12.2 1.5 collective-permute-start.1
  13.7 3.3 %shard_map.57 = (f32[8,128]{1,0:T(8,128)}, bf16[4,6,64,512]{3,2,1,0:T(8,128)(2,1)}) custom-call(s32[1]{0:T(128)} %bitcast.me, s32[4]{0:T(128)} %sizes.13, s32[16]{0:T(128)} %order.13, bf16[16,160,512]{2,1,0:T(8,128)(2,1)} %basis.5, f32[8,128]{1,0:T(8,128)} %get-tuple-element.53.refs_0_), custom_call_target="tpu_custom_call", output_to_operand_aliasing={{0}: (4, {})} | custom-call | flops 1024 | bytes 1024 | tf_op jit(solution)/shard_map/pallas_call | solution.py:80
  17.0 3.3 %shard_map.58 = (f32[8,128]{1,0:T(8,128)}, bf16[4,6,64,512]{3,2,1,0:T(8,128)(2,1)}) custom-call(s32[1]{0:T(128)} %bitcast.me, s32[4]{0:T(128)} %sizes.13, s32[16]{0:T(128)} %order.13, bf16[16,160,512]{2,1,0:T(8,128)(2,1)} %basis.5, f32[8,128]{1,0:T(8,128)} %get-tuple-element.54.refs_0_), custom_call_target="tpu_custom_call", output_to_operand_aliasing={{0}: (4, {})} | custom-call | flops 1024 | bytes 1024 | tf_op jit(solution)/shard_map/pallas_call | solution.py:80
  20.3 10.6 %all-to-all-done.refs_0_ = bf16[4,6,32,512]{3,2,1,0:T(8,128)(2,1)} async-done(((bf16[4,6,32,512]{3,2,1,0:T(8,128)(2,1)}), bf16[4,6,32,512]{3,2,1,0:T(8,128)(2,1)}, u32[]{:S(2)}, u32[]{:S(2)}) %all-to-all-start) | async-done | bytes 786464 | tf_op jit(solution)/shard_map/all_to_all | solution.py:468
  30.9 4.4 %all-to-all-start.1 = ((bf16[4,6,64,512]{3,2,1,0:T(8,128)(2,1)}), bf16[4,6,64,512]{3,2,1,0:T(8,128)(2,1)}, u32[]{:S(2)}, u32[]{:S(2)}) async-start(bf16[4,6,64,512]{3,2,1,0:T(8,128)(2,1)} %get-tuple-element.68), calls=%async_computation.1 | async-start | bytes 3145728 | tf_op jit(solution)/shard_map/all_to_all | solution.py:468
  35.3 0.0 copy-start
  35.3 0.7 copy-done
  36.0 0.1 reshape.330
  36.1 0.1 stack.35
  36.2 0.6 gather_fusion
  36.8 0.7 reshape.331.refs_2_.vb
  37.4 0.1 dynamic_slice.3
  37.5 0.8 copy.47.refs_1_.va
  38.3 2.0 shard_map.62
  40.2 0.0 collective-permute-done.refs_1_
  40.3 1.6 collective-permute-start.2
  41.9 1.5 collective-permute-start.3
  43.3 0.5 collective-permute-start.4
  43.9 0.0 collective-permute-start.6
  43.9 0.5 collective-permute-start.7
  44.4 16.0 %collective-permute-done.2.refs_1_ = bf16[6,160,512]{2,1,0:T(8,128)(2,1)} collective-permute-done((bf16[6,160,512]{2,1,0:T(8,128)(2,1)}, bf16[6,160,512]{2,1,0:T(8,128)(2,1)}, u32[]{:S(2)}, u32[]{:S(2)}) %collective-permute-start.2) | collective-permute-done | bytes 983072 | tf_op jit(solution)/shard_map/ppermute | solution.py:413
  60.4 0.0 collective-permute-start.10
  60.4 0.5 collective-permute-start.8
  60.9 5.8 %collective-permute-done.4.refs_2_ = bf16[3,6,32,512]{3,2,1,0:T(8,128)(2,1)} collective-permute-done((bf16[3,6,32,512]{3,2,1,0:T(8,128)(2,1)}, bf16[3,6,32,512]{3,2,1,0:T(8,128)(2,1)}, u32[]{:S(2)}, u32[]{:S(2)}) %collective-permute-start.4) | collective-permute-done | bytes 589856 | tf_op jit(solution)/shard_map/ppermute | solution.py:413
  66.7 1.5 collective-permute-start.5
  68.2 3.6 %all-to-all-done.1.refs_0_ = bf16[4,6,64,512]{3,2,1,0:T(8,128)(2,1)} async-done(((bf16[4,6,64,512]{3,2,1,0:T(8,128)(2,1)}), bf16[4,6,64,512]{3,2,1,0:T(8,128)(2,1)}, u32[]{:S(2)}, u32[]{:S(2)}) %all-to-all-start.1) | async-done | bytes 1572896 | tf_op jit(solution)/shard_map/all_to_all | solution.py:468
  71.8 2.3 %shard_map.66 = (f32[8,128]{1,0:T(8,128)}, bf16[3,6,64,512]{3,2,1,0:T(8,128)(2,1)}) custom-call(s32[1]{0:T(128)} %bitcast.me, f32[8,128]{1,0:T(8,128)} %get-tuple-element.67.token_in, bf16[4,6,64,512]{3,2,1,0:T(8,128)(2,1)} %all-to-all-done.1.refs_0_), custom_call_target="tpu_custom_call", output_to_operand_aliasing={{0}: (1, {})} | custom-call | flops 1024 | bytes 1024 | tf_op jit(solution)/shard_map/pallas_call | solution.py:139
  74.1 1.6 collective-permute-start.14
  75.7 0.0 collective-permute-done.7.refs_6_
  75.7 1.5 collective-permute-start.15
  77.2 4.5 %all-to-all-start.2 = ((bf16[4,6,64,512]{3,2,1,0:T(8,128)(2,1)}), bf16[4,6,64,512]{3,2,1,0:T(8,128)(2,1)}, u32[]{:S(2)}, u32[]{:S(2)}) async-start(bf16[4,6,64,512]{3,2,1,0:T(8,128)(2,1)} %get-tuple-element.79), calls=%async_computation.2 | async-start | bytes 3145728 | tf_op jit(solution)/shard_map/all_to_all | solution.py:468
  81.8 0.0 collective-permute-done.5.refs_1_
  81.8 0.1 collective-permute-start.9
  81.9 0.5 collective-permute-start.12
  82.4 0.0 collective-permute-done.11.refs_14_
  82.4 0.1 collective-permute-start.13
  82.5 3.1 %collective-permute-done.12.refs_15_ = bf16[3,6,32,512]{3,2,1,0:T(8,128)(2,1)} collective-permute-done((bf16[3,6,32,512]{3,2,1,0:T(8,128)(2,1)}, bf16[3,6,32,512]{3,2,1,0:T(8,128)(2,1)}, u32[]{:S(2)}, u32[]{:S(2)}) %collective-permute-start.12) | collective-permute-done | bytes 589856 | tf_op jit(solution)/shard_map/ppermute | solution.py:416
  85.6 0.8 collective-permute-done.13.refs_16_
  86.5 14.0 %shard_map.68 = (f32[8,128]{1,0:T(8,128)}, f32[6,160,2048]{2,1,0:T(8,128)}) custom-call(s32[1]{0:T(128)} %bitcast.me, s32[4]{0:T(128)} %sizes.13, s32[16]{0:T(128)} %order.13, f32[16]{0:T(128)} %eps_occ.7, f32[160,1]{1,0:T(8,128)} %copy.47.refs_1_.va, f32[5,1,256]{2,1,0:T(1,128)} %reshape.331.refs_2_.vb, ...), custom_call_target="tpu_custom_call", output_to_operand_aliasing={{0}: (6, {})} | custom-call | flops 1024 | bytes 1024 | tf_op jit(solution)/shard_map/pallas_call | solution.py:371
  100.5 2.2 %collective-permute-done.14.refs_1_ = bf16[3,6,64,512]{3,2,1,0:T(8,128)(2,1)} collective-permute-done((bf16[3,6,64,512]{3,2,1,0:T(8,128)(2,1)}, bf16[3,6,64,512]{3,2,1,0:T(8,128)(2,1)}, u32[]{:S(2)}, u32[]{:S(2)}) %collective-permute-start.14) | collective-permute-done | bytes 1179680 | tf_op jit(solution)/shard_map/ppermute | solution.py:413
  102.7 1.0 collective-permute-start.16
  103.7 0.0 collective-permute-start.17
  103.7 0.5 collective-permute-start.18
  104.2 13.4 %all-to-all-done.2.refs_0_ = bf16[4,6,64,512]{3,2,1,0:T(8,128)(2,1)} async-done(((bf16[4,6,64,512]{3,2,1,0:T(8,128)(2,1)}), bf16[4,6,64,512]{3,2,1,0:T(8,128)(2,1)}, u32[]{:S(2)}, u32[]{:S(2)}) %all-to-all-start.2) | async-done | bytes 1572896 | tf_op jit(solution)/shard_map/all_to_all | solution.py:468
  117.6 2.3 %shard_map.70 = (f32[8,128]{1,0:T(8,128)}, bf16[3,6,64,512]{3,2,1,0:T(8,128)(2,1)}) custom-call(s32[1]{0:T(128)} %bitcast.me, f32[8,128]{1,0:T(8,128)} %get-tuple-element.78.token_in, bf16[4,6,64,512]{3,2,1,0:T(8,128)(2,1)} %all-to-all-done.2.refs_0_), custom_call_target="tpu_custom_call", output_to_operand_aliasing={{0}: (1, {})} | custom-call | flops 1024 | bytes 1024 | tf_op jit(solution)/shard_map/pallas_call | solution.py:139
  119.9 0.0 collective-permute-done.16.refs_1_
  119.9 0.1 collective-permute-start.20
  120.0 0.7 collective-permute-start.21
  120.7 0.0 collective-permute-done.17.refs_21_.refs_13_
  120.7 0.5 collective-permute-start.22
  121.2 0.0 collective-permute-done.19.refs_23_.refs_15_
  121.2 2.0 collective-permute-done.20.refs_24_.refs_16_
  123.2 26.5 %shard_map.72 = (f32[8,128]{1,0:T(8,128)}, f32[6,160,2048]{2,1,0:T(8,128)}) custom-call(s32[1]{0:T(128)} %bitcast.me, s32[4]{0:T(128)} %sizes.13, s32[16]{0:T(128)} %order.13, f32[16]{0:T(128)} %eps_occ.7, f32[160,1]{1,0:T(8,128)} %copy.47.refs_1_.va, f32[5,1,256]{2,1,0:T(1,128)} %reshape.331.refs_2_.vb, ...), custom_call_target="tpu_custom_call", output_to_operand_aliasing={{0}: (6, {})} | custom-call | flops 1024 | bytes 1024 | tf_op jit(solution)/shard_map/pallas_call | solution.py:371
  149.7 0.6 collective-permute-start.23
  150.3 0.1 collective-permute-start.24
  150.3 0.5 collective-permute-start.25
  150.8 0.1 collective-permute-start.26
  150.9 19.8 %shard_map.74 = (f32[8,128]{1,0:T(8,128)}, f32[6,160,2048]{2,1,0:T(8,128)}) custom-call(s32[1]{0:T(128)} %bitcast.me, s32[4]{0:T(128)} %sizes.13, s32[16]{0:T(128)} %order.13, f32[16]{0:T(128)} %eps_occ.7, f32[160,1]{1,0:T(8,128)} %copy.47.refs_1_.va, f32[5,1,256]{2,1,0:T(1,128)} %reshape.331.refs_2_.vb, ...), custom_call_target="tpu_custom_call", output_to_operand_aliasing={{0}: (6, {})} | custom-call | flops 1024 | bytes 1024 | tf_op jit(solution)/shard_map/pallas_call | solution.py:371
  170.7 0.5 collective-permute-start.27
  171.3 2.8 %collective-permute-done.27.refs_16_ = bf16[3,6,64,512]{3,2,1,0:T(8,128)(2,1)} collective-permute-done((bf16[3,6,64,512]{3,2,1,0:T(8,128)(2,1)}, bf16[3,6,64,512]{3,2,1,0:T(8,128)(2,1)}, u32[]{:S(2)}, u32[]{:S(2)}) %collective-permute-start.27) | collective-permute-done | bytes 1179680 | tf_op jit(solution)/shard_map/ppermute | solution.py:416
  174.1 32.0 %shard_map.76 = (f32[8,128]{1,0:T(8,128)}, bf16[6,160,2048]{2,1,0:T(8,128)(2,1)}) custom-call(s32[1]{0:T(128)} %bitcast.me, s32[4]{0:T(128)} %sizes.13, s32[16]{0:T(128)} %order.13, f32[16]{0:T(128)} %eps_occ.7, f32[160,1]{1,0:T(8,128)} %copy.47.refs_1_.va, f32[5,1,256]{2,1,0:T(1,128)} %reshape.331.refs_2_.vb, ...), custom_call_target="tpu_custom_call", output_to_operand_aliasing={{0}: (6, {})} | custom-call | flops 1024 | bytes 1024 | tf_op jit(solution)/shard_map/pallas_call | solution.py:371
  (31 shorter events, 0.1 us)
Async XLA Ops:
  4.1 26.8 %all-to-all-start = ((bf16[4,6,32,512]{3,2,1,0:T(8,128)(2,1)}), bf16[4,6,32,512]{3,2,1,0:T(8,128)(2,1)}, u32[]{:S(2)}, u32[]{:S(2)}) async-start(bf16[4,6,32,512]{3,2,1,0:T(8,128)(2,1)} %get-tuple-element.60), calls=%async_computation | async-start | bytes 1572864 | tf_op jit(solution)/shard_map/all_to_all | solution.py:468
  10.7 29.5 %collective-permute-start = (bf16[6,160,512]{2,1,0:T(8,128)(2,1)}, bf16[6,160,512]{2,1,0:T(8,128)(2,1)}, u32[]{:S(2)}, u32[]{:S(2)}) collective-permute-start(bf16[6,160,512]{2,1,0:T(8,128)(2,1)} %get-tuple-element.62.refs_1_), channel_id=1, source_target_pairs={{0,2},{1,5},{2,0},{3,7},{4,6},{5,1},{6,4},{7,3},{8,10},{9,13},{10,... | collective-permute-start | bytes 2949128 | tf_op jit(solution)/shard_map/ppermute | solution.py:413
  12.2 28.1 %collective-permute-start.1 = (bf16[6,160,512]{2,1,0:T(8,128)(2,1)}, bf16[6,160,512]{2,1,0:T(8,128)(2,1)}, u32[]{:S(2)}, u32[]{:S(2)}) collective-permute-start(bf16[6,160,512]{2,1,0:T(8,128)(2,1)} %get-tuple-element.62.refs_1_), channel_id=1, source_target_pairs={{0,4},{1,3},{2,6},{3,1},{4,0},{5,7},{6,2},{7,5},{8,12},{9,11},{10,... | collective-permute-start | bytes 2949128 | tf_op jit(solution)/shard_map/ppermute | solution.py:413
  30.9 40.9 %all-to-all-start.1 = ((bf16[4,6,64,512]{3,2,1,0:T(8,128)(2,1)}), bf16[4,6,64,512]{3,2,1,0:T(8,128)(2,1)}, u32[]{:S(2)}, u32[]{:S(2)}) async-start(bf16[4,6,64,512]{3,2,1,0:T(8,128)(2,1)} %get-tuple-element.68), calls=%async_computation.1 | async-start | bytes 3145728 | tf_op jit(solution)/shard_map/all_to_all | solution.py:468
  35.3 0.7 copy-start
  40.3 20.1 %collective-permute-start.2 = (bf16[6,160,512]{2,1,0:T(8,128)(2,1)}, bf16[6,160,512]{2,1,0:T(8,128)(2,1)}, u32[]{:S(2)}, u32[]{:S(2)}) collective-permute-start(bf16[6,160,512]{2,1,0:T(8,128)(2,1)} %get-tuple-element.64.refs_2_), channel_id=1, source_target_pairs={{0,4},{1,3},{2,6},{3,1},{4,0},{5,7},{6,2},{7,5},{8,12},{9,11},{10,... | collective-permute-start | bytes 2949128 | tf_op jit(solution)/shard_map/ppermute | solution.py:413
  41.9 18.5 %collective-permute-start.3 = (bf16[3,6,32,512]{3,2,1,0:T(8,128)(2,1)}, bf16[3,6,32,512]{3,2,1,0:T(8,128)(2,1)}, u32[]{:S(2)}, u32[]{:S(2)}) collective-permute-start(bf16[3,6,32,512]{3,2,1,0:T(8,128)(2,1)} %get-tuple-element.66.refs_9_.refs_17_), channel_id=1, source_target_pairs={{0,2},{1,5},{2,0},{3,7},{4,6},{5,1},{6,4},{7,3},{8,10},{9,13},{10,... | collective-permute-start | bytes 1769480 | tf_op jit(solution)/shard_map/ppermute | solution.py:413
  43.3 23.3 %collective-permute-start.4 = (bf16[3,6,32,512]{3,2,1,0:T(8,128)(2,1)}, bf16[3,6,32,512]{3,2,1,0:T(8,128)(2,1)}, u32[]{:S(2)}, u32[]{:S(2)}) collective-permute-start(bf16[3,6,32,512]{3,2,1,0:T(8,128)(2,1)} %get-tuple-element.66.refs_9_.refs_17_), channel_id=1, source_target_pairs={{0,4},{1,3},{2,6},{3,1},{4,0},{5,7},{6,2},{7,5},{8,12},{9,11},{10,... | collective-permute-start | bytes 1769480 | tf_op jit(solution)/shard_map/ppermute | solution.py:413
  43.9 24.4 %collective-permute-start.6 = (bf16[6,160,512]{2,1,0:T(8,128)(2,1)}, bf16[6,160,512]{2,1,0:T(8,128)(2,1)}, u32[]{:S(2)}, u32[]{:S(2)}) collective-permute-start(bf16[6,160,512]{2,1,0:T(8,128)(2,1)} %get-tuple-element.62.refs_1_), channel_id=1, source_target_pairs={{0,1},{1,0},{2,3},{3,2},{4,5},{5,4},{6,7},{7,6},{8,9},{9,8},{10,11... | collective-permute-start | bytes 2949128 | tf_op jit(solution)/shard_map/ppermute | solution.py:416
  43.9 31.8 %collective-permute-start.7 = (bf16[6,160,512]{2,1,0:T(8,128)(2,1)}, bf16[6,160,512]{2,1,0:T(8,128)(2,1)}, u32[]{:S(2)}, u32[]{:S(2)}) collective-permute-start(bf16[6,160,512]{2,1,0:T(8,128)(2,1)} %get-tuple-element.64.refs_2_), channel_id=1, source_target_pairs={{0,1},{1,0},{2,3},{3,2},{4,5},{5,4},{6,7},{7,6},{8,9},{9,8},{10,11... | collective-permute-start | bytes 2949128 | tf_op jit(solution)/shard_map/ppermute | solution.py:416
  60.4 13.8 %collective-permute-start.10 = (bf16[3,6,32,512]{3,2,1,0:T(8,128)(2,1)}, bf16[3,6,32,512]{3,2,1,0:T(8,128)(2,1)}, u32[]{:S(2)}, u32[]{:S(2)}) collective-permute-start(bf16[3,6,32,512]{3,2,1,0:T(8,128)(2,1)} %get-tuple-element.66.refs_9_.refs_17_), channel_id=1, source_target_pairs={{0,1},{1,0},{2,3},{3,2},{4,5},{5,4},{6,7},{7,6},{8,9},{9,8},{10,11... | collective-permute-start | bytes 1769480 | tf_op jit(solution)/shard_map/ppermute | solution.py:416
  60.4 21.5 %collective-permute-start.8 = (bf16[6,160,512]{2,1,0:T(8,128)(2,1)}, bf16[6,160,512]{2,1,0:T(8,128)(2,1)}, u32[]{:S(2)}, u32[]{:S(2)}) collective-permute-start(bf16[6,160,512]{2,1,0:T(8,128)(2,1)} %get-tuple-element.72.refs_3_), channel_id=1, source_target_pairs={{0,1},{1,0},{2,3},{3,2},{4,5},{5,4},{6,7},{7,6},{8,9},{9,8},{10,11... | collective-permute-start | bytes 2949128 | tf_op jit(solution)/shard_map/ppermute | solution.py:416
  66.7 15.1 %collective-permute-start.5 = (bf16[3,6,32,512]{3,2,1,0:T(8,128)(2,1)}, bf16[3,6,32,512]{3,2,1,0:T(8,128)(2,1)}, u32[]{:S(2)}, u32[]{:S(2)}) collective-permute-start(bf16[3,6,32,512]{3,2,1,0:T(8,128)(2,1)} %get-tuple-element.70.refs_10_), channel_id=1, source_target_pairs={{0,4},{1,3},{2,6},{3,1},{4,0},{5,7},{6,2},{7,5},{8,12},{9,11},{10,... | collective-permute-start | bytes 1769480 | tf_op jit(solution)/shard_map/ppermute | solution.py:413
  68.2 14.2 %collective-permute-start.11 = (bf16[3,6,32,512]{3,2,1,0:T(8,128)(2,1)}, bf16[3,6,32,512]{3,2,1,0:T(8,128)(2,1)}, u32[]{:S(2)}, u32[]{:S(2)}) collective-permute-start(bf16[3,6,32,512]{3,2,1,0:T(8,128)(2,1)} %get-tuple-element.70.refs_10_), channel_id=1, source_target_pairs={{0,1},{1,0},{2,3},{3,2},{4,5},{5,4},{6,7},{7,6},{8,9},{9,8},{10,11... | collective-permute-start | bytes 1769480 | tf_op jit(solution)/shard_map/ppermute | solution.py:416
  74.1 28.5 %collective-permute-start.14 = (bf16[3,6,64,512]{3,2,1,0:T(8,128)(2,1)}, bf16[3,6,64,512]{3,2,1,0:T(8,128)(2,1)}, u32[]{:S(2)}, u32[]{:S(2)}) collective-permute-start(bf16[3,6,64,512]{3,2,1,0:T(8,128)(2,1)} %get-tuple-element.76.refs_17_.refs_9_.refs_18_), channel_id=1, source_target_pairs={{0,2},{1,5},{2,0},{3,7},{4,6},{5,1},{6,4},{7,3},{8,10},{9,13},{10,... | collective-permute-start | bytes 3538952 | tf_op jit(solution)/shard_map/ppermute | solution.py:413
  75.7 27.0 %collective-permute-start.15 = (bf16[3,6,64,512]{3,2,1,0:T(8,128)(2,1)}, bf16[3,6,64,512]{3,2,1,0:T(8,128)(2,1)}, u32[]{:S(2)}, u32[]{:S(2)}) collective-permute-start(bf16[3,6,64,512]{3,2,1,0:T(8,128)(2,1)} %get-tuple-element.76.refs_17_.refs_9_.refs_18_), channel_id=1, source_target_pairs={{0,4},{1,3},{2,6},{3,1},{4,0},{5,7},{6,2},{7,5},{8,12},{9,11},{10,... | collective-permute-start | bytes 3538952 | tf_op jit(solution)/shard_map/ppermute | solution.py:413
  77.2 40.3 %all-to-all-start.2 = ((bf16[4,6,64,512]{3,2,1,0:T(8,128)(2,1)}), bf16[4,6,64,512]{3,2,1,0:T(8,128)(2,1)}, u32[]{:S(2)}, u32[]{:S(2)}) async-start(bf16[4,6,64,512]{3,2,1,0:T(8,128)(2,1)} %get-tuple-element.79), calls=%async_computation.2 | async-start | bytes 3145728 | tf_op jit(solution)/shard_map/all_to_all | solution.py:468
  81.8 3.8 %collective-permute-start.9 = (bf16[6,160,512]{2,1,0:T(8,128)(2,1)}, bf16[6,160,512]{2,1,0:T(8,128)(2,1)}, u32[]{:S(2)}, u32[]{:S(2)}) collective-permute-start(bf16[6,160,512]{2,1,0:T(8,128)(2,1)} %get-tuple-element.73.refs_4_), channel_id=1, source_target_pairs={{0,1},{1,0},{2,3},{3,2},{4,5},{5,4},{6,7},{7,6},{8,9},{9,8},{10,11... | collective-permute-start | bytes 2949128 | tf_op jit(solution)/shard_map/ppermute | solution.py:416
  81.9 3.7 %collective-permute-start.12 = (bf16[3,6,32,512]{3,2,1,0:T(8,128)(2,1)}, bf16[3,6,32,512]{3,2,1,0:T(8,128)(2,1)}, u32[]{:S(2)}, u32[]{:S(2)}) collective-permute-start(bf16[3,6,32,512]{3,2,1,0:T(8,128)(2,1)} %get-tuple-element.74.refs_11_), channel_id=1, source_target_pairs={{0,1},{1,0},{2,3},{3,2},{4,5},{5,4},{6,7},{7,6},{8,9},{9,8},{10,11... | collective-permute-start | bytes 1769480 | tf_op jit(solution)/shard_map/ppermute | solution.py:416
  82.4 4.1 %collective-permute-start.13 = (bf16[3,6,32,512]{3,2,1,0:T(8,128)(2,1)}, bf16[3,6,32,512]{3,2,1,0:T(8,128)(2,1)}, u32[]{:S(2)}, u32[]{:S(2)}) collective-permute-start(bf16[3,6,32,512]{3,2,1,0:T(8,128)(2,1)} %get-tuple-element.75.refs_12_), channel_id=1, source_target_pairs={{0,1},{1,0},{2,3},{3,2},{4,5},{5,4},{6,7},{7,6},{8,9},{9,8},{10,11... | collective-permute-start | bytes 1769480 | tf_op jit(solution)/shard_map/ppermute | solution.py:416
  102.7 17.2 %collective-permute-start.16 = (bf16[3,6,64,512]{3,2,1,0:T(8,128)(2,1)}, bf16[3,6,64,512]{3,2,1,0:T(8,128)(2,1)}, u32[]{:S(2)}, u32[]{:S(2)}) collective-permute-start(bf16[3,6,64,512]{3,2,1,0:T(8,128)(2,1)} %get-tuple-element.81.refs_18_.refs_10_), channel_id=1, source_target_pairs={{0,4},{1,3},{2,6},{3,1},{4,0},{5,7},{6,2},{7,5},{8,12},{9,11},{10,... | collective-permute-start | bytes 3538952 | tf_op jit(solution)/shard_map/ppermute | solution.py:413
  103.7 17.0 %collective-permute-start.17 = (bf16[3,6,64,512]{3,2,1,0:T(8,128)(2,1)}, bf16[3,6,64,512]{3,2,1,0:T(8,128)(2,1)}, u32[]{:S(2)}, u32[]{:S(2)}) collective-permute-start(bf16[3,6,64,512]{3,2,1,0:T(8,128)(2,1)} %get-tuple-element.76.refs_17_.refs_9_.refs_18_), channel_id=1, source_target_pairs={{0,1},{1,0},{2,3},{3,2},{4,5},{5,4},{6,7},{7,6},{8,9},{9,8},{10,11... | collective-permute-start | bytes 3538952 | tf_op jit(solution)/shard_map/ppermute | solution.py:416
  103.7 17.5 %collective-permute-start.18 = (bf16[3,6,64,512]{3,2,1,0:T(8,128)(2,1)}, bf16[3,6,64,512]{3,2,1,0:T(8,128)(2,1)}, u32[]{:S(2)}, u32[]{:S(2)}) collective-permute-start(bf16[3,6,64,512]{3,2,1,0:T(8,128)(2,1)} %get-tuple-element.81.refs_18_.refs_10_), channel_id=1, source_target_pairs={{0,1},{1,0},{2,3},{3,2},{4,5},{5,4},{6,7},{7,6},{8,9},{9,8},{10,11... | collective-permute-start | bytes 3538952 | tf_op jit(solution)/shard_map/ppermute | solution.py:416
  104.2 17.0 %collective-permute-start.19 = (bf16[3,6,64,512]{3,2,1,0:T(8,128)(2,1)}, bf16[3,6,64,512]{3,2,1,0:T(8,128)(2,1)}, u32[]{:S(2)}, u32[]{:S(2)}) collective-permute-start(bf16[3,6,64,512]{3,2,1,0:T(8,128)(2,1)} %get-tuple-element.83.refs_19_.refs_11_), channel_id=1, source_target_pairs={{0,1},{1,0},{2,3},{3,2},{4,5},{5,4},{6,7},{7,6},{8,9},{9,8},{10,11... | collective-permute-start | bytes 3538952 | tf_op jit(solution)/shard_map/ppermute | solution.py:416
  119.9 3.3 %collective-permute-start.20 = (bf16[3,6,64,512]{3,2,1,0:T(8,128)(2,1)}, bf16[3,6,64,512]{3,2,1,0:T(8,128)(2,1)}, u32[]{:S(2)}, u32[]{:S(2)}) collective-permute-start(bf16[3,6,64,512]{3,2,1,0:T(8,128)(2,1)} %get-tuple-element.84.refs_20_.refs_12_), channel_id=1, source_target_pairs={{0,1},{1,0},{2,3},{3,2},{4,5},{5,4},{6,7},{7,6},{8,9},{9,8},{10,11... | collective-permute-start | bytes 3538952 | tf_op jit(solution)/shard_map/ppermute | solution.py:416
  120.0 29.7 %collective-permute-start.21 = (bf16[3,6,64,512]{3,2,1,0:T(8,128)(2,1)}, bf16[3,6,64,512]{3,2,1,0:T(8,128)(2,1)}, u32[]{:S(2)}, u32[]{:S(2)}) collective-permute-start(bf16[3,6,64,512]{3,2,1,0:T(8,128)(2,1)} %get-tuple-element.85.refs_25_.refs_18_.refs_9_), channel_id=1, source_target_pairs={{0,2},{1,5},{2,0},{3,7},{4,6},{5,1},{6,4},{7,3},{8,10},{9,13},{10,... | collective-permute-start | bytes 3538952 | tf_op jit(solution)/shard_map/ppermute | solution.py:413
  120.7 29.0 %collective-permute-start.22 = (bf16[3,6,64,512]{3,2,1,0:T(8,128)(2,1)}, bf16[3,6,64,512]{3,2,1,0:T(8,128)(2,1)}, u32[]{:S(2)}, u32[]{:S(2)}) collective-permute-start(bf16[3,6,64,512]{3,2,1,0:T(8,128)(2,1)} %get-tuple-element.85.refs_25_.refs_18_.refs_9_), channel_id=1, source_target_pairs={{0,4},{1,3},{2,6},{3,1},{4,0},{5,7},{6,2},{7,5},{8,12},{9,11},{10,... | collective-permute-start | bytes 3538952 | tf_op jit(solution)/shard_map/ppermute | solution.py:413
  149.7 21.0 %collective-permute-start.23 = (bf16[3,6,64,512]{3,2,1,0:T(8,128)(2,1)}, bf16[3,6,64,512]{3,2,1,0:T(8,128)(2,1)}, u32[]{:S(2)}, u32[]{:S(2)}) collective-permute-start(bf16[3,6,64,512]{3,2,1,0:T(8,128)(2,1)} %get-tuple-element.91.refs_10_), channel_id=1, source_target_pairs={{0,4},{1,3},{2,6},{3,1},{4,0},{5,7},{6,2},{7,5},{8,12},{9,11},{10,... | collective-permute-start | bytes 3538952 | tf_op jit(solution)/shard_map/ppermute | solution.py:413
  150.3 21.0 %collective-permute-start.24 = (bf16[3,6,64,512]{3,2,1,0:T(8,128)(2,1)}, bf16[3,6,64,512]{3,2,1,0:T(8,128)(2,1)}, u32[]{:S(2)}, u32[]{:S(2)}) collective-permute-start(bf16[3,6,64,512]{3,2,1,0:T(8,128)(2,1)} %get-tuple-element.85.refs_25_.refs_18_.refs_9_), channel_id=1, source_target_pairs={{0,1},{1,0},{2,3},{3,2},{4,5},{5,4},{6,7},{7,6},{8,9},{9,8},{10,11... | collective-permute-start | bytes 3538952 | tf_op jit(solution)/shard_map/ppermute | solution.py:416
  150.3 20.9 %collective-permute-start.25 = (bf16[3,6,64,512]{3,2,1,0:T(8,128)(2,1)}, bf16[3,6,64,512]{3,2,1,0:T(8,128)(2,1)}, u32[]{:S(2)}, u32[]{:S(2)}) collective-permute-start(bf16[3,6,64,512]{3,2,1,0:T(8,128)(2,1)} %get-tuple-element.91.refs_10_), channel_id=1, source_target_pairs={{0,1},{1,0},{2,3},{3,2},{4,5},{5,4},{6,7},{7,6},{8,9},{9,8},{10,11... | collective-permute-start | bytes 3538952 | tf_op jit(solution)/shard_map/ppermute | solution.py:416
  150.8 20.5 %collective-permute-start.26 = (bf16[3,6,64,512]{3,2,1,0:T(8,128)(2,1)}, bf16[3,6,64,512]{3,2,1,0:T(8,128)(2,1)}, u32[]{:S(2)}, u32[]{:S(2)}) collective-permute-start(bf16[3,6,64,512]{3,2,1,0:T(8,128)(2,1)} %get-tuple-element.93.refs_11_), channel_id=1, source_target_pairs={{0,1},{1,0},{2,3},{3,2},{4,5},{5,4},{6,7},{7,6},{8,9},{9,8},{10,11... | collective-permute-start | bytes 3538952 | tf_op jit(solution)/shard_map/ppermute | solution.py:416
  170.7 3.3 %collective-permute-start.27 = (bf16[3,6,64,512]{3,2,1,0:T(8,128)(2,1)}, bf16[3,6,64,512]{3,2,1,0:T(8,128)(2,1)}, u32[]{:S(2)}, u32[]{:S(2)}) collective-permute-start(bf16[3,6,64,512]{3,2,1,0:T(8,128)(2,1)} %get-tuple-element.94.refs_12_), channel_id=1, source_target_pairs={{0,1},{1,0},{2,3},{3,2},{4,5},{5,4},{6,7},{7,6},{8,9},{9,8},{10,11... | collective-permute-start | bytes 3538952 | tf_op jit(solution)/shard_map/ppermute | solution.py:416

commit v2 on v1

--- a/solution.py
+++ b/solution.py
@@ -164,9 +164,10 @@
 
 
 def density_kernel(
-    n_occ, n_blocks, cuts, jobs, held, last, me, sizes, order, eps_occ, va, vb, *refs
+    n_occ, n_blocks, cuts, jobs, held, last, *refs
 ):
     refs = list(refs)
+    small = [refs.pop(0) for _ in range(6)]
     refs.pop(0)
     n_parts = sum(cuts)
     first_blocks = [refs.pop(0) for _ in range(n_blocks)]
@@ -175,7 +176,7 @@
     own = {c: col_blocks[c][0] if c in chunks else refs.pop(0) for c in row_chunks}
     before = refs.pop(0) if any(held) else None
     refs.pop(0)
-    out, rows, cols, kbuf, abuf, total, result, sems = refs
+    out, me, sizes, order, eps_occ, va, vb, rows, cols, kbuf, abuf, total, result, sems = refs
     width, aux = rows.shape[2], rows.shape[3]
     part = width // n_parts
     n_copies = 0
@@ -186,6 +187,8 @@
         made.start()
         n_copies += 1
         return made
+
+    small_copies = [copy(a, b) for a, b in zip(small, (me, sizes, order, eps_occ, va, vb))]
 
     def load_rows(c):
         place = pl.ds(sum(cuts[:c]) * part, cuts[c] * part)
@@ -229,6 +232,8 @@
     for unit in units[1:]:
         col_copies[unit, 0] = load_cols(unit, 0, CAP)
     total_copies = []
+    for made in small_copies:
+        made.wait()
     energy = []
     for orbital, live in group_slots(sizes, order, me[0], n_occ):
         energy.append(jnp.where(live, eps_occ[orbital], jnp.float32(0.0)))
@@ -374,9 +379,11 @@
             jax.ShapeDtypeStruct(token.shape, token.dtype),
             jax.ShapeDtypeStruct((CAP, width, naux), kept),
         ],
-        in_specs=[SMEM] * 4 + [VMEM] * 2 + [ANY] * (len(operands) - at),
+        in_specs=[ANY] * len(operands),
         out_specs=[ANY] * 2,
         scratch_shapes=[
+            *[pltpu.SMEM(x.shape, x.dtype) for x in scalars[:4]],
+            *[pltpu.VMEM(x.shape, x.dtype) for x in scalars[4:]],
             pltpu.VMEM((n_occ, CAP, width, aux), jnp.bfloat16),
             pltpu.VMEM((len(units), n_occ, CAP, LANES, aux), jnp.bfloat16),
             pltpu.VMEM((CAP, tallest, LANES), jnp.float32),

time: 210 us -> 207 us (0.986)
  Pallas kernels: 110 us -> 106 us
    pallas_call x4, Pallas kernels: 92.3 us -> 89 us  [density(): pl.pallas_call(functools.partial(density_kernel, n_occ, n_blocks, cuts, j...]
  transfers between devices with their start and end apart: 31 -> 31, of which waited for: 10 -> 10; matrix products, arithmetic and copies ran while one was open for 1% -> 1% of each run, Pallas kernels for 36% -> 35%
where the time goes in v2:
time: 207 us; the launch traced here: 204 us
  Pallas kernels  106 us (51%)
  waiting for transfers between devices  61.2 us (30%)
  starting transfers between devices  32.6 us (16%)
  local copies, waits for them, and re-layouts  2.9 us (1%)
    pallas_call x4, Pallas kernels, density(): pl.pallas_call(functools.partial(density_kernel, n_occ, n_blocks, cuts, j...  89 us
    all_to_all x3, waiting for transfers between devices, cross(): crossing.append([lax.all_to_all(gated[0], 'occ', 0, 0, tiled=True)])  27.5 us
    ppermute x12, waiting for transfers between devices, hop(): return lax.ppermute(block, 'virt', pairs)  24.9 us
    all_to_all x3, starting transfers between devices, cross(): crossing.append([lax.all_to_all(gated[0], 'occ', 0, 0, tiled=True)])  15.3 us
    ppermute x12, starting transfers between devices, hop(): return lax.ppermute(block, 'virt', pairs)  14 us
    pallas_call x3, Pallas kernels, stage(): pl.pallas_call(functools.partial(stage_kernel, n_occ, low, high, with_own...  10.7 us
    ppermute x16, waiting for transfers between devices, sibling(): return lax.ppermute(block, 'virt', [(d, d ^ 1) for d in range(n_virt)])  8.77 us
    pallas_call x3, Pallas kernels, join(): pl.pallas_call(functools.partial(join_kernel, n_occ, len(got), parts), ou...  6.62 us
  transfers between devices with their start and end apart: 31, of which 10 were waited for; matrix products, arithmetic and copies ran while one was open for 1% of the time, Pallas kernels for 35%

profile of v2, /device:TPU:0, one launch (start us, length us, event | category | flops | bytes accessed | tf_op | source)
XLA Modules:
  0.0 203.6 jit_solution(16952136358312681097)
XLA Ops:
  0.0 4.1 %shard_map.55 = (f32[8,128]{1,0:T(8,128)}, bf16[4,6,32,512]{3,2,1,0:T(8,128)(2,1)}, bf16[6,160,512]{2,1,0:T(8,128)(2,1)}) custom-call(s32[1]{0:T(128)} %bitcast.me.refs_0_, s32[4]{0:T(128)} %refs_1_.7, s32[16]{0:T(128)} %refs_2_.7, bf16[16,160,512]{2,1,0:T(8,128)(2,1)} %basis.5), custom_call_target="tpu_custom_call" | custom-call | flops 1024 | bytes 1024 | tf_op jit(solution)/shard_map/pallas_call | solution.py:80
  4.1 6.4 %all-to-all-start = ((bf16[4,6,32,512]{3,2,1,0:T(8,128)(2,1)}), bf16[4,6,32,512]{3,2,1,0:T(8,128)(2,1)}, u32[]{:S(2)}, u32[]{:S(2)}) async-start(bf16[4,6,32,512]{3,2,1,0:T(8,128)(2,1)} %get-tuple-element.60), calls=%async_computation | async-start | bytes 1572864 | tf_op jit(solution)/shard_map/all_to_all | solution.py:475
  10.5 1.5 collective-permute-start
  11.9 1.5 collective-permute-start.1
  13.5 3.4 %shard_map.57 = (f32[8,128]{1,0:T(8,128)}, bf16[4,6,64,512]{3,2,1,0:T(8,128)(2,1)}) custom-call(s32[1]{0:T(128)} %bitcast.me.refs_0_, s32[4]{0:T(128)} %refs_1_.7, s32[16]{0:T(128)} %refs_2_.7, bf16[16,160,512]{2,1,0:T(8,128)(2,1)} %basis.5, f32[8,128]{1,0:T(8,128)} %get-tuple-element.53.refs_0_), custom_call_target="tpu_custom_call", output_to_operand_aliasing={{0}: (4, {})} | custom-call | flops 1024 | bytes 1024 | tf_op jit(solution)/shard_map/pallas_call | solution.py:80
  16.9 3.3 %shard_map.58 = (f32[8,128]{1,0:T(8,128)}, bf16[4,6,64,512]{3,2,1,0:T(8,128)(2,1)}) custom-call(s32[1]{0:T(128)} %bitcast.me.refs_0_, s32[4]{0:T(128)} %refs_1_.7, s32[16]{0:T(128)} %refs_2_.7, bf16[16,160,512]{2,1,0:T(8,128)(2,1)} %basis.5, f32[8,128]{1,0:T(8,128)} %get-tuple-element.54.refs_0_), custom_call_target="tpu_custom_call", output_to_operand_aliasing={{0}: (4, {})} | custom-call | flops 1024 | bytes 1024 | tf_op jit(solution)/shard_map/pallas_call | solution.py:80
  20.1 10.5 %all-to-all-done.refs_0_ = bf16[4,6,32,512]{3,2,1,0:T(8,128)(2,1)} async-done(((bf16[4,6,32,512]{3,2,1,0:T(8,128)(2,1)}), bf16[4,6,32,512]{3,2,1,0:T(8,128)(2,1)}, u32[]{:S(2)}, u32[]{:S(2)}) %all-to-all-start) | async-done | bytes 786464 | tf_op jit(solution)/shard_map/all_to_all | solution.py:475
  30.7 4.4 %all-to-all-start.1 = ((bf16[4,6,64,512]{3,2,1,0:T(8,128)(2,1)}), bf16[4,6,64,512]{3,2,1,0:T(8,128)(2,1)}, u32[]{:S(2)}, u32[]{:S(2)}) async-start(bf16[4,6,64,512]{3,2,1,0:T(8,128)(2,1)} %get-tuple-element.68), calls=%async_computation.1 | async-start | bytes 3145728 | tf_op jit(solution)/shard_map/all_to_all | solution.py:475
  35.0 0.0 copy-start
  35.1 0.7 copy-done
  35.7 0.1 reshape.330
  35.8 0.1 stack.35
  35.9 0.6 gather_fusion
  36.5 0.7 reshape.331.refs_2_.refs_5_
  37.2 0.1 dynamic_slice.3
  37.2 0.8 copy.47.refs_1_.refs_4_
  38.0 2.0 shard_map.62
  40.0 0.0 collective-permute-done.refs_1_
  40.0 1.6 collective-permute-start.2
  41.6 1.5 collective-permute-start.3
  43.1 0.5 collective-permute-start.4
  43.6 0.0 collective-permute-start.6
  43.6 0.5 collective-permute-start.7
  44.1 16.0 %collective-permute-done.2.refs_1_ = bf16[6,160,512]{2,1,0:T(8,128)(2,1)} collective-permute-done((bf16[6,160,512]{2,1,0:T(8,128)(2,1)}, bf16[6,160,512]{2,1,0:T(8,128)(2,1)}, u32[]{:S(2)}, u32[]{:S(2)}) %collective-permute-start.2) | collective-permute-done | bytes 983072 | tf_op jit(solution)/shard_map/ppermute | solution.py:420
  60.1 0.0 collective-permute-start.10
  60.1 0.5 collective-permute-start.8
  60.6 5.8 %collective-permute-done.4.refs_2_ = bf16[3,6,32,512]{3,2,1,0:T(8,128)(2,1)} collective-permute-done((bf16[3,6,32,512]{3,2,1,0:T(8,128)(2,1)}, bf16[3,6,32,512]{3,2,1,0:T(8,128)(2,1)}, u32[]{:S(2)}, u32[]{:S(2)}) %collective-permute-start.4) | collective-permute-done | bytes 589856 | tf_op jit(solution)/shard_map/ppermute | solution.py:420
  66.4 1.5 collective-permute-start.5
  68.0 3.6 %all-to-all-done.1.refs_0_ = bf16[4,6,64,512]{3,2,1,0:T(8,128)(2,1)} async-done(((bf16[4,6,64,512]{3,2,1,0:T(8,128)(2,1)}), bf16[4,6,64,512]{3,2,1,0:T(8,128)(2,1)}, u32[]{:S(2)}, u32[]{:S(2)}) %all-to-all-start.1) | async-done | bytes 1572896 | tf_op jit(solution)/shard_map/all_to_all | solution.py:475
  71.6 2.3 %shard_map.66 = (f32[8,128]{1,0:T(8,128)}, bf16[3,6,64,512]{3,2,1,0:T(8,128)(2,1)}) custom-call(s32[1]{0:T(128)} %bitcast.me.refs_0_, f32[8,128]{1,0:T(8,128)} %get-tuple-element.67.token_in, bf16[4,6,64,512]{3,2,1,0:T(8,128)(2,1)} %all-to-all-done.1.refs_0_), custom_call_target="tpu_custom_call", output_to_operand_aliasing={{0}: (1, {})} | custom-call | flops 1024 | bytes 1024 | tf_op jit(solution)/shard_map/pallas_call | solution.py:139
  73.9 1.6 collective-permute-start.14
  75.4 0.0 collective-permute-done.7.refs_12_
  75.4 1.5 collective-permute-start.15
  77.0 4.5 %all-to-all-start.2 = ((bf16[4,6,64,512]{3,2,1,0:T(8,128)(2,1)}), bf16[4,6,64,512]{3,2,1,0:T(8,128)(2,1)}, u32[]{:S(2)}, u32[]{:S(2)}) async-start(bf16[4,6,64,512]{3,2,1,0:T(8,128)(2,1)} %get-tuple-element.79), calls=%async_computation.2 | async-start | bytes 3145728 | tf_op jit(solution)/shard_map/all_to_all | solution.py:475
  81.5 0.1 collective-permute-start.9
  81.6 0.5 collective-permute-start.12
  82.1 0.1 collective-permute-start.13
  82.2 3.1 %collective-permute-done.12.refs_21_ = bf16[3,6,32,512]{3,2,1,0:T(8,128)(2,1)} collective-permute-done((bf16[3,6,32,512]{3,2,1,0:T(8,128)(2,1)}, bf16[3,6,32,512]{3,2,1,0:T(8,128)(2,1)}, u32[]{:S(2)}, u32[]{:S(2)}) %collective-permute-start.12) | collective-permute-done | bytes 589856 | tf_op jit(solution)/shard_map/ppermute | solution.py:423
  85.4 0.0 collective-permute-done.9.refs_14_
  85.4 0.8 collective-permute-done.13.refs_22_
  86.2 13.2 %shard_map.68 = (f32[8,128]{1,0:T(8,128)}, f32[6,160,2048]{2,1,0:T(8,128)}) custom-call(s32[1]{0:T(128)} %bitcast.me.refs_0_, s32[4]{0:T(128)} %refs_1_.7, s32[16]{0:T(128)} %refs_2_.7, f32[16]{0:T(128)} %refs_3_.7, f32[160,1]{1,0:T(8,128)} %copy.47.refs_1_.refs_4_, f32[5,1,256]{2,1,0:T(1,128)} %reshape.331.refs_2_.refs_5_, ...), custom_call_target="tpu_custom_call", output_to_operand_aliasing={{0}: (6, {})} | custom-call | flops 1024 | bytes 1024 | tf_op jit(solution)/shard_map/pallas_call | solution.py:376
  99.4 3.1 %collective-permute-done.14.refs_1_ = bf16[3,6,64,512]{3,2,1,0:T(8,128)(2,1)} collective-permute-done((bf16[3,6,64,512]{3,2,1,0:T(8,128)(2,1)}, bf16[3,6,64,512]{3,2,1,0:T(8,128)(2,1)}, u32[]{:S(2)}, u32[]{:S(2)}) %collective-permute-start.14) | collective-permute-done | bytes 1179680 | tf_op jit(solution)/shard_map/ppermute | solution.py:420
  102.4 1.0 collective-permute-start.16
  103.4 0.0 collective-permute-start.17
  103.4 0.5 collective-permute-start.18
  104.0 13.4 %all-to-all-done.2.refs_0_ = bf16[4,6,64,512]{3,2,1,0:T(8,128)(2,1)} async-done(((bf16[4,6,64,512]{3,2,1,0:T(8,128)(2,1)}), bf16[4,6,64,512]{3,2,1,0:T(8,128)(2,1)}, u32[]{:S(2)}, u32[]{:S(2)}) %all-to-all-start.2) | async-done | bytes 1572896 | tf_op jit(solution)/shard_map/all_to_all | solution.py:475
  117.3 2.3 %shard_map.70 = (f32[8,128]{1,0:T(8,128)}, bf16[3,6,64,512]{3,2,1,0:T(8,128)(2,1)}) custom-call(s32[1]{0:T(128)} %bitcast.me.refs_0_, f32[8,128]{1,0:T(8,128)} %get-tuple-element.78.token_in, bf16[4,6,64,512]{3,2,1,0:T(8,128)(2,1)} %all-to-all-done.2.refs_0_), custom_call_target="tpu_custom_call", output_to_operand_aliasing={{0}: (1, {})} | custom-call | flops 1024 | bytes 1024 | tf_op jit(solution)/shard_map/pallas_call | solution.py:139
  119.7 0.1 collective-permute-start.20
  119.8 0.7 collective-permute-start.21
  120.5 0.0 collective-permute-done.17.refs_27_.refs_19_
  120.5 0.5 collective-permute-start.22
  121.0 2.0 collective-permute-done.20.refs_30_.refs_22_
  122.9 25.7 %shard_map.72 = (f32[8,128]{1,0:T(8,128)}, f32[6,160,2048]{2,1,0:T(8,128)}) custom-call(s32[1]{0:T(128)} %bitcast.me.refs_0_, s32[4]{0:T(128)} %refs_1_.7, s32[16]{0:T(128)} %refs_2_.7, f32[16]{0:T(128)} %refs_3_.7, f32[160,1]{1,0:T(8,128)} %copy.47.refs_1_.refs_4_, f32[5,1,256]{2,1,0:T(1,128)} %reshape.331.refs_2_.refs_5_, ...), custom_call_target="tpu_custom_call", output_to_operand_aliasing={{0}: (6, {})} | custom-call | flops 1024 | bytes 1024 | tf_op jit(solution)/shard_map/pallas_call | solution.py:376
  148.6 0.0 collective-permute-done.21.refs_1_
  148.7 0.0 collective-permute-done.22.refs_2_
  148.7 0.6 collective-permute-start.23
  149.3 0.0 collective-permute-start.24
  149.3 0.5 collective-permute-start.25
  149.8 0.0 collective-permute-start.26
  149.8 19.0 %shard_map.74 = (f32[8,128]{1,0:T(8,128)}, f32[6,160,2048]{2,1,0:T(8,128)}) custom-call(s32[1]{0:T(128)} %bitcast.me.refs_0_, s32[4]{0:T(128)} %refs_1_.7, s32[16]{0:T(128)} %refs_2_.7, f32[16]{0:T(128)} %refs_3_.7, f32[160,1]{1,0:T(8,128)} %copy.47.refs_1_.refs_4_, f32[5,1,256]{2,1,0:T(1,128)} %reshape.331.refs_2_.refs_5_, ...), custom_call_target="tpu_custom_call", output_to_operand_aliasing={{0}: (6, {})} | custom-call | flops 1024 | bytes 1024 | tf_op jit(solution)/shard_map/pallas_call | solution.py:376
  168.8 0.0 collective-permute-done.23.refs_1_
  168.9 0.6 collective-permute-start.27
  169.4 2.8 %collective-permute-done.27.refs_22_ = bf16[3,6,64,512]{3,2,1,0:T(8,128)(2,1)} collective-permute-done((bf16[3,6,64,512]{3,2,1,0:T(8,128)(2,1)}, bf16[3,6,64,512]{3,2,1,0:T(8,128)(2,1)}, u32[]{:S(2)}, u32[]{:S(2)}) %collective-permute-start.27) | collective-permute-done | bytes 1179680 | tf_op jit(solution)/shard_map/ppermute | solution.py:423
  172.2 31.2 %shard_map.76 = (f32[8,128]{1,0:T(8,128)}, bf16[6,160,2048]{2,1,0:T(8,128)(2,1)}) custom-call(s32[1]{0:T(128)} %bitcast.me.refs_0_, s32[4]{0:T(128)} %refs_1_.7, s32[16]{0:T(128)} %refs_2_.7, f32[16]{0:T(128)} %refs_3_.7, f32[160,1]{1,0:T(8,128)} %copy.47.refs_1_.refs_4_, f32[5,1,256]{2,1,0:T(1,128)} %reshape.331.refs_2_.refs_5_, ...), custom_call_target="tpu_custom_call", output_to_operand_aliasing={{0}: (6, {})} | custom-call | flops 1024 | bytes 1024 | tf_op jit(solution)/shard_map/pallas_call | solution.py:376
  (31 shorter events, 0.1 us)
Async XLA Ops:
  4.1 26.6 %all-to-all-start = ((bf16[4,6,32,512]{3,2,1,0:T(8,128)(2,1)}), bf16[4,6,32,512]{3,2,1,0:T(8,128)(2,1)}, u32[]{:S(2)}, u32[]{:S(2)}) async-start(bf16[4,6,32,512]{3,2,1,0:T(8,128)(2,1)} %get-tuple-element.60), calls=%async_computation | async-start | bytes 1572864 | tf_op jit(solution)/shard_map/all_to_all | solution.py:475
  10.5 29.5 %collective-permute-start = (bf16[6,160,512]{2,1,0:T(8,128)(2,1)}, bf16[6,160,512]{2,1,0:T(8,128)(2,1)}, u32[]{:S(2)}, u32[]{:S(2)}) collective-permute-start(bf16[6,160,512]{2,1,0:T(8,128)(2,1)} %get-tuple-element.62.refs_7_), channel_id=1, source_target_pairs={{0,2},{1,5},{2,0},{3,7},{4,6},{5,1},{6,4},{7,3},{8,10},{9,13},{10,... | collective-permute-start | bytes 2949128 | tf_op jit(solution)/shard_map/ppermute | solution.py:420
  11.9 28.1 %collective-permute-start.1 = (bf16[6,160,512]{2,1,0:T(8,128)(2,1)}, bf16[6,160,512]{2,1,0:T(8,128)(2,1)}, u32[]{:S(2)}, u32[]{:S(2)}) collective-permute-start(bf16[6,160,512]{2,1,0:T(8,128)(2,1)} %get-tuple-element.62.refs_7_), channel_id=1, source_target_pairs={{0,4},{1,3},{2,6},{3,1},{4,0},{5,7},{6,2},{7,5},{8,12},{9,11},{10,... | collective-permute-start | bytes 2949128 | tf_op jit(solution)/shard_map/ppermute | solution.py:420
  30.7 40.9 %all-to-all-start.1 = ((bf16[4,6,64,512]{3,2,1,0:T(8,128)(2,1)}), bf16[4,6,64,512]{3,2,1,0:T(8,128)(2,1)}, u32[]{:S(2)}, u32[]{:S(2)}) async-start(bf16[4,6,64,512]{3,2,1,0:T(8,128)(2,1)} %get-tuple-element.68), calls=%async_computation.1 | async-start | bytes 3145728 | tf_op jit(solution)/shard_map/all_to_all | solution.py:475
  35.0 0.7 copy-start
  40.0 20.1 %collective-permute-start.2 = (bf16[6,160,512]{2,1,0:T(8,128)(2,1)}, bf16[6,160,512]{2,1,0:T(8,128)(2,1)}, u32[]{:S(2)}, u32[]{:S(2)}) collective-permute-start(bf16[6,160,512]{2,1,0:T(8,128)(2,1)} %get-tuple-element.64.refs_8_), channel_id=1, source_target_pairs={{0,4},{1,3},{2,6},{3,1},{4,0},{5,7},{6,2},{7,5},{8,12},{9,11},{10,... | collective-permute-start | bytes 2949128 | tf_op jit(solution)/shard_map/ppermute | solution.py:420
  41.6 18.5 %collective-permute-start.3 = (bf16[3,6,32,512]{3,2,1,0:T(8,128)(2,1)}, bf16[3,6,32,512]{3,2,1,0:T(8,128)(2,1)}, u32[]{:S(2)}, u32[]{:S(2)}) collective-permute-start(bf16[3,6,32,512]{3,2,1,0:T(8,128)(2,1)} %get-tuple-element.66.refs_15_.refs_23_), channel_id=1, source_target_pairs={{0,2},{1,5},{2,0},{3,7},{4,6},{5,1},{6,4},{7,3},{8,10},{9,13},{10,... | collective-permute-start | bytes 1769480 | tf_op jit(solution)/shard_map/ppermute | solution.py:420
  43.1 23.3 %collective-permute-start.4 = (bf16[3,6,32,512]{3,2,1,0:T(8,128)(2,1)}, bf16[3,6,32,512]{3,2,1,0:T(8,128)(2,1)}, u32[]{:S(2)}, u32[]{:S(2)}) collective-permute-start(bf16[3,6,32,512]{3,2,1,0:T(8,128)(2,1)} %get-tuple-element.66.refs_15_.refs_23_), channel_id=1, source_target_pairs={{0,4},{1,3},{2,6},{3,1},{4,0},{5,7},{6,2},{7,5},{8,12},{9,11},{10,... | collective-permute-start | bytes 1769480 | tf_op jit(solution)/shard_map/ppermute | solution.py:420
  43.6 24.4 %collective-permute-start.6 = (bf16[6,160,512]{2,1,0:T(8,128)(2,1)}, bf16[6,160,512]{2,1,0:T(8,128)(2,1)}, u32[]{:S(2)}, u32[]{:S(2)}) collective-permute-start(bf16[6,160,512]{2,1,0:T(8,128)(2,1)} %get-tuple-element.62.refs_7_), channel_id=1, source_target_pairs={{0,1},{1,0},{2,3},{3,2},{4,5},{5,4},{6,7},{7,6},{8,9},{9,8},{10,11... | collective-permute-start | bytes 2949128 | tf_op jit(solution)/shard_map/ppermute | solution.py:423
  43.6 31.8 %collective-permute-start.7 = (bf16[6,160,512]{2,1,0:T(8,128)(2,1)}, bf16[6,160,512]{2,1,0:T(8,128)(2,1)}, u32[]{:S(2)}, u32[]{:S(2)}) collective-permute-start(bf16[6,160,512]{2,1,0:T(8,128)(2,1)} %get-tuple-element.64.refs_8_), channel_id=1, source_target_pairs={{0,1},{1,0},{2,3},{3,2},{4,5},{5,4},{6,7},{7,6},{8,9},{9,8},{10,11... | collective-permute-start | bytes 2949128 | tf_op jit(solution)/shard_map/ppermute | solution.py:423
  60.1 13.8 %collective-permute-start.10 = (bf16[3,6,32,512]{3,2,1,0:T(8,128)(2,1)}, bf16[3,6,32,512]{3,2,1,0:T(8,128)(2,1)}, u32[]{:S(2)}, u32[]{:S(2)}) collective-permute-start(bf16[3,6,32,512]{3,2,1,0:T(8,128)(2,1)} %get-tuple-element.66.refs_15_.refs_23_), channel_id=1, source_target_pairs={{0,1},{1,0},{2,3},{3,2},{4,5},{5,4},{6,7},{7,6},{8,9},{9,8},{10,11... | collective-permute-start | bytes 1769480 | tf_op jit(solution)/shard_map/ppermute | solution.py:423
  60.1 21.5 %collective-permute-start.8 = (bf16[6,160,512]{2,1,0:T(8,128)(2,1)}, bf16[6,160,512]{2,1,0:T(8,128)(2,1)}, u32[]{:S(2)}, u32[]{:S(2)}) collective-permute-start(bf16[6,160,512]{2,1,0:T(8,128)(2,1)} %get-tuple-element.72.refs_9_), channel_id=1, source_target_pairs={{0,1},{1,0},{2,3},{3,2},{4,5},{5,4},{6,7},{7,6},{8,9},{9,8},{10,11... | collective-permute-start | bytes 2949128 | tf_op jit(solution)/shard_map/ppermute | solution.py:423
  66.4 15.1 %collective-permute-start.5 = (bf16[3,6,32,512]{3,2,1,0:T(8,128)(2,1)}, bf16[3,6,32,512]{3,2,1,0:T(8,128)(2,1)}, u32[]{:S(2)}, u32[]{:S(2)}) collective-permute-start(bf16[3,6,32,512]{3,2,1,0:T(8,128)(2,1)} %get-tuple-element.70.refs_16_), channel_id=1, source_target_pairs={{0,4},{1,3},{2,6},{3,1},{4,0},{5,7},{6,2},{7,5},{8,12},{9,11},{10,... | collective-permute-start | bytes 1769480 | tf_op jit(solution)/shard_map/ppermute | solution.py:420
  68.0 14.2 %collective-permute-start.11 = (bf16[3,6,32,512]{3,2,1,0:T(8,128)(2,1)}, bf16[3,6,32,512]{3,2,1,0:T(8,128)(2,1)}, u32[]{:S(2)}, u32[]{:S(2)}) collective-permute-start(bf16[3,6,32,512]{3,2,1,0:T(8,128)(2,1)} %get-tuple-element.70.refs_16_), channel_id=1, source_target_pairs={{0,1},{1,0},{2,3},{3,2},{4,5},{5,4},{6,7},{7,6},{8,9},{9,8},{10,11... | collective-permute-start | bytes 1769480 | tf_op jit(solution)/shard_map/ppermute | solution.py:423
  73.9 28.5 %collective-permute-start.14 = (bf16[3,6,64,512]{3,2,1,0:T(8,128)(2,1)}, bf16[3,6,64,512]{3,2,1,0:T(8,128)(2,1)}, u32[]{:S(2)}, u32[]{:S(2)}) collective-permute-start(bf16[3,6,64,512]{3,2,1,0:T(8,128)(2,1)} %get-tuple-element.76.refs_23_.refs_15_.refs_24_), channel_id=1, source_target_pairs={{0,2},{1,5},{2,0},{3,7},{4,6},{5,1},{6,4},{7,3},{8,10},{9,13},{10,... | collective-permute-start | bytes 3538952 | tf_op jit(solution)/shard_map/ppermute | solution.py:420
  75.4 27.0 %collective-permute-start.15 = (bf16[3,6,64,512]{3,2,1,0:T(8,128)(2,1)}, bf16[3,6,64,512]{3,2,1,0:T(8,128)(2,1)}, u32[]{:S(2)}, u32[]{:S(2)}) collective-permute-start(bf16[3,6,64,512]{3,2,1,0:T(8,128)(2,1)} %get-tuple-element.76.refs_23_.refs_15_.refs_24_), channel_id=1, source_target_pairs={{0,4},{1,3},{2,6},{3,1},{4,0},{5,7},{6,2},{7,5},{8,12},{9,11},{10,... | collective-permute-start | bytes 3538952 | tf_op jit(solution)/shard_map/ppermute | solution.py:420
  77.0 40.3 %all-to-all-start.2 = ((bf16[4,6,64,512]{3,2,1,0:T(8,128)(2,1)}), bf16[4,6,64,512]{3,2,1,0:T(8,128)(2,1)}, u32[]{:S(2)}, u32[]{:S(2)}) async-start(bf16[4,6,64,512]{3,2,1,0:T(8,128)(2,1)} %get-tuple-element.79), calls=%async_computation.2 | async-start | bytes 3145728 | tf_op jit(solution)/shard_map/all_to_all | solution.py:475
  81.5 3.8 %collective-permute-start.9 = (bf16[6,160,512]{2,1,0:T(8,128)(2,1)}, bf16[6,160,512]{2,1,0:T(8,128)(2,1)}, u32[]{:S(2)}, u32[]{:S(2)}) collective-permute-start(bf16[6,160,512]{2,1,0:T(8,128)(2,1)} %get-tuple-element.73.refs_10_), channel_id=1, source_target_pairs={{0,1},{1,0},{2,3},{3,2},{4,5},{5,4},{6,7},{7,6},{8,9},{9,8},{10,11... | collective-permute-start | bytes 2949128 | tf_op jit(solution)/shard_map/ppermute | solution.py:423
  81.6 3.7 %collective-permute-start.12 = (bf16[3,6,32,512]{3,2,1,0:T(8,128)(2,1)}, bf16[3,6,32,512]{3,2,1,0:T(8,128)(2,1)}, u32[]{:S(2)}, u32[]{:S(2)}) collective-permute-start(bf16[3,6,32,512]{3,2,1,0:T(8,128)(2,1)} %get-tuple-element.74.refs_17_), channel_id=1, source_target_pairs={{0,1},{1,0},{2,3},{3,2},{4,5},{5,4},{6,7},{7,6},{8,9},{9,8},{10,11... | collective-permute-start | bytes 1769480 | tf_op jit(solution)/shard_map/ppermute | solution.py:423
  82.1 4.1 %collective-permute-start.13 = (bf16[3,6,32,512]{3,2,1,0:T(8,128)(2,1)}, bf16[3,6,32,512]{3,2,1,0:T(8,128)(2,1)}, u32[]{:S(2)}, u32[]{:S(2)}) collective-permute-start(bf16[3,6,32,512]{3,2,1,0:T(8,128)(2,1)} %get-tuple-element.75.refs_18_), channel_id=1, source_target_pairs={{0,1},{1,0},{2,3},{3,2},{4,5},{5,4},{6,7},{7,6},{8,9},{9,8},{10,11... | collective-permute-start | bytes 1769480 | tf_op jit(solution)/shard_map/ppermute | solution.py:423
  102.4 17.2 %collective-permute-start.16 = (bf16[3,6,64,512]{3,2,1,0:T(8,128)(2,1)}, bf16[3,6,64,512]{3,2,1,0:T(8,128)(2,1)}, u32[]{:S(2)}, u32[]{:S(2)}) collective-permute-start(bf16[3,6,64,512]{3,2,1,0:T(8,128)(2,1)} %get-tuple-element.81.refs_24_.refs_16_), channel_id=1, source_target_pairs={{0,4},{1,3},{2,6},{3,1},{4,0},{5,7},{6,2},{7,5},{8,12},{9,11},{10,... | collective-permute-start | bytes 3538952 | tf_op jit(solution)/shard_map/ppermute | solution.py:420
  103.4 17.0 %collective-permute-start.17 = (bf16[3,6,64,512]{3,2,1,0:T(8,128)(2,1)}, bf16[3,6,64,512]{3,2,1,0:T(8,128)(2,1)}, u32[]{:S(2)}, u32[]{:S(2)}) collective-permute-start(bf16[3,6,64,512]{3,2,1,0:T(8,128)(2,1)} %get-tuple-element.76.refs_23_.refs_15_.refs_24_), channel_id=1, source_target_pairs={{0,1},{1,0},{2,3},{3,2},{4,5},{5,4},{6,7},{7,6},{8,9},{9,8},{10,11... | collective-permute-start | bytes 3538952 | tf_op jit(solution)/shard_map/ppermute | solution.py:423
  103.4 17.5 %collective-permute-start.18 = (bf16[3,6,64,512]{3,2,1,0:T(8,128)(2,1)}, bf16[3,6,64,512]{3,2,1,0:T(8,128)(2,1)}, u32[]{:S(2)}, u32[]{:S(2)}) collective-permute-start(bf16[3,6,64,512]{3,2,1,0:T(8,128)(2,1)} %get-tuple-element.81.refs_24_.refs_16_), channel_id=1, source_target_pairs={{0,1},{1,0},{2,3},{3,2},{4,5},{5,4},{6,7},{7,6},{8,9},{9,8},{10,11... | collective-permute-start | bytes 3538952 | tf_op jit(solution)/shard_map/ppermute | solution.py:423
  104.0 17.0 %collective-permute-start.19 = (bf16[3,6,64,512]{3,2,1,0:T(8,128)(2,1)}, bf16[3,6,64,512]{3,2,1,0:T(8,128)(2,1)}, u32[]{:S(2)}, u32[]{:S(2)}) collective-permute-start(bf16[3,6,64,512]{3,2,1,0:T(8,128)(2,1)} %get-tuple-element.83.refs_25_.refs_17_), channel_id=1, source_target_pairs={{0,1},{1,0},{2,3},{3,2},{4,5},{5,4},{6,7},{7,6},{8,9},{9,8},{10,11... | collective-permute-start | bytes 3538952 | tf_op jit(solution)/shard_map/ppermute | solution.py:423
  119.7 3.3 %collective-permute-start.20 = (bf16[3,6,64,512]{3,2,1,0:T(8,128)(2,1)}, bf16[3,6,64,512]{3,2,1,0:T(8,128)(2,1)}, u32[]{:S(2)}, u32[]{:S(2)}) collective-permute-start(bf16[3,6,64,512]{3,2,1,0:T(8,128)(2,1)} %get-tuple-element.84.refs_26_.refs_18_), channel_id=1, source_target_pairs={{0,1},{1,0},{2,3},{3,2},{4,5},{5,4},{6,7},{7,6},{8,9},{9,8},{10,11... | collective-permute-start | bytes 3538952 | tf_op jit(solution)/shard_map/ppermute | solution.py:423
  119.8 28.9 %collective-permute-start.21 = (bf16[3,6,64,512]{3,2,1,0:T(8,128)(2,1)}, bf16[3,6,64,512]{3,2,1,0:T(8,128)(2,1)}, u32[]{:S(2)}, u32[]{:S(2)}) collective-permute-start(bf16[3,6,64,512]{3,2,1,0:T(8,128)(2,1)} %get-tuple-element.85.refs_31_.refs_24_.refs_15_), channel_id=1, source_target_pairs={{0,2},{1,5},{2,0},{3,7},{4,6},{5,1},{6,4},{7,3},{8,10},{9,13},{10,... | collective-permute-start | bytes 3538952 | tf_op jit(solution)/shard_map/ppermute | solution.py:420
  120.5 28.2 %collective-permute-start.22 = (bf16[3,6,64,512]{3,2,1,0:T(8,128)(2,1)}, bf16[3,6,64,512]{3,2,1,0:T(8,128)(2,1)}, u32[]{:S(2)}, u32[]{:S(2)}) collective-permute-start(bf16[3,6,64,512]{3,2,1,0:T(8,128)(2,1)} %get-tuple-element.85.refs_31_.refs_24_.refs_15_), channel_id=1, source_target_pairs={{0,4},{1,3},{2,6},{3,1},{4,0},{5,7},{6,2},{7,5},{8,12},{9,11},{10,... | collective-permute-start | bytes 3538952 | tf_op jit(solution)/shard_map/ppermute | solution.py:420
  148.7 20.2 %collective-permute-start.23 = (bf16[3,6,64,512]{3,2,1,0:T(8,128)(2,1)}, bf16[3,6,64,512]{3,2,1,0:T(8,128)(2,1)}, u32[]{:S(2)}, u32[]{:S(2)}) collective-permute-start(bf16[3,6,64,512]{3,2,1,0:T(8,128)(2,1)} %get-tuple-element.91.refs_16_), channel_id=1, source_target_pairs={{0,4},{1,3},{2,6},{3,1},{4,0},{5,7},{6,2},{7,5},{8,12},{9,11},{10,... | collective-permute-start | bytes 3538952 | tf_op jit(solution)/shard_map/ppermute | solution.py:420
  149.3 20.1 %collective-permute-start.24 = (bf16[3,6,64,512]{3,2,1,0:T(8,128)(2,1)}, bf16[3,6,64,512]{3,2,1,0:T(8,128)(2,1)}, u32[]{:S(2)}, u32[]{:S(2)}) collective-permute-start(bf16[3,6,64,512]{3,2,1,0:T(8,128)(2,1)} %get-tuple-element.85.refs_31_.refs_24_.refs_15_), channel_id=1, source_target_pairs={{0,1},{1,0},{2,3},{3,2},{4,5},{5,4},{6,7},{7,6},{8,9},{9,8},{10,11... | collective-permute-start | bytes 3538952 | tf_op jit(solution)/shard_map/ppermute | solution.py:423
  149.3 20.1 %collective-permute-start.25 = (bf16[3,6,64,512]{3,2,1,0:T(8,128)(2,1)}, bf16[3,6,64,512]{3,2,1,0:T(8,128)(2,1)}, u32[]{:S(2)}, u32[]{:S(2)}) collective-permute-start(bf16[3,6,64,512]{3,2,1,0:T(8,128)(2,1)} %get-tuple-element.91.refs_16_), channel_id=1, source_target_pairs={{0,1},{1,0},{2,3},{3,2},{4,5},{5,4},{6,7},{7,6},{8,9},{9,8},{10,11... | collective-permute-start | bytes 3538952 | tf_op jit(solution)/shard_map/ppermute | solution.py:423
  149.8 19.6 %collective-permute-start.26 = (bf16[3,6,64,512]{3,2,1,0:T(8,128)(2,1)}, bf16[3,6,64,512]{3,2,1,0:T(8,128)(2,1)}, u32[]{:S(2)}, u32[]{:S(2)}) collective-permute-start(bf16[3,6,64,512]{3,2,1,0:T(8,128)(2,1)} %get-tuple-element.93.refs_17_), channel_id=1, source_target_pairs={{0,1},{1,0},{2,3},{3,2},{4,5},{5,4},{6,7},{7,6},{8,9},{9,8},{10,11... | collective-permute-start | bytes 3538952 | tf_op jit(solution)/shard_map/ppermute | solution.py:423
  168.9 3.4 %collective-permute-start.27 = (bf16[3,6,64,512]{3,2,1,0:T(8,128)(2,1)}, bf16[3,6,64,512]{3,2,1,0:T(8,128)(2,1)}, u32[]{:S(2)}, u32[]{:S(2)}) collective-permute-start(bf16[3,6,64,512]{3,2,1,0:T(8,128)(2,1)} %get-tuple-element.94.refs_18_), channel_id=1, source_target_pairs={{0,1},{1,0},{2,3},{3,2},{4,5},{5,4},{6,7},{7,6},{8,9},{9,8},{10,11... | collective-permute-start | bytes 3538952 | tf_op jit(solution)/shard_map/ppermute | solution.py:423

commit v3 on v2

--- a/solution.py
+++ b/solution.py
@@ -118,16 +118,18 @@
         pltpu.make_async_copy(source, held.at[i], read.at[i]) for i, source in enumerate(sources)
     ]
     width = held.shape[2] // parts
-    sends = [
-        pltpu.make_async_copy(held.at[:, :, pl.ds(i * width, width)], outs[i], sent.at[i])
-        for i in range(parts)
-    ]
     for copy in reads:
         copy.start()
-    for copy in reads:
+    sends = []
+    for i, copy in enumerate(reads):
         copy.wait()
-    for copy in sends:
-        copy.start()
+        for p in range(parts):
+            sends.append(
+                pltpu.make_async_copy(
+                    held.at[i, :, pl.ds(p * width, width)], outs[p].at[i], sent.at[len(sends)]
+                )
+            )
+            sends[-1].start()
     for copy in sends:
         copy.wait()
 
@@ -144,7 +146,7 @@
         scratch_shapes=[
             pltpu.VMEM((n_occ - 1, cap, rows, aux), got[0].dtype),
             pltpu.SemaphoreType.DMA((n_occ,)),
-            pltpu.SemaphoreType.DMA((parts,)),
+            pltpu.SemaphoreType.DMA((parts * (n_occ - 1),)),
         ],
         input_output_aliases={1: 0},
         compiler_params=pltpu.CompilerParams(vmem_limit_bytes=VMEM_LIMIT),
@@ -517,7 +519,7 @@
     token = relay(token, 1, 1)
     collect(2)
     arrive(1)
-    add([(early, n_parts, (0,)), (0, n_parts, (1,))])
+    add([(0, n_parts, (1,)), (early, n_parts, (0,))])
     token = relay(token, 2, 1)
     add([(0, n_parts, (2,))])
     arrive(2)

time: 207 us -> 206 us (level)
  transfers between devices with their start and end apart: 31 -> 31, of which waited for: 10 -> 11; matrix products, arithmetic and copies ran while one was open for 1% -> 1% of each run, Pallas kernels for 35% -> 34%
where the time goes in v3:
time: 206 us; the launch traced here: 203 us
  Pallas kernels  105 us (51%)
  waiting for transfers between devices  62.4 us (30%)
  starting transfers between devices  32.6 us (16%)
  local copies, waits for them, and re-layouts  2.9 us (1%)
    pallas_call x4, Pallas kernels, density(): pl.pallas_call(functools.partial(density_kernel, n_occ, n_blocks, cuts, j...  87.9 us
    all_to_all x3, waiting for transfers between devices, cross(): crossing.append([lax.all_to_all(gated[0], 'occ', 0, 0, tiled=True)])  27.6 us
    ppermute x12, waiting for transfers between devices, hop(): return lax.ppermute(block, 'virt', pairs)  26.1 us
    all_to_all x3, starting transfers between devices, cross(): crossing.append([lax.all_to_all(gated[0], 'occ', 0, 0, tiled=True)])  15.3 us
    ppermute x12, starting transfers between devices, hop(): return lax.ppermute(block, 'virt', pairs)  14 us
    pallas_call x3, Pallas kernels, stage(): pl.pallas_call(functools.partial(stage_kernel, n_occ, low, high, with_own...  10.6 us
    ppermute x16, waiting for transfers between devices, sibling(): return lax.ppermute(block, 'virt', [(d, d ^ 1) for d in range(n_virt)])  8.66 us
    pallas_call x3, Pallas kernels, join(): pl.pallas_call(functools.partial(join_kernel, n_occ, len(got), parts), ou...  6.06 us
  transfers between devices with their start and end apart: 31, of which 11 were waited for; matrix products, arithmetic and copies ran while one was open for 1% of the time, Pallas kernels for 34%

profile of v3, /device:TPU:0, one launch (start us, length us, event | category | flops | bytes accessed | tf_op | source)
XLA Modules:
  0.0 203.0 jit_solution(15818928831529327221)
XLA Ops:
  0.0 4.1 %shard_map.55 = (f32[8,128]{1,0:T(8,128)}, bf16[4,6,32,512]{3,2,1,0:T(8,128)(2,1)}, bf16[6,160,512]{2,1,0:T(8,128)(2,1)}) custom-call(s32[1]{0:T(128)} %bitcast.me.refs_0_, s32[4]{0:T(128)} %refs_1_.7, s32[16]{0:T(128)} %refs_2_.7, bf16[16,160,512]{2,1,0:T(8,128)(2,1)} %basis.5), custom_call_target="tpu_custom_call" | custom-call | flops 1024 | bytes 1024 | tf_op jit(solution)/shard_map/pallas_call | solution.py:80
  4.1 6.4 %all-to-all-start = ((bf16[4,6,32,512]{3,2,1,0:T(8,128)(2,1)}), bf16[4,6,32,512]{3,2,1,0:T(8,128)(2,1)}, u32[]{:S(2)}, u32[]{:S(2)}) async-start(bf16[4,6,32,512]{3,2,1,0:T(8,128)(2,1)} %get-tuple-element.60), calls=%async_computation | async-start | bytes 1572864 | tf_op jit(solution)/shard_map/all_to_all | solution.py:477
  10.5 1.5 collective-permute-start
  12.0 1.5 collective-permute-start.1
  13.5 3.3 %shard_map.57 = (f32[8,128]{1,0:T(8,128)}, bf16[4,6,64,512]{3,2,1,0:T(8,128)(2,1)}) custom-call(s32[1]{0:T(128)} %bitcast.me.refs_0_, s32[4]{0:T(128)} %refs_1_.7, s32[16]{0:T(128)} %refs_2_.7, bf16[16,160,512]{2,1,0:T(8,128)(2,1)} %basis.5, f32[8,128]{1,0:T(8,128)} %get-tuple-element.53.refs_0_), custom_call_target="tpu_custom_call", output_to_operand_aliasing={{0}: (4, {})} | custom-call | flops 1024 | bytes 1024 | tf_op jit(solution)/shard_map/pallas_call | solution.py:80
  16.8 3.3 %shard_map.58 = (f32[8,128]{1,0:T(8,128)}, bf16[4,6,64,512]{3,2,1,0:T(8,128)(2,1)}) custom-call(s32[1]{0:T(128)} %bitcast.me.refs_0_, s32[4]{0:T(128)} %refs_1_.7, s32[16]{0:T(128)} %refs_2_.7, bf16[16,160,512]{2,1,0:T(8,128)(2,1)} %basis.5, f32[8,128]{1,0:T(8,128)} %get-tuple-element.54.refs_0_), custom_call_target="tpu_custom_call", output_to_operand_aliasing={{0}: (4, {})} | custom-call | flops 1024 | bytes 1024 | tf_op jit(solution)/shard_map/pallas_call | solution.py:80
  20.1 10.6 %all-to-all-done.refs_0_ = bf16[4,6,32,512]{3,2,1,0:T(8,128)(2,1)} async-done(((bf16[4,6,32,512]{3,2,1,0:T(8,128)(2,1)}), bf16[4,6,32,512]{3,2,1,0:T(8,128)(2,1)}, u32[]{:S(2)}, u32[]{:S(2)}) %all-to-all-start) | async-done | bytes 786464 | tf_op jit(solution)/shard_map/all_to_all | solution.py:477
  30.7 4.4 %all-to-all-start.1 = ((bf16[4,6,64,512]{3,2,1,0:T(8,128)(2,1)}), bf16[4,6,64,512]{3,2,1,0:T(8,128)(2,1)}, u32[]{:S(2)}, u32[]{:S(2)}) async-start(bf16[4,6,64,512]{3,2,1,0:T(8,128)(2,1)} %get-tuple-element.68), calls=%async_computation.1 | async-start | bytes 3145728 | tf_op jit(solution)/shard_map/all_to_all | solution.py:477
  35.1 0.0 copy-start
  35.1 0.7 copy-done
  35.8 0.1 reshape.330
  35.9 0.1 stack.35
  36.0 0.6 gather_fusion
  36.6 0.7 reshape.331.refs_2_.refs_5_
  37.2 0.1 dynamic_slice.3
  37.3 0.8 copy.47.refs_1_.refs_4_
  38.1 1.8 shard_map.62
  39.9 0.0 collective-permute-done.1.refs_2_
  39.9 1.6 collective-permute-start.2
  41.5 1.5 collective-permute-start.3
  43.0 0.5 collective-permute-start.4
  43.5 0.0 collective-permute-start.6
  43.5 0.5 collective-permute-start.7
  44.0 16.0 %collective-permute-done.2.refs_1_ = bf16[6,160,512]{2,1,0:T(8,128)(2,1)} collective-permute-done((bf16[6,160,512]{2,1,0:T(8,128)(2,1)}, bf16[6,160,512]{2,1,0:T(8,128)(2,1)}, u32[]{:S(2)}, u32[]{:S(2)}) %collective-permute-start.2) | collective-permute-done | bytes 983072 | tf_op jit(solution)/shard_map/ppermute | solution.py:422
  60.1 0.0 collective-permute-done.3.refs_1_
  60.1 0.5 collective-permute-start.8
  60.6 5.8 %collective-permute-done.4.refs_2_ = bf16[3,6,32,512]{3,2,1,0:T(8,128)(2,1)} collective-permute-done((bf16[3,6,32,512]{3,2,1,0:T(8,128)(2,1)}, bf16[3,6,32,512]{3,2,1,0:T(8,128)(2,1)}, u32[]{:S(2)}, u32[]{:S(2)}) %collective-permute-start.4) | collective-permute-done | bytes 589856 | tf_op jit(solution)/shard_map/ppermute | solution.py:422
  66.4 1.5 collective-permute-start.5
  67.9 0.0 collective-permute-done.6.refs_11_
  67.9 0.0 collective-permute-start.11
  67.9 3.7 %all-to-all-done.1.refs_0_ = bf16[4,6,64,512]{3,2,1,0:T(8,128)(2,1)} async-done(((bf16[4,6,64,512]{3,2,1,0:T(8,128)(2,1)}), bf16[4,6,64,512]{3,2,1,0:T(8,128)(2,1)}, u32[]{:S(2)}, u32[]{:S(2)}) %all-to-all-start.1) | async-done | bytes 1572896 | tf_op jit(solution)/shard_map/all_to_all | solution.py:477
  71.6 2.1 %shard_map.66 = (f32[8,128]{1,0:T(8,128)}, bf16[3,6,64,512]{3,2,1,0:T(8,128)(2,1)}) custom-call(s32[1]{0:T(128)} %bitcast.me.refs_0_, f32[8,128]{1,0:T(8,128)} %get-tuple-element.67.token_in, bf16[4,6,64,512]{3,2,1,0:T(8,128)(2,1)} %all-to-all-done.1.refs_0_), custom_call_target="tpu_custom_call", output_to_operand_aliasing={{0}: (1, {})} | custom-call | flops 1024 | bytes 1024 | tf_op jit(solution)/shard_map/pallas_call | solution.py:141
  73.7 0.0 collective-permute-done.10.refs_19_
  73.7 1.6 collective-permute-start.14
  75.3 1.5 collective-permute-start.15
  76.8 4.5 %all-to-all-start.2 = ((bf16[4,6,64,512]{3,2,1,0:T(8,128)(2,1)}), bf16[4,6,64,512]{3,2,1,0:T(8,128)(2,1)}, u32[]{:S(2)}, u32[]{:S(2)}) async-start(bf16[4,6,64,512]{3,2,1,0:T(8,128)(2,1)} %get-tuple-element.79), calls=%async_computation.2 | async-start | bytes 3145728 | tf_op jit(solution)/shard_map/all_to_all | solution.py:477
  81.4 0.0 collective-permute-done.5.refs_1_
  81.4 0.1 collective-permute-start.9
  81.5 0.0 collective-permute-done.8.refs_13_
  81.5 0.5 collective-permute-start.12
  82.0 0.0 collective-permute-done.11.refs_20_
  82.0 0.1 collective-permute-start.13
  82.1 3.1 %collective-permute-done.12.refs_21_ = bf16[3,6,32,512]{3,2,1,0:T(8,128)(2,1)} collective-permute-done((bf16[3,6,32,512]{3,2,1,0:T(8,128)(2,1)}, bf16[3,6,32,512]{3,2,1,0:T(8,128)(2,1)}, u32[]{:S(2)}, u32[]{:S(2)}) %collective-permute-start.12) | collective-permute-done | bytes 589856 | tf_op jit(solution)/shard_map/ppermute | solution.py:425
  85.2 0.8 collective-permute-done.13.refs_22_
  86.0 13.2 %shard_map.68 = (f32[8,128]{1,0:T(8,128)}, f32[6,160,2048]{2,1,0:T(8,128)}) custom-call(s32[1]{0:T(128)} %bitcast.me.refs_0_, s32[4]{0:T(128)} %refs_1_.7, s32[16]{0:T(128)} %refs_2_.7, f32[16]{0:T(128)} %refs_3_.7, f32[160,1]{1,0:T(8,128)} %copy.47.refs_1_.refs_4_, f32[5,1,256]{2,1,0:T(1,128)} %reshape.331.refs_2_.refs_5_, ...), custom_call_target="tpu_custom_call", output_to_operand_aliasing={{0}: (6, {})} | custom-call | flops 1024 | bytes 1024 | tf_op jit(solution)/shard_map/pallas_call | solution.py:378
  99.2 3.1 %collective-permute-done.14.refs_1_ = bf16[3,6,64,512]{3,2,1,0:T(8,128)(2,1)} collective-permute-done((bf16[3,6,64,512]{3,2,1,0:T(8,128)(2,1)}, bf16[3,6,64,512]{3,2,1,0:T(8,128)(2,1)}, u32[]{:S(2)}, u32[]{:S(2)}) %collective-permute-start.14) | collective-permute-done | bytes 1179680 | tf_op jit(solution)/shard_map/ppermute | solution.py:422
  102.3 1.1 collective-permute-start.16
  103.4 0.5 collective-permute-start.18
  103.9 13.3 %all-to-all-done.2.refs_0_ = bf16[4,6,64,512]{3,2,1,0:T(8,128)(2,1)} async-done(((bf16[4,6,64,512]{3,2,1,0:T(8,128)(2,1)}), bf16[4,6,64,512]{3,2,1,0:T(8,128)(2,1)}, u32[]{:S(2)}, u32[]{:S(2)}) %all-to-all-start.2) | async-done | bytes 1572896 | tf_op jit(solution)/shard_map/all_to_all | solution.py:477
  117.1 2.1 %shard_map.70 = (f32[8,128]{1,0:T(8,128)}, bf16[3,6,64,512]{3,2,1,0:T(8,128)(2,1)}) custom-call(s32[1]{0:T(128)} %bitcast.me.refs_0_, f32[8,128]{1,0:T(8,128)} %get-tuple-element.78.token_in, bf16[4,6,64,512]{3,2,1,0:T(8,128)(2,1)} %all-to-all-done.2.refs_0_), custom_call_target="tpu_custom_call", output_to_operand_aliasing={{0}: (1, {})} | custom-call | flops 1024 | bytes 1024 | tf_op jit(solution)/shard_map/pallas_call | solution.py:141
  119.3 0.1 collective-permute-start.20
  119.4 0.9 collective-permute-start.21
  120.3 0.5 collective-permute-start.22
  120.8 1.7 collective-permute-done.20.refs_30_.refs_22_
  122.6 24.5 %shard_map.72 = (f32[8,128]{1,0:T(8,128)}, f32[6,160,2048]{2,1,0:T(8,128)}) custom-call(s32[1]{0:T(128)} %bitcast.me.refs_0_, s32[4]{0:T(128)} %refs_1_.7, s32[16]{0:T(128)} %refs_2_.7, f32[16]{0:T(128)} %refs_3_.7, f32[160,1]{1,0:T(8,128)} %copy.47.refs_1_.refs_4_, f32[5,1,256]{2,1,0:T(1,128)} %reshape.331.refs_2_.refs_5_, ...), custom_call_target="tpu_custom_call", output_to_operand_aliasing={{0}: (6, {})} | custom-call | flops 1024 | bytes 1024 | tf_op jit(solution)/shard_map/pallas_call | solution.py:378
  147.1 1.2 collective-permute-done.21.refs_1_
  148.3 0.3 collective-permute-start.23
  148.6 0.2 collective-permute-start.24
  148.8 0.3 collective-permute-start.25
  149.1 0.2 collective-permute-start.26
  149.3 19.0 %shard_map.74 = (f32[8,128]{1,0:T(8,128)}, f32[6,160,2048]{2,1,0:T(8,128)}) custom-call(s32[1]{0:T(128)} %bitcast.me.refs_0_, s32[4]{0:T(128)} %refs_1_.7, s32[16]{0:T(128)} %refs_2_.7, f32[16]{0:T(128)} %refs_3_.7, f32[160,1]{1,0:T(8,128)} %copy.47.refs_1_.refs_4_, f32[5,1,256]{2,1,0:T(1,128)} %reshape.331.refs_2_.refs_5_, ...), custom_call_target="tpu_custom_call", output_to_operand_aliasing={{0}: (6, {})} | custom-call | flops 1024 | bytes 1024 | tf_op jit(solution)/shard_map/pallas_call | solution.py:378
  168.3 0.3 collective-permute-start.27
  168.7 2.9 %collective-permute-done.27.refs_22_ = bf16[3,6,64,512]{3,2,1,0:T(8,128)(2,1)} collective-permute-done((bf16[3,6,64,512]{3,2,1,0:T(8,128)(2,1)}, bf16[3,6,64,512]{3,2,1,0:T(8,128)(2,1)}, u32[]{:S(2)}, u32[]{:S(2)}) %collective-permute-start.27) | collective-permute-done | bytes 1179680 | tf_op jit(solution)/shard_map/ppermute | solution.py:425
  171.6 31.2 %shard_map.76 = (f32[8,128]{1,0:T(8,128)}, bf16[6,160,2048]{2,1,0:T(8,128)(2,1)}) custom-call(s32[1]{0:T(128)} %bitcast.me.refs_0_, s32[4]{0:T(128)} %refs_1_.7, s32[16]{0:T(128)} %refs_2_.7, f32[16]{0:T(128)} %refs_3_.7, f32[160,1]{1,0:T(8,128)} %copy.47.refs_1_.refs_4_, f32[5,1,256]{2,1,0:T(1,128)} %reshape.331.refs_2_.refs_5_, ...), custom_call_target="tpu_custom_call", output_to_operand_aliasing={{0}: (6, {})} | custom-call | flops 1024 | bytes 1024 | tf_op jit(solution)/shard_map/pallas_call | solution.py:378
  (31 shorter events, 0.1 us)
Async XLA Ops:
  4.1 26.7 %all-to-all-start = ((bf16[4,6,32,512]{3,2,1,0:T(8,128)(2,1)}), bf16[4,6,32,512]{3,2,1,0:T(8,128)(2,1)}, u32[]{:S(2)}, u32[]{:S(2)}) async-start(bf16[4,6,32,512]{3,2,1,0:T(8,128)(2,1)} %get-tuple-element.60), calls=%async_computation | async-start | bytes 1572864 | tf_op jit(solution)/shard_map/all_to_all | solution.py:477
  10.5 29.4 %collective-permute-start = (bf16[6,160,512]{2,1,0:T(8,128)(2,1)}, bf16[6,160,512]{2,1,0:T(8,128)(2,1)}, u32[]{:S(2)}, u32[]{:S(2)}) collective-permute-start(bf16[6,160,512]{2,1,0:T(8,128)(2,1)} %get-tuple-element.62.refs_7_), channel_id=1, source_target_pairs={{0,2},{1,5},{2,0},{3,7},{4,6},{5,1},{6,4},{7,3},{8,10},{9,13},{10,... | collective-permute-start | bytes 2949128 | tf_op jit(solution)/shard_map/ppermute | solution.py:422
  12.0 27.9 %collective-permute-start.1 = (bf16[6,160,512]{2,1,0:T(8,128)(2,1)}, bf16[6,160,512]{2,1,0:T(8,128)(2,1)}, u32[]{:S(2)}, u32[]{:S(2)}) collective-permute-start(bf16[6,160,512]{2,1,0:T(8,128)(2,1)} %get-tuple-element.62.refs_7_), channel_id=1, source_target_pairs={{0,4},{1,3},{2,6},{3,1},{4,0},{5,7},{6,2},{7,5},{8,12},{9,11},{10,... | collective-permute-start | bytes 2949128 | tf_op jit(solution)/shard_map/ppermute | solution.py:422
  30.7 40.9 %all-to-all-start.1 = ((bf16[4,6,64,512]{3,2,1,0:T(8,128)(2,1)}), bf16[4,6,64,512]{3,2,1,0:T(8,128)(2,1)}, u32[]{:S(2)}, u32[]{:S(2)}) async-start(bf16[4,6,64,512]{3,2,1,0:T(8,128)(2,1)} %get-tuple-element.68), calls=%async_computation.1 | async-start | bytes 3145728 | tf_op jit(solution)/shard_map/all_to_all | solution.py:477
  35.1 0.7 copy-start
  39.9 20.1 %collective-permute-start.2 = (bf16[6,160,512]{2,1,0:T(8,128)(2,1)}, bf16[6,160,512]{2,1,0:T(8,128)(2,1)}, u32[]{:S(2)}, u32[]{:S(2)}) collective-permute-start(bf16[6,160,512]{2,1,0:T(8,128)(2,1)} %get-tuple-element.64.refs_8_), channel_id=1, source_target_pairs={{0,4},{1,3},{2,6},{3,1},{4,0},{5,7},{6,2},{7,5},{8,12},{9,11},{10,... | collective-permute-start | bytes 2949128 | tf_op jit(solution)/shard_map/ppermute | solution.py:422
  41.5 18.5 %collective-permute-start.3 = (bf16[3,6,32,512]{3,2,1,0:T(8,128)(2,1)}, bf16[3,6,32,512]{3,2,1,0:T(8,128)(2,1)}, u32[]{:S(2)}, u32[]{:S(2)}) collective-permute-start(bf16[3,6,32,512]{3,2,1,0:T(8,128)(2,1)} %get-tuple-element.66.refs_15_.refs_23_), channel_id=1, source_target_pairs={{0,2},{1,5},{2,0},{3,7},{4,6},{5,1},{6,4},{7,3},{8,10},{9,13},{10,... | collective-permute-start | bytes 1769480 | tf_op jit(solution)/shard_map/ppermute | solution.py:422
  43.0 23.3 %collective-permute-start.4 = (bf16[3,6,32,512]{3,2,1,0:T(8,128)(2,1)}, bf16[3,6,32,512]{3,2,1,0:T(8,128)(2,1)}, u32[]{:S(2)}, u32[]{:S(2)}) collective-permute-start(bf16[3,6,32,512]{3,2,1,0:T(8,128)(2,1)} %get-tuple-element.66.refs_15_.refs_23_), channel_id=1, source_target_pairs={{0,4},{1,3},{2,6},{3,1},{4,0},{5,7},{6,2},{7,5},{8,12},{9,11},{10,... | collective-permute-start | bytes 1769480 | tf_op jit(solution)/shard_map/ppermute | solution.py:422
  43.5 24.4 %collective-permute-start.6 = (bf16[6,160,512]{2,1,0:T(8,128)(2,1)}, bf16[6,160,512]{2,1,0:T(8,128)(2,1)}, u32[]{:S(2)}, u32[]{:S(2)}) collective-permute-start(bf16[6,160,512]{2,1,0:T(8,128)(2,1)} %get-tuple-element.62.refs_7_), channel_id=1, source_target_pairs={{0,1},{1,0},{2,3},{3,2},{4,5},{5,4},{6,7},{7,6},{8,9},{9,8},{10,11... | collective-permute-start | bytes 2949128 | tf_op jit(solution)/shard_map/ppermute | solution.py:425
  43.5 31.8 %collective-permute-start.7 = (bf16[6,160,512]{2,1,0:T(8,128)(2,1)}, bf16[6,160,512]{2,1,0:T(8,128)(2,1)}, u32[]{:S(2)}, u32[]{:S(2)}) collective-permute-start(bf16[6,160,512]{2,1,0:T(8,128)(2,1)} %get-tuple-element.64.refs_8_), channel_id=1, source_target_pairs={{0,1},{1,0},{2,3},{3,2},{4,5},{5,4},{6,7},{7,6},{8,9},{9,8},{10,11... | collective-permute-start | bytes 2949128 | tf_op jit(solution)/shard_map/ppermute | solution.py:425
  60.0 13.7 %collective-permute-start.10 = (bf16[3,6,32,512]{3,2,1,0:T(8,128)(2,1)}, bf16[3,6,32,512]{3,2,1,0:T(8,128)(2,1)}, u32[]{:S(2)}, u32[]{:S(2)}) collective-permute-start(bf16[3,6,32,512]{3,2,1,0:T(8,128)(2,1)} %get-tuple-element.66.refs_15_.refs_23_), channel_id=1, source_target_pairs={{0,1},{1,0},{2,3},{3,2},{4,5},{5,4},{6,7},{7,6},{8,9},{9,8},{10,11... | collective-permute-start | bytes 1769480 | tf_op jit(solution)/shard_map/ppermute | solution.py:425
  60.1 21.4 %collective-permute-start.8 = (bf16[6,160,512]{2,1,0:T(8,128)(2,1)}, bf16[6,160,512]{2,1,0:T(8,128)(2,1)}, u32[]{:S(2)}, u32[]{:S(2)}) collective-permute-start(bf16[6,160,512]{2,1,0:T(8,128)(2,1)} %get-tuple-element.72.refs_9_), channel_id=1, source_target_pairs={{0,1},{1,0},{2,3},{3,2},{4,5},{5,4},{6,7},{7,6},{8,9},{9,8},{10,11... | collective-permute-start | bytes 2949128 | tf_op jit(solution)/shard_map/ppermute | solution.py:425
  66.4 15.0 %collective-permute-start.5 = (bf16[3,6,32,512]{3,2,1,0:T(8,128)(2,1)}, bf16[3,6,32,512]{3,2,1,0:T(8,128)(2,1)}, u32[]{:S(2)}, u32[]{:S(2)}) collective-permute-start(bf16[3,6,32,512]{3,2,1,0:T(8,128)(2,1)} %get-tuple-element.70.refs_16_), channel_id=1, source_target_pairs={{0,4},{1,3},{2,6},{3,1},{4,0},{5,7},{6,2},{7,5},{8,12},{9,11},{10,... | collective-permute-start | bytes 1769480 | tf_op jit(solution)/shard_map/ppermute | solution.py:422
  67.9 14.1 %collective-permute-start.11 = (bf16[3,6,32,512]{3,2,1,0:T(8,128)(2,1)}, bf16[3,6,32,512]{3,2,1,0:T(8,128)(2,1)}, u32[]{:S(2)}, u32[]{:S(2)}) collective-permute-start(bf16[3,6,32,512]{3,2,1,0:T(8,128)(2,1)} %get-tuple-element.70.refs_16_), channel_id=1, source_target_pairs={{0,1},{1,0},{2,3},{3,2},{4,5},{5,4},{6,7},{7,6},{8,9},{9,8},{10,11... | collective-permute-start | bytes 1769480 | tf_op jit(solution)/shard_map/ppermute | solution.py:425
  73.7 28.5 %collective-permute-start.14 = (bf16[3,6,64,512]{3,2,1,0:T(8,128)(2,1)}, bf16[3,6,64,512]{3,2,1,0:T(8,128)(2,1)}, u32[]{:S(2)}, u32[]{:S(2)}) collective-permute-start(bf16[3,6,64,512]{3,2,1,0:T(8,128)(2,1)} %get-tuple-element.76.refs_23_.refs_15_.refs_24_), channel_id=1, source_target_pairs={{0,2},{1,5},{2,0},{3,7},{4,6},{5,1},{6,4},{7,3},{8,10},{9,13},{10,... | collective-permute-start | bytes 3538952 | tf_op jit(solution)/shard_map/ppermute | solution.py:422
  75.3 27.0 %collective-permute-start.15 = (bf16[3,6,64,512]{3,2,1,0:T(8,128)(2,1)}, bf16[3,6,64,512]{3,2,1,0:T(8,128)(2,1)}, u32[]{:S(2)}, u32[]{:S(2)}) collective-permute-start(bf16[3,6,64,512]{3,2,1,0:T(8,128)(2,1)} %get-tuple-element.76.refs_23_.refs_15_.refs_24_), channel_id=1, source_target_pairs={{0,4},{1,3},{2,6},{3,1},{4,0},{5,7},{6,2},{7,5},{8,12},{9,11},{10,... | collective-permute-start | bytes 3538952 | tf_op jit(solution)/shard_map/ppermute | solution.py:422
  76.8 40.3 %all-to-all-start.2 = ((bf16[4,6,64,512]{3,2,1,0:T(8,128)(2,1)}), bf16[4,6,64,512]{3,2,1,0:T(8,128)(2,1)}, u32[]{:S(2)}, u32[]{:S(2)}) async-start(bf16[4,6,64,512]{3,2,1,0:T(8,128)(2,1)} %get-tuple-element.79), calls=%async_computation.2 | async-start | bytes 3145728 | tf_op jit(solution)/shard_map/all_to_all | solution.py:477
  81.4 3.8 %collective-permute-start.9 = (bf16[6,160,512]{2,1,0:T(8,128)(2,1)}, bf16[6,160,512]{2,1,0:T(8,128)(2,1)}, u32[]{:S(2)}, u32[]{:S(2)}) collective-permute-start(bf16[6,160,512]{2,1,0:T(8,128)(2,1)} %get-tuple-element.73.refs_10_), channel_id=1, source_target_pairs={{0,1},{1,0},{2,3},{3,2},{4,5},{5,4},{6,7},{7,6},{8,9},{9,8},{10,11... | collective-permute-start | bytes 2949128 | tf_op jit(solution)/shard_map/ppermute | solution.py:425
  81.5 3.7 %collective-permute-start.12 = (bf16[3,6,32,512]{3,2,1,0:T(8,128)(2,1)}, bf16[3,6,32,512]{3,2,1,0:T(8,128)(2,1)}, u32[]{:S(2)}, u32[]{:S(2)}) collective-permute-start(bf16[3,6,32,512]{3,2,1,0:T(8,128)(2,1)} %get-tuple-element.74.refs_17_), channel_id=1, source_target_pairs={{0,1},{1,0},{2,3},{3,2},{4,5},{5,4},{6,7},{7,6},{8,9},{9,8},{10,11... | collective-permute-start | bytes 1769480 | tf_op jit(solution)/shard_map/ppermute | solution.py:425
  82.0 4.1 %collective-permute-start.13 = (bf16[3,6,32,512]{3,2,1,0:T(8,128)(2,1)}, bf16[3,6,32,512]{3,2,1,0:T(8,128)(2,1)}, u32[]{:S(2)}, u32[]{:S(2)}) collective-permute-start(bf16[3,6,32,512]{3,2,1,0:T(8,128)(2,1)} %get-tuple-element.75.refs_18_), channel_id=1, source_target_pairs={{0,1},{1,0},{2,3},{3,2},{4,5},{5,4},{6,7},{7,6},{8,9},{9,8},{10,11... | collective-permute-start | bytes 1769480 | tf_op jit(solution)/shard_map/ppermute | solution.py:425
  102.3 17.0 %collective-permute-start.16 = (bf16[3,6,64,512]{3,2,1,0:T(8,128)(2,1)}, bf16[3,6,64,512]{3,2,1,0:T(8,128)(2,1)}, u32[]{:S(2)}, u32[]{:S(2)}) collective-permute-start(bf16[3,6,64,512]{3,2,1,0:T(8,128)(2,1)} %get-tuple-element.81.refs_24_.refs_16_), channel_id=1, source_target_pairs={{0,4},{1,3},{2,6},{3,1},{4,0},{5,7},{6,2},{7,5},{8,12},{9,11},{10,... | collective-permute-start | bytes 3538952 | tf_op jit(solution)/shard_map/ppermute | solution.py:422
  103.4 16.9 %collective-permute-start.17 = (bf16[3,6,64,512]{3,2,1,0:T(8,128)(2,1)}, bf16[3,6,64,512]{3,2,1,0:T(8,128)(2,1)}, u32[]{:S(2)}, u32[]{:S(2)}) collective-permute-start(bf16[3,6,64,512]{3,2,1,0:T(8,128)(2,1)} %get-tuple-element.76.refs_23_.refs_15_.refs_24_), channel_id=1, source_target_pairs={{0,1},{1,0},{2,3},{3,2},{4,5},{5,4},{6,7},{7,6},{8,9},{9,8},{10,11... | collective-permute-start | bytes 3538952 | tf_op jit(solution)/shard_map/ppermute | solution.py:425
  103.4 17.4 %collective-permute-start.18 = (bf16[3,6,64,512]{3,2,1,0:T(8,128)(2,1)}, bf16[3,6,64,512]{3,2,1,0:T(8,128)(2,1)}, u32[]{:S(2)}, u32[]{:S(2)}) collective-permute-start(bf16[3,6,64,512]{3,2,1,0:T(8,128)(2,1)} %get-tuple-element.81.refs_24_.refs_16_), channel_id=1, source_target_pairs={{0,1},{1,0},{2,3},{3,2},{4,5},{5,4},{6,7},{7,6},{8,9},{9,8},{10,11... | collective-permute-start | bytes 3538952 | tf_op jit(solution)/shard_map/ppermute | solution.py:425
  103.9 16.9 %collective-permute-start.19 = (bf16[3,6,64,512]{3,2,1,0:T(8,128)(2,1)}, bf16[3,6,64,512]{3,2,1,0:T(8,128)(2,1)}, u32[]{:S(2)}, u32[]{:S(2)}) collective-permute-start(bf16[3,6,64,512]{3,2,1,0:T(8,128)(2,1)} %get-tuple-element.83.refs_25_.refs_17_), channel_id=1, source_target_pairs={{0,1},{1,0},{2,3},{3,2},{4,5},{5,4},{6,7},{7,6},{8,9},{9,8},{10,11... | collective-permute-start | bytes 3538952 | tf_op jit(solution)/shard_map/ppermute | solution.py:425
  119.3 3.3 %collective-permute-start.20 = (bf16[3,6,64,512]{3,2,1,0:T(8,128)(2,1)}, bf16[3,6,64,512]{3,2,1,0:T(8,128)(2,1)}, u32[]{:S(2)}, u32[]{:S(2)}) collective-permute-start(bf16[3,6,64,512]{3,2,1,0:T(8,128)(2,1)} %get-tuple-element.84.refs_26_.refs_18_), channel_id=1, source_target_pairs={{0,1},{1,0},{2,3},{3,2},{4,5},{5,4},{6,7},{7,6},{8,9},{9,8},{10,11... | collective-permute-start | bytes 3538952 | tf_op jit(solution)/shard_map/ppermute | solution.py:425
  119.4 28.9 %collective-permute-start.21 = (bf16[3,6,64,512]{3,2,1,0:T(8,128)(2,1)}, bf16[3,6,64,512]{3,2,1,0:T(8,128)(2,1)}, u32[]{:S(2)}, u32[]{:S(2)}) collective-permute-start(bf16[3,6,64,512]{3,2,1,0:T(8,128)(2,1)} %get-tuple-element.85.refs_31_.refs_24_.refs_15_), channel_id=1, source_target_pairs={{0,2},{1,5},{2,0},{3,7},{4,6},{5,1},{6,4},{7,3},{8,10},{9,13},{10,... | collective-permute-start | bytes 3538952 | tf_op jit(solution)/shard_map/ppermute | solution.py:422
  120.3 28.0 %collective-permute-start.22 = (bf16[3,6,64,512]{3,2,1,0:T(8,128)(2,1)}, bf16[3,6,64,512]{3,2,1,0:T(8,128)(2,1)}, u32[]{:S(2)}, u32[]{:S(2)}) collective-permute-start(bf16[3,6,64,512]{3,2,1,0:T(8,128)(2,1)} %get-tuple-element.85.refs_31_.refs_24_.refs_15_), channel_id=1, source_target_pairs={{0,4},{1,3},{2,6},{3,1},{4,0},{5,7},{6,2},{7,5},{8,12},{9,11},{10,... | collective-permute-start | bytes 3538952 | tf_op jit(solution)/shard_map/ppermute | solution.py:422
  148.3 20.0 %collective-permute-start.23 = (bf16[3,6,64,512]{3,2,1,0:T(8,128)(2,1)}, bf16[3,6,64,512]{3,2,1,0:T(8,128)(2,1)}, u32[]{:S(2)}, u32[]{:S(2)}) collective-permute-start(bf16[3,6,64,512]{3,2,1,0:T(8,128)(2,1)} %get-tuple-element.91.refs_16_), channel_id=1, source_target_pairs={{0,4},{1,3},{2,6},{3,1},{4,0},{5,7},{6,2},{7,5},{8,12},{9,11},{10,... | collective-permute-start | bytes 3538952 | tf_op jit(solution)/shard_map/ppermute | solution.py:422
  148.6 20.1 %collective-permute-start.24 = (bf16[3,6,64,512]{3,2,1,0:T(8,128)(2,1)}, bf16[3,6,64,512]{3,2,1,0:T(8,128)(2,1)}, u32[]{:S(2)}, u32[]{:S(2)}) collective-permute-start(bf16[3,6,64,512]{3,2,1,0:T(8,128)(2,1)} %get-tuple-element.85.refs_31_.refs_24_.refs_15_), channel_id=1, source_target_pairs={{0,1},{1,0},{2,3},{3,2},{4,5},{5,4},{6,7},{7,6},{8,9},{9,8},{10,11... | collective-permute-start | bytes 3538952 | tf_op jit(solution)/shard_map/ppermute | solution.py:425
  148.8 19.9 %collective-permute-start.25 = (bf16[3,6,64,512]{3,2,1,0:T(8,128)(2,1)}, bf16[3,6,64,512]{3,2,1,0:T(8,128)(2,1)}, u32[]{:S(2)}, u32[]{:S(2)}) collective-permute-start(bf16[3,6,64,512]{3,2,1,0:T(8,128)(2,1)} %get-tuple-element.91.refs_16_), channel_id=1, source_target_pairs={{0,1},{1,0},{2,3},{3,2},{4,5},{5,4},{6,7},{7,6},{8,9},{9,8},{10,11... | collective-permute-start | bytes 3538952 | tf_op jit(solution)/shard_map/ppermute | solution.py:425
  149.1 19.6 %collective-permute-start.26 = (bf16[3,6,64,512]{3,2,1,0:T(8,128)(2,1)}, bf16[3,6,64,512]{3,2,1,0:T(8,128)(2,1)}, u32[]{:S(2)}, u32[]{:S(2)}) collective-permute-start(bf16[3,6,64,512]{3,2,1,0:T(8,128)(2,1)} %get-tuple-element.93.refs_17_), channel_id=1, source_target_pairs={{0,1},{1,0},{2,3},{3,2},{4,5},{5,4},{6,7},{7,6},{8,9},{9,8},{10,11... | collective-permute-start | bytes 3538952 | tf_op jit(solution)/shard_map/ppermute | solution.py:425
  168.3 3.3 %collective-permute-start.27 = (bf16[3,6,64,512]{3,2,1,0:T(8,128)(2,1)}, bf16[3,6,64,512]{3,2,1,0:T(8,128)(2,1)}, u32[]{:S(2)}, u32[]{:S(2)}) collective-permute-start(bf16[3,6,64,512]{3,2,1,0:T(8,128)(2,1)} %get-tuple-element.94.refs_18_), channel_id=1, source_target_pairs={{0,1},{1,0},{2,3},{3,2},{4,5},{5,4},{6,7},{7,6},{8,9},{9,8},{10,11... | collective-permute-start | bytes 3538952 | tf_op jit(solution)/shard_map/ppermute | solution.py:425

commit v4 on v3

--- a/solution.py
+++ b/solution.py
@@ -519,9 +519,9 @@
     token = relay(token, 1, 1)
     collect(2)
     arrive(1)
-    add([(0, n_parts, (1,)), (early, n_parts, (0,))])
+    add([(0, n_parts, (1,)), (early, n_parts, (0, 2))])
     token = relay(token, 2, 1)
-    add([(0, n_parts, (2,))])
+    add([(0, early, (2,))])
     arrive(2)
     add([(0, n_parts, (3, 4))], True)
     return total.reshape(1, CAP, width, n_occ * aux)

time: 206 us -> 207 us (level)
  no operation moved by 1% of the time
where the time goes in v4:
time: 207 us; the launch traced here: 203 us
  Pallas kernels  104 us (50%)
  waiting for transfers between devices  62.8 us (30%)
  starting transfers between devices  32.6 us (16%)
  local copies, waits for them, and re-layouts  2.9 us (1%)
    pallas_call x4, Pallas kernels, density(): pl.pallas_call(functools.partial(density_kernel, n_occ, n_blocks, cuts, j...  87.5 us
    all_to_all x3, waiting for transfers between devices, cross(): crossing.append([lax.all_to_all(gated[0], 'occ', 0, 0, tiled=True)])  27.5 us
    ppermute x12, waiting for transfers between devices, hop(): return lax.ppermute(block, 'virt', pairs)  26.4 us
    all_to_all x3, starting transfers between devices, cross(): crossing.append([lax.all_to_all(gated[0], 'occ', 0, 0, tiled=True)])  15.3 us
    ppermute x12, starting transfers between devices, hop(): return lax.ppermute(block, 'virt', pairs)  14.3 us
    pallas_call x3, Pallas kernels, stage(): pl.pallas_call(functools.partial(stage_kernel, n_occ, low, high, with_own...  10.7 us
    ppermute x16, waiting for transfers between devices, sibling(): return lax.ppermute(block, 'virt', [(d, d ^ 1) for d in range(n_virt)])  8.92 us
    pallas_call x3, Pallas kernels, join(): pl.pallas_call(functools.partial(join_kernel, n_occ, len(got), parts), ou...  6.06 us
  transfers between devices with their start and end apart: 31, of which 11 were waited for; matrix products, arithmetic and copies ran while one was open for 1% of the time, Pallas kernels for 34%

profile of v4, /device:TPU:0, one launch (start us, length us, event | category | flops | bytes accessed | tf_op | source)
XLA Modules:
  0.0 203.1 jit_solution(15786014585221588806)
XLA Ops:
  0.0 4.1 %shard_map.55 = (f32[8,128]{1,0:T(8,128)}, bf16[4,6,32,512]{3,2,1,0:T(8,128)(2,1)}, bf16[6,160,512]{2,1,0:T(8,128)(2,1)}) custom-call(s32[1]{0:T(128)} %bitcast.me.refs_0_, s32[4]{0:T(128)} %refs_1_.7, s32[16]{0:T(128)} %refs_2_.7, bf16[16,160,512]{2,1,0:T(8,128)(2,1)} %basis.5), custom_call_target="tpu_custom_call" | custom-call | flops 1024 | bytes 1024 | tf_op jit(solution)/shard_map/pallas_call | solution.py:80
  4.1 6.4 %all-to-all-start = ((bf16[4,6,32,512]{3,2,1,0:T(8,128)(2,1)}), bf16[4,6,32,512]{3,2,1,0:T(8,128)(2,1)}, u32[]{:S(2)}, u32[]{:S(2)}) async-start(bf16[4,6,32,512]{3,2,1,0:T(8,128)(2,1)} %get-tuple-element.60), calls=%async_computation | async-start | bytes 1572864 | tf_op jit(solution)/shard_map/all_to_all | solution.py:477
  10.4 1.5 collective-permute-start
  11.9 1.5 collective-permute-start.1
  13.4 3.4 %shard_map.57 = (f32[8,128]{1,0:T(8,128)}, bf16[4,6,64,512]{3,2,1,0:T(8,128)(2,1)}) custom-call(s32[1]{0:T(128)} %bitcast.me.refs_0_, s32[4]{0:T(128)} %refs_1_.7, s32[16]{0:T(128)} %refs_2_.7, bf16[16,160,512]{2,1,0:T(8,128)(2,1)} %basis.5, f32[8,128]{1,0:T(8,128)} %get-tuple-element.53.refs_0_), custom_call_target="tpu_custom_call", output_to_operand_aliasing={{0}: (4, {})} | custom-call | flops 1024 | bytes 1024 | tf_op jit(solution)/shard_map/pallas_call | solution.py:80
  16.8 3.3 %shard_map.58 = (f32[8,128]{1,0:T(8,128)}, bf16[4,6,64,512]{3,2,1,0:T(8,128)(2,1)}) custom-call(s32[1]{0:T(128)} %bitcast.me.refs_0_, s32[4]{0:T(128)} %refs_1_.7, s32[16]{0:T(128)} %refs_2_.7, bf16[16,160,512]{2,1,0:T(8,128)(2,1)} %basis.5, f32[8,128]{1,0:T(8,128)} %get-tuple-element.54.refs_0_), custom_call_target="tpu_custom_call", output_to_operand_aliasing={{0}: (4, {})} | custom-call | flops 1024 | bytes 1024 | tf_op jit(solution)/shard_map/pallas_call | solution.py:80
  20.2 10.5 %all-to-all-done.refs_0_ = bf16[4,6,32,512]{3,2,1,0:T(8,128)(2,1)} async-done(((bf16[4,6,32,512]{3,2,1,0:T(8,128)(2,1)}), bf16[4,6,32,512]{3,2,1,0:T(8,128)(2,1)}, u32[]{:S(2)}, u32[]{:S(2)}) %all-to-all-start) | async-done | bytes 786464 | tf_op jit(solution)/shard_map/all_to_all | solution.py:477
  30.6 4.4 %all-to-all-start.1 = ((bf16[4,6,64,512]{3,2,1,0:T(8,128)(2,1)}), bf16[4,6,64,512]{3,2,1,0:T(8,128)(2,1)}, u32[]{:S(2)}, u32[]{:S(2)}) async-start(bf16[4,6,64,512]{3,2,1,0:T(8,128)(2,1)} %get-tuple-element.68), calls=%async_computation.1 | async-start | bytes 3145728 | tf_op jit(solution)/shard_map/all_to_all | solution.py:477
  35.0 0.0 copy-start
  35.0 0.7 copy-done
  35.7 0.1 reshape.330
  35.8 0.1 stack.35
  35.9 0.6 gather_fusion
  36.5 0.7 reshape.331.refs_2_.refs_5_
  37.1 0.1 dynamic_slice.3
  37.2 0.8 copy.47.refs_1_.refs_4_
  38.0 1.8 shard_map.62
  39.8 0.0 collective-permute-done.1.refs_2_
  39.9 1.6 collective-permute-start.2
  41.5 1.5 collective-permute-start.3
  42.9 0.5 collective-permute-start.4
  43.5 0.5 collective-permute-start.7
  44.0 16.0 %collective-permute-done.2.refs_1_ = bf16[6,160,512]{2,1,0:T(8,128)(2,1)} collective-permute-done((bf16[6,160,512]{2,1,0:T(8,128)(2,1)}, bf16[6,160,512]{2,1,0:T(8,128)(2,1)}, u32[]{:S(2)}, u32[]{:S(2)}) %collective-permute-start.2) | collective-permute-done | bytes 983072 | tf_op jit(solution)/shard_map/ppermute | solution.py:422
  60.0 0.0 collective-permute-done.3.refs_1_
  60.0 0.5 collective-permute-start.8
  60.5 5.8 %collective-permute-done.4.refs_2_ = bf16[3,6,32,512]{3,2,1,0:T(8,128)(2,1)} collective-permute-done((bf16[3,6,32,512]{3,2,1,0:T(8,128)(2,1)}, bf16[3,6,32,512]{3,2,1,0:T(8,128)(2,1)}, u32[]{:S(2)}, u32[]{:S(2)}) %collective-permute-start.4) | collective-permute-done | bytes 589856 | tf_op jit(solution)/shard_map/ppermute | solution.py:422
  66.3 1.5 collective-permute-start.5
  67.8 0.0 collective-permute-done.6.refs_11_
  67.8 0.0 collective-permute-start.11
  67.8 3.7 %all-to-all-done.1.refs_0_ = bf16[4,6,64,512]{3,2,1,0:T(8,128)(2,1)} async-done(((bf16[4,6,64,512]{3,2,1,0:T(8,128)(2,1)}), bf16[4,6,64,512]{3,2,1,0:T(8,128)(2,1)}, u32[]{:S(2)}, u32[]{:S(2)}) %all-to-all-start.1) | async-done | bytes 1572896 | tf_op jit(solution)/shard_map/all_to_all | solution.py:477
  71.5 2.1 %shard_map.66 = (f32[8,128]{1,0:T(8,128)}, bf16[3,6,64,512]{3,2,1,0:T(8,128)(2,1)}) custom-call(s32[1]{0:T(128)} %bitcast.me.refs_0_, f32[8,128]{1,0:T(8,128)} %get-tuple-element.67.token_in, bf16[4,6,64,512]{3,2,1,0:T(8,128)(2,1)} %all-to-all-done.1.refs_0_), custom_call_target="tpu_custom_call", output_to_operand_aliasing={{0}: (1, {})} | custom-call | flops 1024 | bytes 1024 | tf_op jit(solution)/shard_map/pallas_call | solution.py:141
  73.6 0.0 collective-permute-done.10.refs_19_
  73.7 1.6 collective-permute-start.14
  75.2 1.5 collective-permute-start.15
  76.7 4.5 %all-to-all-start.2 = ((bf16[4,6,64,512]{3,2,1,0:T(8,128)(2,1)}), bf16[4,6,64,512]{3,2,1,0:T(8,128)(2,1)}, u32[]{:S(2)}, u32[]{:S(2)}) async-start(bf16[4,6,64,512]{3,2,1,0:T(8,128)(2,1)} %get-tuple-element.79), calls=%async_computation.2 | async-start | bytes 3145728 | tf_op jit(solution)/shard_map/all_to_all | solution.py:477
  81.3 0.0 collective-permute-done.5.refs_1_
  81.3 0.1 collective-permute-start.9
  81.4 0.0 collective-permute-done.8.refs_13_
  81.4 0.5 collective-permute-start.12
  81.9 0.0 collective-permute-done.11.refs_20_
  81.9 0.1 collective-permute-start.13
  82.0 3.1 %collective-permute-done.12.refs_21_ = bf16[3,6,32,512]{3,2,1,0:T(8,128)(2,1)} collective-permute-done((bf16[3,6,32,512]{3,2,1,0:T(8,128)(2,1)}, bf16[3,6,32,512]{3,2,1,0:T(8,128)(2,1)}, u32[]{:S(2)}, u32[]{:S(2)}) %collective-permute-start.12) | collective-permute-done | bytes 589856 | tf_op jit(solution)/shard_map/ppermute | solution.py:425
  85.1 0.0 collective-permute-done.9.refs_14_
  85.1 0.8 collective-permute-done.13.refs_22_
  86.0 13.2 %shard_map.68 = (f32[8,128]{1,0:T(8,128)}, f32[6,160,2048]{2,1,0:T(8,128)}) custom-call(s32[1]{0:T(128)} %bitcast.me.refs_0_, s32[4]{0:T(128)} %refs_1_.7, s32[16]{0:T(128)} %refs_2_.7, f32[16]{0:T(128)} %refs_3_.7, f32[160,1]{1,0:T(8,128)} %copy.47.refs_1_.refs_4_, f32[5,1,256]{2,1,0:T(1,128)} %reshape.331.refs_2_.refs_5_, ...), custom_call_target="tpu_custom_call", output_to_operand_aliasing={{0}: (6, {})} | custom-call | flops 1024 | bytes 1024 | tf_op jit(solution)/shard_map/pallas_call | solution.py:378
  99.1 3.1 %collective-permute-done.14.refs_1_ = bf16[3,6,64,512]{3,2,1,0:T(8,128)(2,1)} collective-permute-done((bf16[3,6,64,512]{3,2,1,0:T(8,128)(2,1)}, bf16[3,6,64,512]{3,2,1,0:T(8,128)(2,1)}, u32[]{:S(2)}, u32[]{:S(2)}) %collective-permute-start.14) | collective-permute-done | bytes 1179680 | tf_op jit(solution)/shard_map/ppermute | solution.py:422
  102.2 0.0 collective-permute-done.15.refs_2_
  102.2 1.1 collective-permute-start.16
  103.3 0.5 collective-permute-start.18
  103.8 13.3 %all-to-all-done.2.refs_0_ = bf16[4,6,64,512]{3,2,1,0:T(8,128)(2,1)} async-done(((bf16[4,6,64,512]{3,2,1,0:T(8,128)(2,1)}), bf16[4,6,64,512]{3,2,1,0:T(8,128)(2,1)}, u32[]{:S(2)}, u32[]{:S(2)}) %all-to-all-start.2) | async-done | bytes 1572896 | tf_op jit(solution)/shard_map/all_to_all | solution.py:477
  117.1 2.1 %shard_map.70 = (f32[8,128]{1,0:T(8,128)}, bf16[3,6,64,512]{3,2,1,0:T(8,128)(2,1)}) custom-call(s32[1]{0:T(128)} %bitcast.me.refs_0_, f32[8,128]{1,0:T(8,128)} %get-tuple-element.78.token_in, bf16[4,6,64,512]{3,2,1,0:T(8,128)(2,1)} %all-to-all-done.2.refs_0_), custom_call_target="tpu_custom_call", output_to_operand_aliasing={{0}: (1, {})} | custom-call | flops 1024 | bytes 1024 | tf_op jit(solution)/shard_map/pallas_call | solution.py:141
  119.2 0.1 collective-permute-start.20
  119.3 0.9 collective-permute-start.21
  120.2 0.5 collective-permute-start.22
  120.7 1.7 collective-permute-done.20.refs_30_.refs_22_
  122.5 29.4 %shard_map.72 = (f32[8,128]{1,0:T(8,128)}, f32[6,160,2048]{2,1,0:T(8,128)}) custom-call(s32[1]{0:T(128)} %bitcast.me.refs_0_, s32[4]{0:T(128)} %refs_1_.7, s32[16]{0:T(128)} %refs_2_.7, f32[16]{0:T(128)} %refs_3_.7, f32[160,1]{1,0:T(8,128)} %copy.47.refs_1_.refs_4_, f32[5,1,256]{2,1,0:T(1,128)} %reshape.331.refs_2_.refs_5_, ...), custom_call_target="tpu_custom_call", output_to_operand_aliasing={{0}: (6, {})} | custom-call | flops 1024 | bytes 1024 | tf_op jit(solution)/shard_map/pallas_call | solution.py:378
  151.9 0.6 collective-permute-start.23
  152.5 0.2 collective-permute-start.24
  152.8 0.3 collective-permute-start.25
  153.0 0.2 collective-permute-start.26
  153.3 13.8 %shard_map.74 = (f32[8,128]{1,0:T(8,128)}, f32[6,160,2048]{2,1,0:T(8,128)}) custom-call(s32[1]{0:T(128)} %bitcast.me.refs_0_, s32[4]{0:T(128)} %refs_1_.7, s32[16]{0:T(128)} %refs_2_.7, f32[16]{0:T(128)} %refs_3_.7, f32[160,1]{1,0:T(8,128)} %copy.47.refs_1_.refs_4_, f32[5,1,256]{2,1,0:T(1,128)} %reshape.331.refs_2_.refs_5_, ...), custom_call_target="tpu_custom_call", output_to_operand_aliasing={{0}: (6, {})} | custom-call | flops 1024 | bytes 1024 | tf_op jit(solution)/shard_map/pallas_call | solution.py:378
  167.0 1.5 collective-permute-done.23.refs_1_
  168.5 3.2 %collective-permute-done.27.refs_22_ = bf16[3,6,64,512]{3,2,1,0:T(8,128)(2,1)} collective-permute-done((bf16[3,6,64,512]{3,2,1,0:T(8,128)(2,1)}, bf16[3,6,64,512]{3,2,1,0:T(8,128)(2,1)}, u32[]{:S(2)}, u32[]{:S(2)}) %collective-permute-start.27) | collective-permute-done | bytes 1179680 | tf_op jit(solution)/shard_map/ppermute | solution.py:425
  171.7 31.2 %shard_map.76 = (f32[8,128]{1,0:T(8,128)}, bf16[6,160,2048]{2,1,0:T(8,128)(2,1)}) custom-call(s32[1]{0:T(128)} %bitcast.me.refs_0_, s32[4]{0:T(128)} %refs_1_.7, s32[16]{0:T(128)} %refs_2_.7, f32[16]{0:T(128)} %refs_3_.7, f32[160,1]{1,0:T(8,128)} %copy.47.refs_1_.refs_4_, f32[5,1,256]{2,1,0:T(1,128)} %reshape.331.refs_2_.refs_5_, ...), custom_call_target="tpu_custom_call", output_to_operand_aliasing={{0}: (6, {})} | custom-call | flops 1024 | bytes 1024 | tf_op jit(solution)/shard_map/pallas_call | solution.py:378
  (31 shorter events, 0.1 us)
Async XLA Ops:
  4.1 26.6 %all-to-all-start = ((bf16[4,6,32,512]{3,2,1,0:T(8,128)(2,1)}), bf16[4,6,32,512]{3,2,1,0:T(8,128)(2,1)}, u32[]{:S(2)}, u32[]{:S(2)}) async-start(bf16[4,6,32,512]{3,2,1,0:T(8,128)(2,1)} %get-tuple-element.60), calls=%async_computation | async-start | bytes 1572864 | tf_op jit(solution)/shard_map/all_to_all | solution.py:477
  10.4 29.4 %collective-permute-start = (bf16[6,160,512]{2,1,0:T(8,128)(2,1)}, bf16[6,160,512]{2,1,0:T(8,128)(2,1)}, u32[]{:S(2)}, u32[]{:S(2)}) collective-permute-start(bf16[6,160,512]{2,1,0:T(8,128)(2,1)} %get-tuple-element.62.refs_7_), channel_id=1, source_target_pairs={{0,2},{1,5},{2,0},{3,7},{4,6},{5,1},{6,4},{7,3},{8,10},{9,13},{10,... | collective-permute-start | bytes 2949128 | tf_op jit(solution)/shard_map/ppermute | solution.py:422
  11.9 27.9 %collective-permute-start.1 = (bf16[6,160,512]{2,1,0:T(8,128)(2,1)}, bf16[6,160,512]{2,1,0:T(8,128)(2,1)}, u32[]{:S(2)}, u32[]{:S(2)}) collective-permute-start(bf16[6,160,512]{2,1,0:T(8,128)(2,1)} %get-tuple-element.62.refs_7_), channel_id=1, source_target_pairs={{0,4},{1,3},{2,6},{3,1},{4,0},{5,7},{6,2},{7,5},{8,12},{9,11},{10,... | collective-permute-start | bytes 2949128 | tf_op jit(solution)/shard_map/ppermute | solution.py:422
  30.6 40.9 %all-to-all-start.1 = ((bf16[4,6,64,512]{3,2,1,0:T(8,128)(2,1)}), bf16[4,6,64,512]{3,2,1,0:T(8,128)(2,1)}, u32[]{:S(2)}, u32[]{:S(2)}) async-start(bf16[4,6,64,512]{3,2,1,0:T(8,128)(2,1)} %get-tuple-element.68), calls=%async_computation.1 | async-start | bytes 3145728 | tf_op jit(solution)/shard_map/all_to_all | solution.py:477
  35.0 0.7 copy-start
  39.9 20.1 %collective-permute-start.2 = (bf16[6,160,512]{2,1,0:T(8,128)(2,1)}, bf16[6,160,512]{2,1,0:T(8,128)(2,1)}, u32[]{:S(2)}, u32[]{:S(2)}) collective-permute-start(bf16[6,160,512]{2,1,0:T(8,128)(2,1)} %get-tuple-element.64.refs_8_), channel_id=1, source_target_pairs={{0,4},{1,3},{2,6},{3,1},{4,0},{5,7},{6,2},{7,5},{8,12},{9,11},{10,... | collective-permute-start | bytes 2949128 | tf_op jit(solution)/shard_map/ppermute | solution.py:422
  41.5 18.5 %collective-permute-start.3 = (bf16[3,6,32,512]{3,2,1,0:T(8,128)(2,1)}, bf16[3,6,32,512]{3,2,1,0:T(8,128)(2,1)}, u32[]{:S(2)}, u32[]{:S(2)}) collective-permute-start(bf16[3,6,32,512]{3,2,1,0:T(8,128)(2,1)} %get-tuple-element.66.refs_15_.refs_23_), channel_id=1, source_target_pairs={{0,2},{1,5},{2,0},{3,7},{4,6},{5,1},{6,4},{7,3},{8,10},{9,13},{10,... | collective-permute-start | bytes 1769480 | tf_op jit(solution)/shard_map/ppermute | solution.py:422
  42.9 23.3 %collective-permute-start.4 = (bf16[3,6,32,512]{3,2,1,0:T(8,128)(2,1)}, bf16[3,6,32,512]{3,2,1,0:T(8,128)(2,1)}, u32[]{:S(2)}, u32[]{:S(2)}) collective-permute-start(bf16[3,6,32,512]{3,2,1,0:T(8,128)(2,1)} %get-tuple-element.66.refs_15_.refs_23_), channel_id=1, source_target_pairs={{0,4},{1,3},{2,6},{3,1},{4,0},{5,7},{6,2},{7,5},{8,12},{9,11},{10,... | collective-permute-start | bytes 1769480 | tf_op jit(solution)/shard_map/ppermute | solution.py:422
  43.5 24.4 %collective-permute-start.6 = (bf16[6,160,512]{2,1,0:T(8,128)(2,1)}, bf16[6,160,512]{2,1,0:T(8,128)(2,1)}, u32[]{:S(2)}, u32[]{:S(2)}) collective-permute-start(bf16[6,160,512]{2,1,0:T(8,128)(2,1)} %get-tuple-element.62.refs_7_), channel_id=1, source_target_pairs={{0,1},{1,0},{2,3},{3,2},{4,5},{5,4},{6,7},{7,6},{8,9},{9,8},{10,11... | collective-permute-start | bytes 2949128 | tf_op jit(solution)/shard_map/ppermute | solution.py:425
  43.5 31.8 %collective-permute-start.7 = (bf16[6,160,512]{2,1,0:T(8,128)(2,1)}, bf16[6,160,512]{2,1,0:T(8,128)(2,1)}, u32[]{:S(2)}, u32[]{:S(2)}) collective-permute-start(bf16[6,160,512]{2,1,0:T(8,128)(2,1)} %get-tuple-element.64.refs_8_), channel_id=1, source_target_pairs={{0,1},{1,0},{2,3},{3,2},{4,5},{5,4},{6,7},{7,6},{8,9},{9,8},{10,11... | collective-permute-start | bytes 2949128 | tf_op jit(solution)/shard_map/ppermute | solution.py:425
  60.0 13.7 %collective-permute-start.10 = (bf16[3,6,32,512]{3,2,1,0:T(8,128)(2,1)}, bf16[3,6,32,512]{3,2,1,0:T(8,128)(2,1)}, u32[]{:S(2)}, u32[]{:S(2)}) collective-permute-start(bf16[3,6,32,512]{3,2,1,0:T(8,128)(2,1)} %get-tuple-element.66.refs_15_.refs_23_), channel_id=1, source_target_pairs={{0,1},{1,0},{2,3},{3,2},{4,5},{5,4},{6,7},{7,6},{8,9},{9,8},{10,11... | collective-permute-start | bytes 1769480 | tf_op jit(solution)/shard_map/ppermute | solution.py:425
  60.0 21.4 %collective-permute-start.8 = (bf16[6,160,512]{2,1,0:T(8,128)(2,1)}, bf16[6,160,512]{2,1,0:T(8,128)(2,1)}, u32[]{:S(2)}, u32[]{:S(2)}) collective-permute-start(bf16[6,160,512]{2,1,0:T(8,128)(2,1)} %get-tuple-element.72.refs_9_), channel_id=1, source_target_pairs={{0,1},{1,0},{2,3},{3,2},{4,5},{5,4},{6,7},{7,6},{8,9},{9,8},{10,11... | collective-permute-start | bytes 2949128 | tf_op jit(solution)/shard_map/ppermute | solution.py:425
  66.3 15.0 %collective-permute-start.5 = (bf16[3,6,32,512]{3,2,1,0:T(8,128)(2,1)}, bf16[3,6,32,512]{3,2,1,0:T(8,128)(2,1)}, u32[]{:S(2)}, u32[]{:S(2)}) collective-permute-start(bf16[3,6,32,512]{3,2,1,0:T(8,128)(2,1)} %get-tuple-element.70.refs_16_), channel_id=1, source_target_pairs={{0,4},{1,3},{2,6},{3,1},{4,0},{5,7},{6,2},{7,5},{8,12},{9,11},{10,... | collective-permute-start | bytes 1769480 | tf_op jit(solution)/shard_map/ppermute | solution.py:422
  67.8 14.1 %collective-permute-start.11 = (bf16[3,6,32,512]{3,2,1,0:T(8,128)(2,1)}, bf16[3,6,32,512]{3,2,1,0:T(8,128)(2,1)}, u32[]{:S(2)}, u32[]{:S(2)}) collective-permute-start(bf16[3,6,32,512]{3,2,1,0:T(8,128)(2,1)} %get-tuple-element.70.refs_16_), channel_id=1, source_target_pairs={{0,1},{1,0},{2,3},{3,2},{4,5},{5,4},{6,7},{7,6},{8,9},{9,8},{10,11... | collective-permute-start | bytes 1769480 | tf_op jit(solution)/shard_map/ppermute | solution.py:425
  73.7 28.5 %collective-permute-start.14 = (bf16[3,6,64,512]{3,2,1,0:T(8,128)(2,1)}, bf16[3,6,64,512]{3,2,1,0:T(8,128)(2,1)}, u32[]{:S(2)}, u32[]{:S(2)}) collective-permute-start(bf16[3,6,64,512]{3,2,1,0:T(8,128)(2,1)} %get-tuple-element.76.refs_23_.refs_15_.refs_24_), channel_id=1, source_target_pairs={{0,2},{1,5},{2,0},{3,7},{4,6},{5,1},{6,4},{7,3},{8,10},{9,13},{10,... | collective-permute-start | bytes 3538952 | tf_op jit(solution)/shard_map/ppermute | solution.py:422
  75.2 27.0 %collective-permute-start.15 = (bf16[3,6,64,512]{3,2,1,0:T(8,128)(2,1)}, bf16[3,6,64,512]{3,2,1,0:T(8,128)(2,1)}, u32[]{:S(2)}, u32[]{:S(2)}) collective-permute-start(bf16[3,6,64,512]{3,2,1,0:T(8,128)(2,1)} %get-tuple-element.76.refs_23_.refs_15_.refs_24_), channel_id=1, source_target_pairs={{0,4},{1,3},{2,6},{3,1},{4,0},{5,7},{6,2},{7,5},{8,12},{9,11},{10,... | collective-permute-start | bytes 3538952 | tf_op jit(solution)/shard_map/ppermute | solution.py:422
  76.7 40.3 %all-to-all-start.2 = ((bf16[4,6,64,512]{3,2,1,0:T(8,128)(2,1)}), bf16[4,6,64,512]{3,2,1,0:T(8,128)(2,1)}, u32[]{:S(2)}, u32[]{:S(2)}) async-start(bf16[4,6,64,512]{3,2,1,0:T(8,128)(2,1)} %get-tuple-element.79), calls=%async_computation.2 | async-start | bytes 3145728 | tf_op jit(solution)/shard_map/all_to_all | solution.py:477
  81.3 3.8 %collective-permute-start.9 = (bf16[6,160,512]{2,1,0:T(8,128)(2,1)}, bf16[6,160,512]{2,1,0:T(8,128)(2,1)}, u32[]{:S(2)}, u32[]{:S(2)}) collective-permute-start(bf16[6,160,512]{2,1,0:T(8,128)(2,1)} %get-tuple-element.73.refs_10_), channel_id=1, source_target_pairs={{0,1},{1,0},{2,3},{3,2},{4,5},{5,4},{6,7},{7,6},{8,9},{9,8},{10,11... | collective-permute-start | bytes 2949128 | tf_op jit(solution)/shard_map/ppermute | solution.py:425
  81.4 3.7 %collective-permute-start.12 = (bf16[3,6,32,512]{3,2,1,0:T(8,128)(2,1)}, bf16[3,6,32,512]{3,2,1,0:T(8,128)(2,1)}, u32[]{:S(2)}, u32[]{:S(2)}) collective-permute-start(bf16[3,6,32,512]{3,2,1,0:T(8,128)(2,1)} %get-tuple-element.74.refs_17_), channel_id=1, source_target_pairs={{0,1},{1,0},{2,3},{3,2},{4,5},{5,4},{6,7},{7,6},{8,9},{9,8},{10,11... | collective-permute-start | bytes 1769480 | tf_op jit(solution)/shard_map/ppermute | solution.py:425
  81.9 4.1 %collective-permute-start.13 = (bf16[3,6,32,512]{3,2,1,0:T(8,128)(2,1)}, bf16[3,6,32,512]{3,2,1,0:T(8,128)(2,1)}, u32[]{:S(2)}, u32[]{:S(2)}) collective-permute-start(bf16[3,6,32,512]{3,2,1,0:T(8,128)(2,1)} %get-tuple-element.75.refs_18_), channel_id=1, source_target_pairs={{0,1},{1,0},{2,3},{3,2},{4,5},{5,4},{6,7},{7,6},{8,9},{9,8},{10,11... | collective-permute-start | bytes 1769480 | tf_op jit(solution)/shard_map/ppermute | solution.py:425
  102.2 17.0 %collective-permute-start.16 = (bf16[3,6,64,512]{3,2,1,0:T(8,128)(2,1)}, bf16[3,6,64,512]{3,2,1,0:T(8,128)(2,1)}, u32[]{:S(2)}, u32[]{:S(2)}) collective-permute-start(bf16[3,6,64,512]{3,2,1,0:T(8,128)(2,1)} %get-tuple-element.81.refs_24_.refs_16_), channel_id=1, source_target_pairs={{0,4},{1,3},{2,6},{3,1},{4,0},{5,7},{6,2},{7,5},{8,12},{9,11},{10,... | collective-permute-start | bytes 3538952 | tf_op jit(solution)/shard_map/ppermute | solution.py:422
  103.3 16.9 %collective-permute-start.17 = (bf16[3,6,64,512]{3,2,1,0:T(8,128)(2,1)}, bf16[3,6,64,512]{3,2,1,0:T(8,128)(2,1)}, u32[]{:S(2)}, u32[]{:S(2)}) collective-permute-start(bf16[3,6,64,512]{3,2,1,0:T(8,128)(2,1)} %get-tuple-element.76.refs_23_.refs_15_.refs_24_), channel_id=1, source_target_pairs={{0,1},{1,0},{2,3},{3,2},{4,5},{5,4},{6,7},{7,6},{8,9},{9,8},{10,11... | collective-permute-start | bytes 3538952 | tf_op jit(solution)/shard_map/ppermute | solution.py:425
  103.3 17.4 %collective-permute-start.18 = (bf16[3,6,64,512]{3,2,1,0:T(8,128)(2,1)}, bf16[3,6,64,512]{3,2,1,0:T(8,128)(2,1)}, u32[]{:S(2)}, u32[]{:S(2)}) collective-permute-start(bf16[3,6,64,512]{3,2,1,0:T(8,128)(2,1)} %get-tuple-element.81.refs_24_.refs_16_), channel_id=1, source_target_pairs={{0,1},{1,0},{2,3},{3,2},{4,5},{5,4},{6,7},{7,6},{8,9},{9,8},{10,11... | collective-permute-start | bytes 3538952 | tf_op jit(solution)/shard_map/ppermute | solution.py:425
  103.8 16.9 %collective-permute-start.19 = (bf16[3,6,64,512]{3,2,1,0:T(8,128)(2,1)}, bf16[3,6,64,512]{3,2,1,0:T(8,128)(2,1)}, u32[]{:S(2)}, u32[]{:S(2)}) collective-permute-start(bf16[3,6,64,512]{3,2,1,0:T(8,128)(2,1)} %get-tuple-element.83.refs_25_.refs_17_), channel_id=1, source_target_pairs={{0,1},{1,0},{2,3},{3,2},{4,5},{5,4},{6,7},{7,6},{8,9},{9,8},{10,11... | collective-permute-start | bytes 3538952 | tf_op jit(solution)/shard_map/ppermute | solution.py:425
  119.2 3.3 %collective-permute-start.20 = (bf16[3,6,64,512]{3,2,1,0:T(8,128)(2,1)}, bf16[3,6,64,512]{3,2,1,0:T(8,128)(2,1)}, u32[]{:S(2)}, u32[]{:S(2)}) collective-permute-start(bf16[3,6,64,512]{3,2,1,0:T(8,128)(2,1)} %get-tuple-element.84.refs_26_.refs_18_), channel_id=1, source_target_pairs={{0,1},{1,0},{2,3},{3,2},{4,5},{5,4},{6,7},{7,6},{8,9},{9,8},{10,11... | collective-permute-start | bytes 3538952 | tf_op jit(solution)/shard_map/ppermute | solution.py:425
  119.3 32.6 %collective-permute-start.21 = (bf16[3,6,64,512]{3,2,1,0:T(8,128)(2,1)}, bf16[3,6,64,512]{3,2,1,0:T(8,128)(2,1)}, u32[]{:S(2)}, u32[]{:S(2)}) collective-permute-start(bf16[3,6,64,512]{3,2,1,0:T(8,128)(2,1)} %get-tuple-element.85.refs_31_.refs_15_), channel_id=1, source_target_pairs={{0,2},{1,5},{2,0},{3,7},{4,6},{5,1},{6,4},{7,3},{8,10},{9,13},{10,... | collective-permute-start | bytes 3538952 | tf_op jit(solution)/shard_map/ppermute | solution.py:422
  120.2 31.7 %collective-permute-start.22 = (bf16[3,6,64,512]{3,2,1,0:T(8,128)(2,1)}, bf16[3,6,64,512]{3,2,1,0:T(8,128)(2,1)}, u32[]{:S(2)}, u32[]{:S(2)}) collective-permute-start(bf16[3,6,64,512]{3,2,1,0:T(8,128)(2,1)} %get-tuple-element.85.refs_31_.refs_15_), channel_id=1, source_target_pairs={{0,4},{1,3},{2,6},{3,1},{4,0},{5,7},{6,2},{7,5},{8,12},{9,11},{10,... | collective-permute-start | bytes 3538952 | tf_op jit(solution)/shard_map/ppermute | solution.py:422
  151.9 16.6 %collective-permute-start.23 = (bf16[3,6,64,512]{3,2,1,0:T(8,128)(2,1)}, bf16[3,6,64,512]{3,2,1,0:T(8,128)(2,1)}, u32[]{:S(2)}, u32[]{:S(2)}) collective-permute-start(bf16[3,6,64,512]{3,2,1,0:T(8,128)(2,1)} %get-tuple-element.91.refs_16_), channel_id=1, source_target_pairs={{0,4},{1,3},{2,6},{3,1},{4,0},{5,7},{6,2},{7,5},{8,12},{9,11},{10,... | collective-permute-start | bytes 3538952 | tf_op jit(solution)/shard_map/ppermute | solution.py:422
  152.5 16.0 %collective-permute-start.24 = (bf16[3,6,64,512]{3,2,1,0:T(8,128)(2,1)}, bf16[3,6,64,512]{3,2,1,0:T(8,128)(2,1)}, u32[]{:S(2)}, u32[]{:S(2)}) collective-permute-start(bf16[3,6,64,512]{3,2,1,0:T(8,128)(2,1)} %get-tuple-element.85.refs_31_.refs_15_), channel_id=1, source_target_pairs={{0,1},{1,0},{2,3},{3,2},{4,5},{5,4},{6,7},{7,6},{8,9},{9,8},{10,11... | collective-permute-start | bytes 3538952 | tf_op jit(solution)/shard_map/ppermute | solution.py:425
  152.8 15.8 %collective-permute-start.25 = (bf16[3,6,64,512]{3,2,1,0:T(8,128)(2,1)}, bf16[3,6,64,512]{3,2,1,0:T(8,128)(2,1)}, u32[]{:S(2)}, u32[]{:S(2)}) collective-permute-start(bf16[3,6,64,512]{3,2,1,0:T(8,128)(2,1)} %get-tuple-element.91.refs_16_), channel_id=1, source_target_pairs={{0,1},{1,0},{2,3},{3,2},{4,5},{5,4},{6,7},{7,6},{8,9},{9,8},{10,11... | collective-permute-start | bytes 3538952 | tf_op jit(solution)/shard_map/ppermute | solution.py:425
  153.0 15.5 %collective-permute-start.26 = (bf16[3,6,64,512]{3,2,1,0:T(8,128)(2,1)}, bf16[3,6,64,512]{3,2,1,0:T(8,128)(2,1)}, u32[]{:S(2)}, u32[]{:S(2)}) collective-permute-start(bf16[3,6,64,512]{3,2,1,0:T(8,128)(2,1)} %get-tuple-element.93.refs_17_), channel_id=1, source_target_pairs={{0,1},{1,0},{2,3},{3,2},{4,5},{5,4},{6,7},{7,6},{8,9},{9,8},{10,11... | collective-permute-start | bytes 3538952 | tf_op jit(solution)/shard_map/ppermute | solution.py:425
  168.5 3.2 %collective-permute-start.27 = (bf16[3,6,64,512]{3,2,1,0:T(8,128)(2,1)}, bf16[3,6,64,512]{3,2,1,0:T(8,128)(2,1)}, u32[]{:S(2)}, u32[]{:S(2)}) collective-permute-start(bf16[3,6,64,512]{3,2,1,0:T(8,128)(2,1)} %get-tuple-element.94.refs_18_), channel_id=1, source_target_pairs={{0,1},{1,0},{2,3},{3,2},{4,5},{5,4},{6,7},{7,6},{8,9},{9,8},{10,11... | collective-permute-start | bytes 3538952 | tf_op jit(solution)/shard_map/ppermute | solution.py:425
